TPU v7x, 32 devices: a whole 2x2x4 slice. The times are simulated.
32 devices in a mesh: fsdp: 2 (over core), ctx: 8 (over z, x), tp: 2 (over y).
Axes of the slice: x: 2, y: 2, z: 4, core: 2. Of those that a mesh axis runs over, the one named last changes fastest.
Arguments:
- tokens: bfloat16 [4096, 2048], P(('fsdp', 'ctx')), may hold values from -6 to 6
- cotangent: bfloat16 [4096, 2048], P(('fsdp', 'ctx')), may hold values from -6 to 6
- token_order: int32 [2, 2048], P('fsdp'), may hold values from 0 to 2047, each once within a row
- seq_lengths: int32 [2, 3], P('fsdp'), may hold values from 1 to 1024, 2048 in all within a row
- rel_buckets: int32 [2047], replicated, may hold values from 0 to 31, as said below
- gain_attn: bfloat16 [2048], P('fsdp'), may hold values from 0.5 to 1.5
- w_query: bfloat16 [2048, 2048], P('fsdp', 'tp'), may hold values from -1 to 1
- w_key: bfloat16 [2048, 2048], P('fsdp', 'tp'), may hold values from -0.125 to 0.125
- w_value: bfloat16 [2048, 2048], P('fsdp', 'tp'), may hold values from -0.125 to 0.125
- w_out: bfloat16 [2048, 2048], P('tp', 'fsdp'), may hold values from -0.75 to 0.75
- rel_bias: bfloat16 [32, 32], P('fsdp', 'tp'), may hold values from -4 to 4
- gain_ffn: bfloat16 [2048], P('fsdp'), may hold values from 0.5 to 1.5
- w_gate: bfloat16 [2048, 5120], P('fsdp', 'tp'), may hold values from -0.125 to 0.125
- w_up: bfloat16 [2048, 5120], P('fsdp', 'tp'), may hold values from -0.125 to 0.125
- w_down: bfloat16 [5120, 2048], P('tp', 'fsdp'), may hold values from -0.125 to 0.125
Outputs:
- output: bfloat16 [4096, 2048], P(('fsdp', 'ctx'))
- grad_tokens: float32 [4096, 2048], P(('fsdp', 'ctx'))
- grad_gain_attn: float32 [2048], P('fsdp')
- grad_query: float32 [2048, 2048], P('fsdp', 'tp')
- grad_key: float32 [2048, 2048], P('fsdp', 'tp')
- grad_value: float32 [2048, 2048], P('fsdp', 'tp')
- grad_out: float32 [2048, 2048], P('tp', 'fsdp')
- grad_bias: float32 [32, 32], P('fsdp', 'tp')
- grad_gain_ffn: float32 [2048], P('fsdp')
- grad_gate: float32 [2048, 5120], P('fsdp', 'tp')
- grad_up: float32 [2048, 5120], P('fsdp', 'tp')
- grad_down: float32 [5120, 2048], P('tp', 'fsdp')
- head_maxima: float32 [32], P('tp')
- query_clipped: bfloat16 [2048, 2048], P('fsdp', 'tp')
- key_clipped: bfloat16 [2048, 2048], P('fsdp', 'tp')
Inputs may be any that keep to these rules, and one draw needn't show every extreme that they name: `token_order`: each row names every position 0 to 2047 once. `seq_lengths`: each row holds 3 lengths that sum to 2048; the largest is 1024. `rel_buckets`: for relative position r: |r| for |r| < 8, else 8 to 15 and non-decreasing in |r|; plus 16 when r > 0.
All inputs are finite; a program needn't handle non-finite values.
Results may differ from a plain program's by a relative error of at most 0.025.
Values may be sent and summed in bfloat16 or wider, within the bound.
A program may use at most 256 MiB of HBM per device.

v0:
```python
import jax
import jax.numpy as jnp
from jax import lax
from jax.sharding import PartitionSpec as P

DH = 64
NB = 32


EPS = 1e-06
TAU_CLIP = 6.0


def rms_norm(values, gain):
    return values * lax.rsqrt(jnp.mean(values * values, axis=-1, keepdims=True) + EPS) * gain


def geglu(gate_pre, up_pre):
    return jax.nn.gelu(gate_pre, approximate=True) * up_pre


def segment_of(positions, lengths_row):
    offsets = jnp.cumsum(lengths_row) - lengths_row
    return jnp.sum((positions[:, None] >= offsets[None, :]).astype(jnp.int32), axis=1) - 1


def bucket_ranges(rel_buckets):
    table_len = rel_buckets.shape[0]
    index_all = jnp.arange(table_len, dtype=jnp.int32)
    bucket_ids = jnp.arange(NB, dtype=jnp.int32)
    matched = rel_buckets[:, None] == bucket_ids[None, :]
    range_first = jnp.min(jnp.where(matched, index_all[:, None], table_len), axis=0)
    range_last = jnp.max(jnp.where(matched, index_all[:, None], -1), axis=0)
    return (range_first, range_last, table_len)


def pair_terms(query_pos, query_seg, key_pos, key_seg, ranges, bias_table):
    range_first, range_last, table_len = ranges
    longest = (table_len + 1) // 2
    offset = jnp.clip(key_pos[None, :] - query_pos[:, None] + longest - 1, 0, 2 * longest - 2)
    inside = (offset[None, :, :] >= range_first[:, None, None]) & (
        offset[None, :, :] <= range_last[:, None, None]
    )
    bucket_hot = inside.astype(jnp.bfloat16)
    pair_bias = jnp.einsum(
        "btk,bh->htk", bucket_hot, bias_table, preferred_element_type=jnp.float32
    )
    same_seq = (query_seg[:, None] == key_seg[None, :])[None]
    return (bucket_hot, pair_bias, same_seq)


def per_device(
    tokens,
    cotangent,
    token_order,
    seq_lengths,
    rel_buckets,
    gain_attn,
    w_query,
    w_key,
    w_value,
    w_out,
    rel_bias,
    gain_ffn,
    w_gate,
    w_up,
    w_down,
):
    local_rows = tokens.shape[0]
    head_count = w_query.shape[1] // DH
    group_rows = local_rows * lax.axis_size("ctx")
    key_block = min(512, group_rows)
    block_count = group_rows // key_block
    ranges = bucket_ranges(rel_buckets)
    gain_a, full_query, full_key, full_value, full_out, bias_local = (
        lax.all_gather(gain_attn, "fsdp", axis=0, tiled=True),
        lax.all_gather(w_query, "fsdp", axis=0, tiled=True),
        lax.all_gather(w_key, "fsdp", axis=0, tiled=True),
        lax.all_gather(w_value, "fsdp", axis=0, tiled=True),
        lax.all_gather(w_out, "fsdp", axis=1, tiled=True),
        lax.all_gather(rel_bias, "fsdp", axis=0, tiled=True),
    )
    tokens_f = tokens.astype(jnp.float32)
    gain_a32 = gain_a.astype(jnp.float32)
    normed = rms_norm(tokens_f, gain_a32).astype(jnp.bfloat16)
    queries = jnp.dot(normed, full_query, preferred_element_type=jnp.float32).astype(jnp.bfloat16)
    keys_here = jnp.dot(normed, full_key, preferred_element_type=jnp.float32).astype(jnp.bfloat16)
    values_here = jnp.dot(normed, full_value, preferred_element_type=jnp.float32).astype(
        jnp.bfloat16
    )
    order_row = token_order[0]
    seq_ids = segment_of(order_row, seq_lengths[0])
    row_start = lax.axis_index("ctx") * local_rows
    query_pos = lax.dynamic_slice_in_dim(order_row, row_start, local_rows)
    query_seg = lax.dynamic_slice_in_dim(seq_ids, row_start, local_rows)
    pos_blocks = order_row.reshape(block_count, key_block)
    seg_blocks = seq_ids.reshape(block_count, key_block)
    query_heads = queries.reshape(local_rows, head_count, DH)
    key_all, value_all = (
        lax.all_gather(keys_here, "ctx", axis=0, tiled=True),
        lax.all_gather(values_here, "ctx", axis=0, tiled=True),
    )

    def blocked(array_in):
        return array_in.reshape(block_count, key_block, head_count, DH)

    def forward_block(running, inputs):
        summed, totals, head_top = running
        key_blk, value_blk, pos_blk, seg_blk = inputs
        raw_scores = jnp.einsum(
            "thd,khd->htk", query_heads, key_blk, preferred_element_type=jnp.float32
        )
        bucket_hot, pair_bias, same_seq = pair_terms(
            query_pos, query_seg, pos_blk, seg_blk, ranges, bias_local
        )
        weights = jnp.where(same_seq, jnp.exp(raw_scores + pair_bias), 0.0)
        totals = totals + jnp.sum(weights, axis=2)
        summed = summed + jnp.einsum(
            "htk,khd->thd",
            weights.astype(jnp.bfloat16),
            value_blk,
            preferred_element_type=jnp.float32,
        )
        head_top = jnp.maximum(
            head_top, jnp.max(jnp.where(same_seq, raw_scores, -1e30), axis=(1, 2))
        )
        return ((summed, totals, head_top), None)

    start_state = (
        jnp.zeros((local_rows, head_count, DH), jnp.float32),
        jnp.zeros((head_count, local_rows), jnp.float32),
        jnp.full((head_count,), -1e30, jnp.float32),
    )
    (summed, totals, head_top), unused = lax.scan(
        forward_block, start_state, (blocked(key_all), blocked(value_all), pos_blocks, seg_blocks)
    )
    row_totals = jnp.transpose(totals)[:, :, None]
    context_exact = summed / row_totals
    context = context_exact.reshape(local_rows, head_count * DH).astype(jnp.bfloat16)
    head_maxima = lax.pmax(head_top, ("fsdp", "ctx"))
    attn_out = lax.psum(
        jnp.dot(context, full_out, preferred_element_type=jnp.float32).astype(jnp.bfloat16), "tp"
    ).astype(jnp.float32)
    hidden_state = tokens_f + attn_out
    gain_f, full_gate, full_up, full_down = (
        lax.all_gather(gain_ffn, "fsdp", axis=0, tiled=True),
        lax.all_gather(w_gate, "fsdp", axis=0, tiled=True),
        lax.all_gather(w_up, "fsdp", axis=0, tiled=True),
        lax.all_gather(w_down, "fsdp", axis=1, tiled=True),
    )
    gain_f32 = gain_f.astype(jnp.float32)
    normed_ffn = rms_norm(hidden_state, gain_f32).astype(jnp.bfloat16)
    gate_pre = jnp.dot(normed_ffn, full_gate, preferred_element_type=jnp.float32)
    up_pre = jnp.dot(normed_ffn, full_up, preferred_element_type=jnp.float32)
    inner_act = geglu(gate_pre, up_pre).astype(jnp.bfloat16)
    ffn_out = lax.psum(
        jnp.dot(inner_act, full_down, preferred_element_type=jnp.float32).astype(jnp.bfloat16), "tp"
    ).astype(jnp.float32)
    output = (hidden_state + ffn_out).astype(jnp.bfloat16)
    grad_down = jnp.einsum("tf,td->fd", inner_act, cotangent, preferred_element_type=jnp.float32)
    inner_grad = jnp.einsum("td,fd->tf", cotangent, full_down, preferred_element_type=jnp.float32)
    unused, geglu_back = jax.vjp(geglu, gate_pre, up_pre)
    gate_grad, up_grad = geglu_back(inner_grad)
    gate_grad = gate_grad.astype(jnp.bfloat16)
    up_grad = up_grad.astype(jnp.bfloat16)
    grad_gate = jnp.einsum("tc,tf->cf", normed_ffn, gate_grad, preferred_element_type=jnp.float32)
    grad_up = jnp.einsum("tc,tf->cf", normed_ffn, up_grad, preferred_element_type=jnp.float32)
    ffn_term = jnp.einsum(
        "tf,cf->tc", gate_grad, full_gate, preferred_element_type=jnp.float32
    ) + jnp.einsum("tf,cf->tc", up_grad, full_up, preferred_element_type=jnp.float32)
    normed_ffn_grad = lax.psum(ffn_term.astype(jnp.bfloat16), "tp").astype(jnp.float32)
    unused, norm_ffn_back = jax.vjp(rms_norm, hidden_state, gain_f32)
    hidden_norm_grad, grad_gain_ffn = norm_ffn_back(normed_ffn_grad)
    hidden_grad = cotangent.astype(jnp.float32) + hidden_norm_grad
    attn_grad = hidden_grad.astype(jnp.bfloat16)
    grad_out = jnp.einsum("tc,td->cd", context, attn_grad, preferred_element_type=jnp.float32)
    context_grad = jnp.einsum(
        "td,cd->tc", attn_grad, full_out, preferred_element_type=jnp.float32
    ).reshape(local_rows, head_count, DH)
    summed_grad = (context_grad / row_totals).astype(jnp.bfloat16)
    total_grad = jnp.transpose(-jnp.sum(context_grad * context_exact, axis=2) / row_totals[:, :, 0])
    key_back, value_back = (key_all, value_all)

    def backward_block(running, inputs):
        query_acc, bias_acc = running
        key_blk, value_blk, pos_blk, seg_blk = inputs
        raw_scores = jnp.einsum(
            "thd,khd->htk", query_heads, key_blk, preferred_element_type=jnp.float32
        )
        bucket_hot, pair_bias, same_seq = pair_terms(
            query_pos, query_seg, pos_blk, seg_blk, ranges, bias_local
        )
        weights = jnp.where(same_seq, jnp.exp(raw_scores + pair_bias), 0.0)
        prob_grad = (
            jnp.einsum("thd,khd->htk", summed_grad, value_blk, preferred_element_type=jnp.float32)
            + total_grad[:, :, None]
        )
        score_grad = (weights * prob_grad).astype(jnp.bfloat16)
        query_acc = query_acc + jnp.einsum(
            "htk,khd->thd", score_grad, key_blk, preferred_element_type=jnp.float32
        )
        key_grad = jnp.einsum(
            "htk,thd->khd", score_grad, query_heads, preferred_element_type=jnp.float32
        )
        value_grad = jnp.einsum(
            "htk,thd->khd",
            weights.astype(jnp.bfloat16),
            summed_grad,
            preferred_element_type=jnp.float32,
        )
        bucket_sums = jnp.einsum(
            "htk,btk->hb", score_grad, bucket_hot, preferred_element_type=jnp.float32
        )
        return ((query_acc, bias_acc + bucket_sums), (key_grad, value_grad))

    zero_state = (
        jnp.zeros((local_rows, head_count, DH), jnp.float32),
        jnp.zeros((head_count, NB), jnp.float32),
    )
    (query_acc, bias_acc), (key_grads, value_grads) = lax.scan(
        backward_block, zero_state, (blocked(key_back), blocked(value_back), pos_blocks, seg_blocks)
    )
    key_grad_all, value_grad_all = (
        lax.psum_scatter(
            key_grads.reshape(group_rows, head_count * DH).astype(jnp.bfloat16),
            "ctx",
            scatter_dimension=0,
            tiled=True,
        ).astype(jnp.float32),
        lax.psum_scatter(
            value_grads.reshape(group_rows, head_count * DH).astype(jnp.bfloat16),
            "ctx",
            scatter_dimension=0,
            tiled=True,
        ).astype(jnp.float32),
    )
    query_grad = query_acc.reshape(local_rows, head_count * DH).astype(jnp.bfloat16)
    key_grad = key_grad_all.astype(jnp.bfloat16)
    value_grad = value_grad_all.astype(jnp.bfloat16)
    attn_term = jnp.einsum("tc,dc->td", query_grad, full_query, preferred_element_type=jnp.float32)
    attn_term = attn_term + jnp.einsum(
        "tc,dc->td", key_grad, full_key, preferred_element_type=jnp.float32
    )
    attn_term = attn_term + jnp.einsum(
        "tc,dc->td", value_grad, full_value, preferred_element_type=jnp.float32
    )
    normed_grad = lax.psum(attn_term.astype(jnp.bfloat16), "tp").astype(jnp.float32)
    unused, norm_attn_back = jax.vjp(rms_norm, tokens_f, gain_a32)
    token_norm_grad, grad_gain_attn = norm_attn_back(normed_grad)
    grad_tokens = hidden_grad + token_norm_grad
    grad_query = jnp.einsum("td,tc->dc", normed, query_grad, preferred_element_type=jnp.float32)
    grad_key = jnp.einsum("td,tc->dc", normed, key_grad, preferred_element_type=jnp.float32)
    grad_value = jnp.einsum("td,tc->dc", normed, value_grad, preferred_element_type=jnp.float32)
    grad_bias = jnp.transpose(bias_acc)
    (
        share_gain_a,
        share_query,
        share_key,
        share_value,
        share_out,
        share_bias,
        share_gain_f,
        share_gate,
        share_up,
        share_down,
    ) = (
        lax.psum_scatter(
            grad_gain_attn.astype(jnp.bfloat16), "fsdp", scatter_dimension=0, tiled=True
        ).astype(jnp.float32),
        lax.psum_scatter(
            grad_query.astype(jnp.bfloat16), "fsdp", scatter_dimension=0, tiled=True
        ).astype(jnp.float32),
        lax.psum_scatter(
            grad_key.astype(jnp.bfloat16), "fsdp", scatter_dimension=0, tiled=True
        ).astype(jnp.float32),
        lax.psum_scatter(
            grad_value.astype(jnp.bfloat16), "fsdp", scatter_dimension=0, tiled=True
        ).astype(jnp.float32),
        lax.psum_scatter(
            grad_out.astype(jnp.bfloat16), "fsdp", scatter_dimension=1, tiled=True
        ).astype(jnp.float32),
        lax.psum_scatter(
            grad_bias.astype(jnp.bfloat16), "fsdp", scatter_dimension=0, tiled=True
        ).astype(jnp.float32),
        lax.psum_scatter(
            grad_gain_ffn.astype(jnp.bfloat16), "fsdp", scatter_dimension=0, tiled=True
        ).astype(jnp.float32),
        lax.psum_scatter(
            grad_gate.astype(jnp.bfloat16), "fsdp", scatter_dimension=0, tiled=True
        ).astype(jnp.float32),
        lax.psum_scatter(
            grad_up.astype(jnp.bfloat16), "fsdp", scatter_dimension=0, tiled=True
        ).astype(jnp.float32),
        lax.psum_scatter(
            grad_down.astype(jnp.bfloat16), "fsdp", scatter_dimension=1, tiled=True
        ).astype(jnp.float32),
    )
    (
        final_gain_a,
        final_query,
        final_key,
        final_value,
        final_out,
        final_bias,
        final_gain_f,
        final_gate,
        final_up,
        final_down,
    ) = (
        lax.psum(share_gain_a.astype(jnp.bfloat16), "ctx").astype(jnp.float32),
        lax.psum(share_query.astype(jnp.bfloat16), "ctx").astype(jnp.float32),
        lax.psum(share_key.astype(jnp.bfloat16), "ctx").astype(jnp.float32),
        lax.psum(share_value.astype(jnp.bfloat16), "ctx").astype(jnp.float32),
        lax.psum(share_out.astype(jnp.bfloat16), "ctx").astype(jnp.float32),
        lax.psum(share_bias.astype(jnp.bfloat16), "ctx").astype(jnp.float32),
        lax.psum(share_gain_f.astype(jnp.bfloat16), "ctx").astype(jnp.float32),
        lax.psum(share_gate.astype(jnp.bfloat16), "ctx").astype(jnp.float32),
        lax.psum(share_up.astype(jnp.bfloat16), "ctx").astype(jnp.float32),
        lax.psum(share_down.astype(jnp.bfloat16), "ctx").astype(jnp.float32),
    )
    clip_scale = TAU_CLIP / jnp.maximum(head_maxima, TAU_CLIP)
    column_scale = jnp.repeat(jnp.sqrt(clip_scale), DH)
    query_clipped = (w_query.astype(jnp.float32) * column_scale[None, :]).astype(jnp.bfloat16)
    key_clipped = (w_key.astype(jnp.float32) * column_scale[None, :]).astype(jnp.bfloat16)
    return (
        output,
        grad_tokens,
        final_gain_a,
        final_query,
        final_key,
        final_value,
        final_out,
        final_bias,
        final_gain_f,
        final_gate,
        final_up,
        final_down,
        head_maxima,
        query_clipped,
        key_clipped,
    )


def solution(mesh):
    in_specs = (
        P(("fsdp", "ctx"), None),
        P(("fsdp", "ctx"), None),
        P("fsdp", None),
        P("fsdp", None),
        P(),
        P("fsdp"),
        P("fsdp", "tp"),
        P("fsdp", "tp"),
        P("fsdp", "tp"),
        P("tp", "fsdp"),
        P("fsdp", "tp"),
        P("fsdp"),
        P("fsdp", "tp"),
        P("fsdp", "tp"),
        P("tp", "fsdp"),
    )
    out_specs = (
        P(("fsdp", "ctx"), None),
        P(("fsdp", "ctx"), None),
        P("fsdp"),
        P("fsdp", "tp"),
        P("fsdp", "tp"),
        P("fsdp", "tp"),
        P("tp", "fsdp"),
        P("fsdp", "tp"),
        P("fsdp"),
        P("fsdp", "tp"),
        P("fsdp", "tp"),
        P("tp", "fsdp"),
        P("tp"),
        P("fsdp", "tp"),
        P("fsdp", "tp"),
    )
    return jax.shard_map(
        per_device, mesh=mesh, in_specs=in_specs, out_specs=out_specs, check_vma=False
    )
```

profile of v0, /device:TPU:0, one launch (start us, length us, event | category | flops | bytes accessed | tf_op | source)
XLA Modules:
  0.0 1826.5 jit_solution(8322462910621269968)
XLA Ops:
  12.3 13.7 all-gather.10.cloned.1.call-done
  30.3 12.1 all-gather.14.cloned.1.call-done
  62.5 73.5 %all-gather.12.cloned.1.call-done = bf16[2048,1024]{1,0:T(8,128)(2,1)} async-done(((bf16[256,1024]{1,0:T(8,128)(2,1)}), bf16[2048,1024]{1,0:T(8,128)(2,1)}) %all-gather.12.cloned.1.call-update) | async-done | bytes 4194320 | tf_op jit(solution)/shard_map/all_gather | solution.py:101
  136.0 11.7 reshape.265
  147.6 9.7 copy.138
  157.4 52.8 %all-gather.16.cloned.1.call-done = bf16[2048,1024]{1,0:T(8,128)(2,1)} async-done(((bf16[256,1024]{1,0:T(8,128)(2,1)}), bf16[2048,1024]{1,0:T(8,128)(2,1)}) %all-gather.16.cloned.1.call-update) | async-done | bytes 4194320 | tf_op jit(solution)/shard_map/all_gather | solution.py:100
  210.2 11.8 reshape.266
  222.0 9.7 copy.139
  231.8 127.7 %while.40 = (s32[]{:T(128)}, f32[256,16,64]{0,2,1:T(8,128)S(1)}, f32[16,256]{1,0:T(8,128)S(1)}, f32[16]{0:T(128)S(1)}, bf16[4,512,16,64]{1,3,2,0:T(8,128)(2,1)},...) while((s32[]{:T(128)}, f32[256,16,64]{0,2,1:T(8,128)S(1)}, ...), condition=%wide.region_8.9_spmd.clone, body=%wide.region_5.8_spmd.clone.sunk | while | flops 701501440 | bytes 64963232 | solution.py:134
  238.6 10.4 copy.171
  249.1 7.6 fusion.175
  256.7 7.9 fusion.176
  270.7 9.9 copy.171
  280.8 7.6 fusion.175
  288.4 7.8 fusion.176
  302.3 9.9 copy.171
  312.4 7.6 fusion.175
  320.0 7.8 fusion.176
  333.9 9.9 copy.171
  344.0 7.6 fusion.175
  351.6 7.8 fusion.176
  367.9 8.8 fusion.99
  376.6 26.2 %all-reduce.11.cloned.1.call-done = bf16[256,2048]{1,0:T(8,128)(2,1)} async-done(((bf16[256,2048]{1,0:T(8,128)(2,1)}), bf16[256,2048]{1,0:T(8,128)(2,1)}) %all-reduce.11.cloned.1.call-update) | async-done | bytes 1048592 | tf_op jit(solution)/shard_map/psum | solution.py:141
  406.1 21.3 %all-gather.22.cloned.1.call-done = bf16[2048,2560]{1,0:T(8,128)(2,1)} async-done(((bf16[1024,2560]{1,0:T(8,128)(2,1)}), bf16[2048,2560]{1,0:T(8,128)(2,1)}) %all-gather.22.cloned.1.call-update) | async-done | bytes 10485776 | tf_op jit(solution)/shard_map/all_gather | solution.py:147
  427.4 8.7 fusion.98
  436.1 16.9 all-gather.24.cloned.1.call-done
  453.0 11.3 multiply_convert_fusion.3
  467.2 7.9 fusion.71
  475.2 41.3 %all-reduce.13.cloned.1.call-done = bf16[256,2048]{1,0:T(8,128)(2,1)} async-done(((bf16[256,2048]{1,0:T(8,128)(2,1)}), bf16[256,2048]{1,0:T(8,128)(2,1)}) %all-reduce.13.cloned.1.call-update) | async-done | bytes 1048592 | tf_op jit(solution)/shard_map/psum | solution.py:171
  524.0 132.4 %while.41 = (s32[]{:T(128)}, f32[256,16,64]{0,2,1:T(8,128)}, f32[16,32]{1,0:T(8,128)S(1)}, bf16[4,512,16,64]{1,3,2,0:T(8,128)(2,1)}, bf16[4,512,16,64]{1,3,2,0:T...) while((s32[]{:T(128)}, f32[256,16,64]{0,2,1:T(8,128)}, ...), condition=%wide.region_16.17_spmd.clone, body=%wide.region_15.16_spmd.clone.sunk | while | flops 1649411072 | bytes 156014960 | solution.py:220
  547.0 7.8 fusion.194
  580.0 7.8 fusion.194
  612.9 7.8 fusion.194
  645.9 7.8 fusion.194
  687.1 66.9 %reduce-scatter.13.cloned.1.call-done = bf16[256,1024]{0,1:T(8,128)(2,1)} async-done(((bf16[2048,1024]{0,1:T(8,128)(2,1)}), bf16[256,1024]{0,1:T(8,128)(2,1)}) %reduce-scatter.13.cloned.1.call-update) | async-done | bytes 524304 | tf_op jit(solution)/shard_map/reduce_scatter | solution.py:224
  758.6 88.3 %reduce-scatter.15.cloned.1.call-done = bf16[256,1024]{0,1:T(8,128)(2,1)} async-done(((bf16[2048,1024]{0,1:T(8,128)(2,1)}), bf16[256,1024]{0,1:T(8,128)(2,1)}) %reduce-scatter.15.cloned.1.call-update) | async-done | bytes 524304 | tf_op jit(solution)/shard_map/reduce_scatter | solution.py:230
  852.6 7.5 convolution_convert_fusion.2
  868.5 7.5 convolution_convert_fusion
  876.3 8.4 convolution_convert_fusion.7
  895.5 14.5 reduce-scatter.21.cloned.1.call-done
  910.0 23.1 %reduce-scatter.25.cloned.1.call-done = bf16[1024,2560]{1,0:T(8,128)(2,1)} async-done(((bf16[2048,2560]{1,0:T(8,128)(2,1)}), bf16[1024,2560]{1,0:T(8,128)(2,1)}) %reduce-scatter.25.cloned.1.call-update) | async-done | bytes 5242896 | tf_op jit(solution)/shard_map/reduce_scatter | solution.py:288
  933.1 23.2 %reduce-scatter.27.cloned.1.call-done = bf16[1024,2560]{1,0:T(8,128)(2,1)} async-done(((bf16[2048,2560]{1,0:T(8,128)(2,1)}), bf16[1024,2560]{1,0:T(8,128)(2,1)}) %reduce-scatter.27.cloned.1.call-update) | async-done | bytes 5242896 | tf_op jit(solution)/shard_map/reduce_scatter | solution.py:291
  956.3 23.0 %reduce-scatter.29.cloned.1.call-done = bf16[2560,1024]{1,0:T(8,128)(2,1)} async-done(((bf16[2560,2048]{1,0:T(8,128)(2,1)}), bf16[2560,1024]{1,0:T(8,128)(2,1)}) %reduce-scatter.29.cloned.1.call-update) | async-done | bytes 5242896 | tf_op jit(solution)/shard_map/reduce_scatter | solution.py:294
  981.2 33.9 %pmax.7 = f32[16]{0:T(128)S(1)} all-reduce(f32[16]{0:T(128)S(1)} %copy-done.38), channel_id=1, replica_groups=mesh['fsdp'=2,'ctx'=8,'tp'=2] {'fsdp','ctx'}, use_global_device_ids=true, to_apply=%region_43.44 | all-reduce | flops 16 | bytes 128 | tf_op jit(solution)/shard_map/pmax | solution.py:140
  1021.5 36.5 %all-reduce.17.cloned.1.call-done = (bf16[256,2048]{1,0:T(8,128)(2,1)}, bf16[256,2048]{1,0:T(8,128)(2,1)}) async-done(((bf16[256,2048]{1,0:T(8,128)(2,1)}, bf16[256,2048]{1,0:T(8,128)(2,1)}), (bf16[256,2048]{1,0:T(8,128)(2,1)}, bf16[256,2048]{1,0:T(8,128)(2,1)})) %all-reduce.17.cloned.1.call-update) | async-done | bytes 2097168 | tf_op jit(solution)/shard_map/psum | solution.py:247
  1062.8 22.4 %all-reduce.2 = (bf16[16,16]{0,1:T(8,128)(2,1)S(1)}, bf16[1024]{0:T(1024)(128)(2,1)S(1)}, bf16[1024]{0:T(1024)(128)(2,1)S(1)}) all-reduce(bf16[16,16]{0,1:T(8,128)(2,1)S(1)} %copy.154, bf16[1024]{0:T(1024)(128)(2,1)S(1)} %dynamic-slice.2, bf16[1024]{0:T(1024)(128)(2,1)S(1)} %dynamic-slice.4), channel_id=1, replica_groups=mesh['fsdp'=2,'ctx'=8,'tp'=2] {'ctx'}, use_global_device_ids=true, to_apply=%region_33.34 | all-reduce | flops 2304 | bytes 9216 | tf_op jit(solution)/shard_map/psum | solution.py:315
  1092.1 698.5 %all-reduce.15.cloned.1.call-done = (bf16[1024,1024]{1,0:T(8,128)(2,1)}, bf16[1024,1024]{1,0:T(8,128)(2,1)}, bf16[1024,1024]{1,0:T(8,128)(2,1)}, bf16[1024,1024]...) async-done(((bf16[1024,1024]{1,0:T(8,128)(2,1)}, bf16[1024,1024]{1,0:T(8,128)(2,1)}, ...) | async-done | bytes 24117264 | tf_op jit(solution)/shard_map/psum | solution.py:311
  1790.6 8.2 convert_element_type.272
  (343 shorter events, 277.9 us)
Async XLA Ops:
  7.2 18.8 %all-gather.10.cloned.1.call-start = ((), (), s32[]{:S(2)}) async-start(), calls=%async_computation.10 | async-start | bytes 6291456 | tf_op jit(solution)/shard_map/all_gather | solution.py:79
  7.9 34.5 %all-gather.14.cloned.1.call-start = ((), (), s32[]{:S(2)}) async-start(), calls=%async_computation.12 | async-start | bytes 6291456 | tf_op jit(solution)/shard_map/all_gather | solution.py:78
  8.7 50.1 %all-gather.18.cloned.1.call-start = ((), (), s32[]{:S(2)}) async-start(), calls=%async_computation.14 | async-start | bytes 6291456 | tf_op jit(solution)/shard_map/all_gather | solution.py:77
  9.4 126.5 %all-gather.12.cloned.1.call-start = ((), (), s32[]{:S(2)}) async-start(), calls=%async_computation.11 | async-start | bytes 4718592 | tf_op jit(solution)/shard_map/all_gather | solution.py:101
  11.4 47.4 %copy-start.26 = (f32[2048]{0:T(1024)}, f32[2048]{0:T(1024)S(1)}, u32[]{:S(2)}) copy-start(f32[2048]{0:T(1024)S(1)} %convert_element_type.225) | copy-start | bytes 24580
  12.3 46.5 %copy-start.31 = (f32[256]{0:T(256)}, f32[256]{0:T(256)S(1)}, u32[]{:S(2)}) copy-start(f32[256]{0:T(256)S(1)} %fusion.88) | copy-start | bytes 3076
  30.3 179.9 %all-gather.16.cloned.1.call-start = ((), (), s32[]{:S(2)}) async-start(), calls=%async_computation.13 | async-start | bytes 4718592 | tf_op jit(solution)/shard_map/all_gather | solution.py:100
  46.7 312.9 %all-gather.20.cloned.1.call-start = ((), (), s32[]{:S(2)}) async-start(), calls=%async_computation.15 | async-start | bytes 6291456 | tf_op jit(solution)/shard_map/all_gather | solution.py:80
  47.3 320.5 %all-gather.26.cloned.1.call-start = ((), (), s32[]{:S(2)}) async-start(), calls=%async_computation.19 | async-start | bytes 15728640 | tf_op jit(solution)/shard_map/all_gather | solution.py:149
  48.1 354.8 %all-reduce.11.cloned.1.call-start = ((), (), s32[]{:S(2)}) async-start(), calls=%async_computation.16 | async-start | bytes 2097152 | tf_op jit(solution)/shard_map/psum | solution.py:141
  359.4 4.8 copy-start.37
  364.2 63.2 %all-gather.22.cloned.1.call-start = ((), (), s32[]{:S(2)}) async-start(), calls=%async_computation.17 | async-start | bytes 15728640 | tf_op jit(solution)/shard_map/all_gather | solution.py:147
  365.0 88.0 %all-gather.24.cloned.1.call-start = ((), (), s32[]{:S(2)}) async-start(), calls=%async_computation.18 | async-start | bytes 15728640 | tf_op jit(solution)/shard_map/all_gather | solution.py:148
  365.6 151.0 %all-reduce.13.cloned.1.call-start = ((), (), s32[]{:S(2)}) async-start(), calls=%async_computation.20 | async-start | bytes 2097152 | tf_op jit(solution)/shard_map/psum | solution.py:171
  367.8 152.0 %copy-start.29 = (f32[2048]{0:T(1024)}, f32[2048]{0:T(1024)S(1)}, u32[]{:S(2)}) copy-start(f32[2048]{0:T(1024)S(1)} %convert_element_type.235) | copy-start | bytes 24580
  404.6 115.1 %copy-start.34 = (f32[256]{0:T(256)}, f32[256]{0:T(256)S(1)}, u32[]{:S(2)}) copy-start(f32[256]{0:T(256)S(1)} %fusion.89) | copy-start | bytes 3076
  453.0 11.3 copy-start.47
  475.1 279.0 %reduce-scatter.13.cloned.1.call-start = ((), (), s32[]{:S(2)}) async-start(), calls=%async_computation.21 | async-start | bytes 4718592 | tf_op jit(solution)/shard_map/reduce_scatter | solution.py:224
  543.4 11.3 slice-start
  547.0 7.8 copy-start.5
  547.0 7.8 slice-start.1
  576.4 11.3 slice-start
  579.9 7.8 copy-start.5
  579.9 7.8 slice-start.1
  609.4 11.3 slice-start
  612.9 7.8 copy-start.5
  612.9 7.8 slice-start.1
  642.3 11.3 slice-start
  645.8 7.8 copy-start.5
  645.9 7.8 slice-start.1
  665.5 181.4 %reduce-scatter.15.cloned.1.call-start = ((), (), s32[]{:S(2)}) async-start(), calls=%async_computation.22 | async-start | bytes 4718592 | tf_op jit(solution)/shard_map/reduce_scatter | solution.py:230
  674.7 220.7 %reduce-scatter.23.cloned.1.call-start = ((), (), s32[]{:S(2)}) async-start(), calls=%async_computation.26 | async-start | bytes 6291456 | tf_op jit(solution)/shard_map/reduce_scatter | solution.py:279
  681.6 213.9 %reduce-scatter.17.cloned.1.call-start = ((), (), s32[]{:S(2)}) async-start(), calls=%async_computation.23 | async-start | bytes 6291456 | tf_op jit(solution)/shard_map/reduce_scatter | solution.py:270
  687.1 208.4 %reduce-scatter.19.cloned.1.call-start = ((), (), s32[]{:S(2)}) async-start(), calls=%async_computation.24 | async-start | bytes 6291456 | tf_op jit(solution)/shard_map/reduce_scatter | solution.py:273
  758.6 151.4 %reduce-scatter.21.cloned.1.call-start = ((), (), s32[]{:S(2)}) async-start(), calls=%async_computation.25 | async-start | bytes 6291456 | tf_op jit(solution)/shard_map/reduce_scatter | solution.py:276
  851.4 81.6 %reduce-scatter.25.cloned.1.call-start = ((), (), s32[]{:S(2)}) async-start(), calls=%async_computation.27 | async-start | bytes 15728640 | tf_op jit(solution)/shard_map/reduce_scatter | solution.py:288
  860.2 96.1 %reduce-scatter.27.cloned.1.call-start = ((), (), s32[]{:S(2)}) async-start(), calls=%async_computation.28 | async-start | bytes 15728640 | tf_op jit(solution)/shard_map/reduce_scatter | solution.py:291
  867.3 112.0 %reduce-scatter.29.cloned.1.call-start = ((), (), s32[]{:S(2)}) async-start(), calls=%async_computation.29 | async-start | bytes 15728640 | tf_op jit(solution)/shard_map/reduce_scatter | solution.py:294
  876.0 144.7 %reduce-scatter.31.cloned.1.call-start = ((), (), s32[]{:S(2)}) async-start(), calls=%async_computation.30 | async-start | bytes 12288
  885.4 172.6 %all-reduce.17.cloned.1.call-start = ((), (), s32[]{:S(2)}) async-start(), calls=%async_computation.32 | async-start | bytes 4194304 | tf_op jit(solution)/shard_map/psum | solution.py:247
  895.4 895.2 %all-reduce.15.cloned.1.call-start = ((), (), s32[]{:S(2)}) async-start(), calls=%async_computation.31 | async-start | bytes 48234496 | tf_op jit(solution)/shard_map/psum | solution.py:311
  1015.1 5.7 copy-start.51
  1015.2 45.0 %copy-start.36 = (bf16[2048]{0:T(1024)(128)(2,1)S(1)}, bf16[2048]{0:T(1024)(128)(2,1)}, u32[]{:S(2)}) copy-start(bf16[2048]{0:T(1024)(128)(2,1)} %get-tuple-element.949) | copy-start | bytes 12292
  1015.2 71.8 %copy-start.42 = (f32[256]{0:T(256)S(1)}, f32[256]{0:T(256)}, u32[]{:S(2)}) copy-start(f32[256]{0:T(256)} %copy-done.41) | copy-start | bytes 3076
  1790.6 8.2 copy-start.15
  1790.6 13.7 slice-start.2
  1798.8 5.5 slice-start.3
  1804.3 5.4 copy-start.21
  (49 other events, 112.0 us)
Sparse Core Ops, SparseCore 0:
  9.6 16.3 all-gather.9
  27.5 14.8 all-gather.13
  43.9 14.8 all-gather.17
  61.4 74.5 all-gather.11
  138.5 71.6 all-gather.15
  211.6 11.9 all-gather.19
  225.1 24.0 all-gather.25
  364.3 38.4 all-reduce.10
  404.5 22.8 all-gather.21
  428.9 24.0 all-gather.23
  475.3 41.2 all-reduce.12
  665.6 88.4 reduce-scatter.12
  758.7 88.1 reduce-scatter.14
  849.7 11.8 reduce-scatter.22
  864.4 13.3 reduce-scatter.16
  880.4 13.3 reduce-scatter.18
  896.6 13.3 reduce-scatter.20
  912.7 20.3 reduce-scatter.24
  936.0 20.2 reduce-scatter.26
  959.0 20.2 reduce-scatter.28
  982.1 8.6 reduce-scatter.30
  993.7 64.2 all-reduce.16
  1064.9 725.6 all-reduce.14
where the time goes:
time: 1830 us
  waiting for transfers between devices  1240 us (68%)
  matrix products  324 us (18%)
  local copies, waits for them, and re-layouts  123 us (7%)
  blocking collectives  64.8 us (4%)
  other arithmetic  54.1 us (3%)
    psum x1, waiting for transfers between devices, per_device(): lax.psum(share_query.astype(jnp.bfloat16), 'ctx').astype(jnp.float32)  698 us
    reduce_scatter x1, waiting for transfers between devices, per_device(): lax.psum_scatter(value_grads.reshape(group_rows, head_count * DH).astype(...  88.3 us
    all_gather x1, waiting for transfers between devices, per_device(): lax.all_gather(values_here, 'ctx', axis=0, tiled=True)  73.5 us
    reduce_scatter x1, waiting for transfers between devices, per_device(): lax.psum_scatter(key_grads.reshape(group_rows, head_count * DH).astype(jn...  66.9 us
    all_gather x1, waiting for transfers between devices, per_device(): lax.all_gather(keys_here, 'ctx', axis=0, tiled=True)  52.8 us
    psum x1, waiting for transfers between devices, per_device(): lax.psum(ffn_term.astype(jnp.bfloat16), 'tp').astype(jnp.float32)  41.3 us
    dot_general x4, local copies, waits for them, and re-layouts, pair_terms(): jnp.einsum('btk,bh->htk', bucket_hot, bias_table, preferred_element_type=...  40.1 us
    dot_general x8, matrix products, pair_terms(): jnp.einsum('btk,bh->htk', bucket_hot, bias_table, preferred_element_type=...  39.2 us
  transfers between devices with their start and end apart: 23, of which 17 were waited for; matrix products, arithmetic and copies ran while one was open for 16% of the time, Pallas kernels for 0%

commit v1 on v0

--- a/solution.py
+++ b/solution.py
@@ -49,7 +49,7 @@
     return (bucket_hot, pair_bias, same_seq)
 
 
-def per_device(
+def per_device_generic(
     tokens,
     cotangent,
     token_order,
@@ -341,6 +341,373 @@
     )
 
 
+RING = (0, 2, 4, 6, 7, 5, 3, 1)
+F32 = jnp.float32
+BF16 = jnp.bfloat16
+
+
+def look_up(table, index):
+    found = jnp.int32(table[0])
+    for place in range(1, len(table)):
+        found = jnp.where(index == place, table[place], found)
+    return found
+
+
+def swap(array_in, axis_name):
+    return lax.ppermute(array_in, axis_name, [(0, 1), (1, 0)])
+
+
+def dot_f32(left, right):
+    return jnp.dot(left, right, preferred_element_type=F32)
+
+
+def dot_nt(left, right):
+    return lax.dot_general(left, right, (((1,), (1,)), ((), ())), preferred_element_type=F32)
+
+
+def dot_tn(left, right):
+    return lax.dot_general(left, right, (((0,), (0,)), ((), ())), preferred_element_type=F32)
+
+
+def ring_sum(forward_parts, backward_parts):
+    count = len(RING)
+    up_pairs = [(RING[i], RING[(i + 1) % count]) for i in range(count)]
+    down_pairs = [(after, before) for before, after in up_pairs]
+    me = look_up([RING.index(c) for c in range(count)], lax.axis_index("ctx"))
+    flows = [(array_in, 1, up_pairs) for array_in in forward_parts]
+    flows += [(array_in, -1, down_pairs) for array_in in backward_parts]
+
+    def piece(array_in, chunk):
+        rows = array_in.shape[0] // count
+        return lax.dynamic_slice_in_dim(array_in, jnp.mod(chunk, count) * rows, rows)
+
+    current = [piece(array_in, me) for array_in, way, pairs in flows]
+    for step in range(count - 1):
+        arrived = [
+            lax.ppermute(held, "ctx", pairs) for held, (array_in, way, pairs) in zip(current, flows)
+        ]
+        current = [
+            (got.astype(F32) + piece(array_in, me - way * (step + 1)).astype(F32)).astype(BF16)
+            for got, (array_in, way, pairs) in zip(arrived, flows)
+        ]
+    results = [jnp.zeros(array_in.shape, F32) for array_in, way, pairs in flows]
+
+    def place(result, chunk, held):
+        rows = held.shape[0]
+        return lax.dynamic_update_slice_in_dim(
+            result, held.astype(F32), jnp.mod(chunk, count) * rows, 0
+        )
+
+    for step in range(count):
+        results = [
+            place(result, me - way * (count - 1 + step), held)
+            for result, held, (array_in, way, pairs) in zip(results, current, flows)
+        ]
+        if step < count - 1:
+            current = [
+                lax.ppermute(held, "ctx", pairs)
+                for held, (array_in, way, pairs) in zip(current, flows)
+            ]
+    forward_count = len(forward_parts)
+    return (results[:forward_count], results[forward_count:])
+
+
+def per_device_ring(
+    tokens,
+    cotangent,
+    token_order,
+    seq_lengths,
+    rel_buckets,
+    gain_attn,
+    w_query,
+    w_key,
+    w_value,
+    w_out,
+    rel_bias,
+    gain_ffn,
+    w_gate,
+    w_up,
+    w_down,
+):
+    core = lax.axis_index("fsdp")
+    ctx = lax.axis_index("ctx")
+    tp = lax.axis_index("tp")
+    local_rows = tokens.shape[0]
+    half = w_query.shape[0]
+    head_count = w_query.shape[1] // DH
+    group_rows = local_rows * lax.axis_size("ctx")
+    first = core == 0
+
+    def halves(array_in):
+        left, right = (array_in[:, :half], array_in[:, half:])
+        return (jnp.where(first, left, right), jnp.where(first, right, left))
+
+    def whole(own, other):
+        return jnp.concatenate(
+            [jnp.where(first, own, other), jnp.where(first, other, own)], axis=1
+        )
+
+    small = jnp.concatenate([gain_attn, gain_ffn, rel_bias.reshape(-1)])
+    small_far = swap(small, "fsdp")
+    wq_far, wk_far, wv_far = (swap(w_query, "fsdp"), swap(w_key, "fsdp"), swap(w_value, "fsdp"))
+    wo_far = swap(w_out, "fsdp")
+    wg_far, wu_far, wd_far = (swap(w_gate, "fsdp"), swap(w_up, "fsdp"), swap(w_down, "fsdp"))
+    ga_own, ga_far = (gain_attn.astype(F32), small_far[:half].astype(F32))
+    gf_own, gf_far = (gain_ffn.astype(F32), small_far[half : 2 * half].astype(F32))
+    bias_far = small_far[2 * half :].reshape(rel_bias.shape)
+    bias_local = jnp.where(
+        first,
+        jnp.concatenate([rel_bias, bias_far]),
+        jnp.concatenate([bias_far, rel_bias]),
+    )
+    tok_own, tok_far = halves(tokens)
+    cot_own, cot_far = halves(cotangent)
+    tok_own, tok_far = (tok_own.astype(F32), tok_far.astype(F32))
+
+    def norm_scale(own, far):
+        total = jnp.sum(own * own, axis=1, keepdims=True) + jnp.sum(far * far, axis=1, keepdims=True)
+        return lax.rsqrt(total / (2 * half) + EPS)
+
+    scale_a = norm_scale(tok_own, tok_far)
+    normed_own = (tok_own * scale_a * ga_own).astype(BF16)
+    normed_far = (tok_far * scale_a * ga_far).astype(BF16)
+    queries = (dot_f32(normed_own, w_query) + dot_f32(normed_far, wq_far)).astype(BF16)
+    keys_here = (dot_f32(normed_own, w_key) + dot_f32(normed_far, wk_far)).astype(BF16)
+    values_here = (dot_f32(normed_own, w_value) + dot_f32(normed_far, wv_far)).astype(BF16)
+    key_block = min(512, group_rows)
+    block_count = group_rows // key_block
+    ranges = bucket_ranges(rel_buckets)
+    order_row = token_order[0]
+    seq_ids = segment_of(order_row, seq_lengths[0])
+    row_start = lax.axis_index("ctx") * local_rows
+    query_pos = lax.dynamic_slice_in_dim(order_row, row_start, local_rows)
+    query_seg = lax.dynamic_slice_in_dim(seq_ids, row_start, local_rows)
+    pos_blocks = order_row.reshape(block_count, key_block)
+    seg_blocks = seq_ids.reshape(block_count, key_block)
+    query_heads = queries.reshape(local_rows, head_count, DH)
+    key_all, value_all = (
+        lax.all_gather(keys_here, "ctx", axis=0, tiled=True),
+        lax.all_gather(values_here, "ctx", axis=0, tiled=True),
+    )
+
+    def blocked(array_in):
+        return array_in.reshape(block_count, key_block, head_count, DH)
+
+    def forward_block(running, inputs):
+        summed, totals, head_top = running
+        key_blk, value_blk, pos_blk, seg_blk = inputs
+        raw_scores = jnp.einsum(
+            "thd,khd->htk", query_heads, key_blk, preferred_element_type=jnp.float32
+        )
+        bucket_hot, pair_bias, same_seq = pair_terms(
+            query_pos, query_seg, pos_blk, seg_blk, ranges, bias_local
+        )
+        weights = jnp.where(same_seq, jnp.exp(raw_scores + pair_bias), 0.0)
+        totals = totals + jnp.sum(weights, axis=2)
+        summed = summed + jnp.einsum(
+            "htk,khd->thd",
+            weights.astype(jnp.bfloat16),
+            value_blk,
+            preferred_element_type=jnp.float32,
+        )
+        head_top = jnp.maximum(
+            head_top, jnp.max(jnp.where(same_seq, raw_scores, -1e30), axis=(1, 2))
+        )
+        return ((summed, totals, head_top), None)
+
+    start_state = (
+        jnp.zeros((local_rows, head_count, DH), jnp.float32),
+        jnp.zeros((head_count, local_rows), jnp.float32),
+        jnp.full((head_count,), -1e30, jnp.float32),
+    )
+    (summed, totals, head_top), unused = lax.scan(
+        forward_block, start_state, (blocked(key_all), blocked(value_all), pos_blocks, seg_blocks)
+    )
+    row_totals = jnp.transpose(totals)[:, :, None]
+    context_exact = summed / row_totals
+    context = context_exact.reshape(local_rows, head_count * DH).astype(jnp.bfloat16)
+    head_maxima = lax.pmax(head_top, ("fsdp", "ctx"))
+
+    def tp_sum(own, far):
+        own, far = (own.astype(BF16), far.astype(BF16))
+        return (
+            own.astype(F32) + swap(own, "tp").astype(F32),
+            far.astype(F32) + swap(far, "tp").astype(F32),
+        )
+
+    attn_own, attn_far = tp_sum(dot_f32(context, w_out), dot_f32(context, wo_far))
+    hid_own, hid_far = (tok_own + attn_own, tok_far + attn_far)
+    inner_grad = dot_nt(cot_own, w_down) + dot_nt(cot_far, wd_far)
+    scale_f = norm_scale(hid_own, hid_far)
+    nffn_own = (hid_own * scale_f * gf_own).astype(BF16)
+    nffn_far = (hid_far * scale_f * gf_far).astype(BF16)
+    gate_pre = dot_f32(nffn_own, w_gate) + dot_f32(nffn_far, wg_far)
+    up_pre = dot_f32(nffn_own, w_up) + dot_f32(nffn_far, wu_far)
+    inner_act = geglu(gate_pre, up_pre).astype(BF16)
+    unused, geglu_back = jax.vjp(geglu, gate_pre, up_pre)
+    gate_grad, up_grad = geglu_back(inner_grad)
+    gate_grad = gate_grad.astype(BF16)
+    up_grad = up_grad.astype(BF16)
+    dnf_own, dnf_far = tp_sum(
+        dot_nt(gate_grad, w_gate) + dot_nt(up_grad, w_up),
+        dot_nt(gate_grad, wg_far) + dot_nt(up_grad, wu_far),
+    )
+    ffn_own, ffn_far = tp_sum(dot_f32(inner_act, w_down), dot_f32(inner_act, wd_far))
+    output = whole(hid_own + ffn_own, hid_far + ffn_far).astype(BF16)
+
+    def pair_rows(own):
+        return jnp.concatenate([own, swap(own, "fsdp")])
+
+    def pair_half(own, far):
+        return jnp.concatenate([own, swap(far, "fsdp")])
+
+    nffn_pair = pair_half(nffn_own, nffn_far)
+    grad_gate = dot_tn(nffn_pair, pair_rows(gate_grad)).astype(BF16)
+    grad_up = dot_tn(nffn_pair, pair_rows(up_grad)).astype(BF16)
+    grad_down = dot_tn(pair_rows(inner_act), pair_half(cot_own, cot_far)).astype(BF16)
+    down_rows = grad_down.shape[0] // 2
+
+    def norm_back(own, far, scale, gain_own, gain_far, dy_own, dy_far):
+        mean_term = (
+            jnp.sum(gain_own * dy_own * own, axis=1, keepdims=True)
+            + jnp.sum(gain_far * dy_far * far, axis=1, keepdims=True)
+        ) / (2 * half)
+        cubed = scale * scale * scale * mean_term
+        return (
+            scale * (gain_own * dy_own) - own * cubed,
+            scale * (gain_far * dy_far) - far * cubed,
+            jnp.sum(dy_own * own * scale, axis=0),
+            jnp.sum(dy_far * far * scale, axis=0),
+        )
+
+    back_own, back_far, dgf_own, dgf_far = norm_back(
+        hid_own, hid_far, scale_f, gf_own, gf_far, dnf_own, dnf_far
+    )
+    hgrad_own = cot_own.astype(F32) + back_own
+    hgrad_far = cot_far.astype(F32) + back_far
+    ag_own, ag_far = (hgrad_own.astype(BF16), hgrad_far.astype(BF16))
+    grad_out = dot_tn(pair_rows(context), pair_half(ag_own, ag_far)).astype(BF16)
+    context_grad = dot_nt(ag_own, w_out) + dot_nt(ag_far, wo_far)
+    context_grad = context_grad.reshape(local_rows, head_count, DH)
+    summed_grad = (context_grad / row_totals).astype(jnp.bfloat16)
+    total_grad = jnp.transpose(-jnp.sum(context_grad * context_exact, axis=2) / row_totals[:, :, 0])
+    key_back, value_back = (key_all, value_all)
+
+    def backward_block(running, inputs):
+        query_acc, bias_acc = running
+        key_blk, value_blk, pos_blk, seg_blk = inputs
+        raw_scores = jnp.einsum(
+            "thd,khd->htk", query_heads, key_blk, preferred_element_type=jnp.float32
+        )
+        bucket_hot, pair_bias, same_seq = pair_terms(
+            query_pos, query_seg, pos_blk, seg_blk, ranges, bias_local
+        )
+        weights = jnp.where(same_seq, jnp.exp(raw_scores + pair_bias), 0.0)
+        prob_grad = (
+            jnp.einsum("thd,khd->htk", summed_grad, value_blk, preferred_element_type=jnp.float32)
+            + total_grad[:, :, None]
+        )
+        score_grad = (weights * prob_grad).astype(jnp.bfloat16)
+        query_acc = query_acc + jnp.einsum(
+            "htk,khd->thd", score_grad, key_blk, preferred_element_type=jnp.float32
+        )
+        key_grad = jnp.einsum(
+            "htk,thd->khd", score_grad, query_heads, preferred_element_type=jnp.float32
+        )
+        value_grad = jnp.einsum(
+            "htk,thd->khd",
+            weights.astype(jnp.bfloat16),
+            summed_grad,
+            preferred_element_type=jnp.float32,
+        )
+        bucket_sums = jnp.einsum(
+            "htk,btk->hb", score_grad, bucket_hot, preferred_element_type=jnp.float32
+        )
+        return ((query_acc, bias_acc + bucket_sums), (key_grad, value_grad))
+
+    zero_state = (
+        jnp.zeros((local_rows, head_count, DH), jnp.float32),
+        jnp.zeros((head_count, NB), jnp.float32),
+    )
+    (query_acc, bias_acc), (key_grads, value_grads) = lax.scan(
+        backward_block, zero_state, (blocked(key_back), blocked(value_back), pos_blocks, seg_blocks)
+    )
+    key_grad_all, value_grad_all = (
+        lax.psum_scatter(
+            key_grads.reshape(group_rows, head_count * DH).astype(jnp.bfloat16),
+            "ctx",
+            scatter_dimension=0,
+            tiled=True,
+        ).astype(jnp.float32),
+        lax.psum_scatter(
+            value_grads.reshape(group_rows, head_count * DH).astype(jnp.bfloat16),
+            "ctx",
+            scatter_dimension=0,
+            tiled=True,
+        ).astype(jnp.float32),
+    )
+    query_grad = query_acc.reshape(local_rows, head_count * DH).astype(jnp.bfloat16)
+    key_grad = key_grad_all.astype(jnp.bfloat16)
+    value_grad = value_grad_all.astype(jnp.bfloat16)
+    grad_bias = jnp.transpose(bias_acc)
+    (final_gate, down_low), (final_up, down_high) = ring_sum(
+        [grad_gate, grad_down[:down_rows]], [grad_up, grad_down[down_rows:]]
+    )
+    final_down = jnp.concatenate([down_low, down_high])
+    dn_own, dn_far = tp_sum(
+        dot_nt(query_grad, w_query) + dot_nt(key_grad, w_key) + dot_nt(value_grad, w_value),
+        dot_nt(query_grad, wq_far) + dot_nt(key_grad, wk_far) + dot_nt(value_grad, wv_far),
+    )
+    tback_own, tback_far, dga_own, dga_far = norm_back(
+        tok_own, tok_far, scale_a, ga_own, ga_far, dn_own, dn_far
+    )
+    grad_tokens = whole(hgrad_own + tback_own, hgrad_far + tback_far)
+    normed_pair = pair_half(normed_own, normed_far)
+    grad_query = dot_tn(normed_pair, pair_rows(query_grad)).astype(BF16)
+    grad_key = dot_tn(normed_pair, pair_rows(key_grad)).astype(BF16)
+    grad_value = dot_tn(normed_pair, pair_rows(value_grad)).astype(BF16)
+    (final_query, final_key), (final_value, final_out) = ring_sum(
+        [grad_query, grad_key], [grad_value, grad_out]
+    )
+    bias_rows = rel_bias.shape[0]
+    small_own = jnp.concatenate([dga_own, dgf_own])
+    small_sent = jnp.concatenate([dga_far, dgf_far])
+    bias_flat = grad_bias.reshape(2, -1)
+    small_own = jnp.concatenate([small_own, jnp.where(first, bias_flat[0], bias_flat[1])])
+    small_sent = jnp.concatenate([small_sent, jnp.where(first, bias_flat[1], bias_flat[0])])
+    small_sum = lax.psum(small_own + swap(small_sent, "fsdp"), "ctx")
+    final_gain_a, final_gain_f = (small_sum[:half], small_sum[half : 2 * half])
+    final_bias = small_sum[2 * half :].reshape(rel_bias.shape)
+    clip_scale = TAU_CLIP / jnp.maximum(head_maxima, TAU_CLIP)
+    column_scale = jnp.repeat(jnp.sqrt(clip_scale), DH)
+    query_clipped = (w_query.astype(F32) * column_scale[None, :]).astype(BF16)
+    key_clipped = (w_key.astype(F32) * column_scale[None, :]).astype(BF16)
+    return (
+        output,
+        grad_tokens,
+        final_gain_a,
+        final_query,
+        final_key,
+        final_value,
+        final_out,
+        final_bias,
+        final_gain_f,
+        final_gate,
+        final_up,
+        final_down,
+        head_maxima,
+        query_clipped,
+        key_clipped,
+    )
+
+
+def pick_program(mesh):
+    sizes = dict(mesh.shape)
+    if sizes["fsdp"] == 2 and sizes["ctx"] == len(RING) and sizes["tp"] == 2:
+        return per_device_ring
+    return per_device_generic
+
+
 def solution(mesh):
     in_specs = (
         P(("fsdp", "ctx"), None),
@@ -376,6 +743,7 @@
         P("fsdp", "tp"),
         P("fsdp", "tp"),
     )
+    per_device = pick_program(mesh)
     return jax.shard_map(
         per_device, mesh=mesh, in_specs=in_specs, out_specs=out_specs, check_vma=False
     )

time: 1830 us -> 1270 us (0.69)
  waiting for transfers between devices: 1240 us -> 502 us
  starting transfers between devices: 1.31 us -> 127 us
  other arithmetic: 54.1 us -> 102 us
  local copies, waits for them, and re-layouts: 123 us -> 143 us
  matrix products: 324 us -> 305 us
    psum x4 -> x0, waiting for transfers between devices: 802 us -> none  [the longest x1 698 us: per_device(): lax.psum(share_query.astype(jnp.bfloat16), 'ctx').astype(jnp.float32)]
    ppermute x0 -> x140, waiting for transfers between devices: none -> 394 us  [the longest x112 351 us: ring_sum(): lax.ppermute(held, 'ctx', pairs)]
    reduce_scatter x9 -> x2, waiting for transfers between devices: 239 us -> 0.01 us  [the longest x1 0.01 us: per_device_ring(): lax.psum_scatter(key_grads.reshape(group_rows, head_count * DH).astype(jn...]
    ppermute x0 -> x140, starting transfers between devices: none -> 127 us  [the longest x112 112 us: ring_sum(): lax.ppermute(held, 'ctx', pairs)]
    all_gather x9 -> x2, waiting for transfers between devices: 197 us -> 108 us  [the longest x1 54.9 us: per_device_ring(): lax.all_gather(values_here, 'ctx', axis=0, tiled=True)]
    dynamic_update_slice x0 -> x64, other arithmetic: none -> 46.2 us  [place(): lax.dynamic_update_slice_in_dim(result, held.astype(F32), jnp.mod(chunk,...]
    convert_element_type x16 -> x57, other arithmetic: 37.4 us -> 21.7 us  [the longest x48 11.4 us: ring_sum(): (got.astype(F32) + piece(array_in, me - way * (step + 1)).astype(F32)).as...]
    dot_general x21 -> x35, matrix products: 116 us -> 108 us  [the longest x14 48.6 us: dot_nt(): lax.dot_general(left, right, (((1,), (1,)), ((), ())), preferred_element_...]
  transfers between devices with their start and end apart: 23 -> 144, of which waited for: 17 -> 71; matrix products, arithmetic and copies ran while one was open for 16% -> 29% of each run, Pallas kernels for 0% -> 0%
where the time goes in v1:
time: 1270 us
  waiting for transfers between devices  502 us (40%)
  matrix products  305 us (24%)
  local copies, waits for them, and re-layouts  143 us (11%)
  starting transfers between devices  127 us (10%)
  other arithmetic  102 us (8%)
  blocking collectives  68.8 us (5%)
  between operations  16.9 us (1%)
    ppermute x112, waiting for transfers between devices, ring_sum(): lax.ppermute(held, 'ctx', pairs)  351 us
    ppermute x112, starting transfers between devices, ring_sum(): lax.ppermute(held, 'ctx', pairs)  112 us
    all_gather x1, waiting for transfers between devices, per_device_ring(): lax.all_gather(values_here, 'ctx', axis=0, tiled=True)  54.9 us
    all_gather x1, waiting for transfers between devices, per_device_ring(): lax.all_gather(keys_here, 'ctx', axis=0, tiled=True)  53 us
    dot_general x14, matrix products, dot_nt(): lax.dot_general(left, right, (((1,), (1,)), ((), ())), preferred_element_...  48.6 us
    dynamic_update_slice x64, other arithmetic, place(): lax.dynamic_update_slice_in_dim(result, held.astype(F32), jnp.mod(chunk,...  46.2 us
    ppermute x28, waiting for transfers between devices, swap(): return lax.ppermute(array_in, axis_name, [(0, 1), (1, 0)])  43.3 us
    dot_general x4, local copies, waits for them, and re-layouts, pair_terms(): jnp.einsum('btk,bh->htk', bucket_hot, bias_table, preferred_element_type=...  39.6 us
  transfers between devices with their start and end apart: 144, of which 71 were waited for; matrix products, arithmetic and copies ran while one was open for 29% of the time, Pallas kernels for 0%

profile of v1, /device:TPU:0, one launch (start us, length us, event | category | flops | bytes accessed | tf_op | source)
XLA Modules:
  0.0 1266.2 jit_solution(9910260092884709949)
XLA Ops:
  38.3 54.9 %all-gather.3.cloned.1.call-done = bf16[2048,1024]{1,0:T(8,128)(2,1)} async-done(((bf16[256,1024]{1,0:T(8,128)(2,1)}), bf16[2048,1024]{1,0:T(8,128)(2,1)}) %all-gather.3.cloned.1.call-update) | async-done | bytes 4194320 | tf_op jit(solution)/shard_map/all_gather | solution.py:490
  93.2 11.7 reshape.322
  104.9 9.8 copy.80
  114.6 53.0 %all-gather.5.cloned.1.call-done = bf16[2048,1024]{1,0:T(8,128)(2,1)} async-done(((bf16[256,1024]{1,0:T(8,128)(2,1)}), bf16[2048,1024]{1,0:T(8,128)(2,1)}) %all-gather.5.cloned.1.call-update) | async-done | bytes 4194320 | tf_op jit(solution)/shard_map/all_gather | solution.py:489
  167.6 11.5 reshape.323
  179.1 9.7 copy.81
  188.9 126.6 %while.40 = (s32[]{:T(128)}, f32[256,16,64]{0,2,1:T(8,128)S(1)}, f32[16,256]{1,0:T(8,128)S(1)}, f32[16]{0:T(128)S(1)}, bf16[4,512,16,64]{1,3,2,0:T(8,128)(2,1)},...) while((s32[]{:T(128)}, f32[256,16,64]{0,2,1:T(8,128)S(1)}, ...), condition=%wide.region_9.10_spmd.clone, body=%wide.region_6.9_spmd.clone.sunk | while | flops 701501440 | bytes 64962224 | solution.py:523
  195.0 9.9 copy.111
  205.0 7.6 fusion.248
  212.6 7.8 fusion.249
  226.6 9.9 copy.111
  236.6 7.6 fusion.248
  244.2 7.8 fusion.249
  258.2 9.9 copy.111
  268.2 7.6 fusion.248
  275.8 7.8 fusion.249
  289.8 9.9 copy.111
  299.8 7.6 fusion.248
  307.4 7.8 fusion.249
  333.4 8.5 collective-permute-done.6
  354.9 7.0 multiply_convert_fusion.2
  394.7 11.2 collective-permute-done.9
  405.9 8.2 collective-permute-done.11
  433.3 126.1 %while.41 = (s32[]{:T(128)}, f32[256,16,64]{0,2,1:T(8,128)S(1)}, f32[16,32]{1,0:T(8,128)S(1)}, bf16[4,512,16,64]{1,3,2,0:T(8,128)(2,1)}, bf16[4,512,16,64]{1,3,2...) while((s32[]{:T(128)}, f32[256,16,64]{0,2,1:T(8,128)S(1)}, ...), condition=%wide.region_16.17_spmd.clone, body=%wide.region_15.16_spmd.clone.sunk | while | flops 1649411072 | bytes 214732752 | solution.py:632
  437.5 7.4 fusion.264
  468.9 7.4 fusion.264
  500.3 7.4 fusion.264
  531.7 7.4 fusion.264
  570.1 35.0 %pmax.7 = f32[16]{0:T(128)S(1)} all-reduce(f32[16]{0:T(128)S(1)} %copy-done.67), channel_id=1, replica_groups=mesh['fsdp'=2,'ctx'=8,'tp'=2] {'fsdp','ctx'}, use_global_device_ids=true, to_apply=%region_26.27 | all-reduce | flops 16 | bytes 128 | tf_op jit(solution)/shard_map/pmax | solution.py:529
  654.6 20.4 %collective-permute-done.20 = bf16[128,1024]{1,0:T(8,128)(2,1)S(1)} collective-permute-done((bf16[128,1024]{1,0:T(8,128)(2,1)S(1)}, bf16[128,1024]{1,0:T(8,128)(2,1)S(1)}, u32[]{:S(2)}, u32[]{:S(2)}) %collective-permute-start.20) | collective-permute-done | bytes 262176 | tf_op jit(solution)/shard_map/ppermute | solution.py:387
  677.5 6.7 collective-permute-done.66
  689.1 8.1 collective-permute-done.21
  709.0 10.3 collective-permute-done.127
  720.1 8.7 collective-permute-done.22
  733.1 27.7 %collective-permute-done.128 = bf16[160,1024]{1,0:T(8,128)(2,1)S(1)} collective-permute-done((bf16[160,1024]{1,0:T(8,128)(2,1)S(1)}, bf16[160,1024]{1,0:T(8,128)(2,1)S(1)}, u32[]{:S(2)}, u32[]{:S(2)}) %collective-permute-start.128) | collective-permute-done | bytes 327712 | tf_op jit(solution)/shard_map/ppermute | solution.py:387
  789.1 23.1 %collective-permute-done.25 = bf16[128,1024]{1,0:T(8,128)(2,1)S(1)} collective-permute-done((bf16[128,1024]{1,0:T(8,128)(2,1)S(1)}, bf16[128,1024]{1,0:T(8,128)(2,1)S(1)}, u32[]{:S(2)}, u32[]{:S(2)}) %collective-permute-start.25) | collective-permute-done | bytes 262176 | tf_op jit(solution)/shard_map/ppermute | solution.py:387
  817.5 7.0 collective-permute-done.71
  891.5 18.8 %collective-permute-done.30 = bf16[128,1024]{1,0:T(8,128)(2,1)S(1)} collective-permute-done((bf16[128,1024]{1,0:T(8,128)(2,1)S(1)}, bf16[128,1024]{1,0:T(8,128)(2,1)S(1)}, u32[]{:S(2)}, u32[]{:S(2)}) %collective-permute-start.30) | collective-permute-done | bytes 262176 | tf_op jit(solution)/shard_map/ppermute | solution.py:408
  922.2 9.7 collective-permute-done.77
  947.2 7.0 collective-permute-done.136
  958.5 13.9 %collective-permute-done.137 = bf16[160,1024]{1,0:T(8,128)(2,1)S(1)} collective-permute-done((bf16[160,1024]{1,0:T(8,128)(2,1)S(1)}, bf16[160,1024]{1,0:T(8,128)(2,1)S(1)}, u32[]{:S(2)}, u32[]{:S(2)}) %collective-permute-start.137) | collective-permute-done | bytes 327712 | tf_op jit(solution)/shard_map/ppermute | solution.py:408
  987.4 9.8 collective-permute-done.139
  1013.6 10.3 pad_maximum_fusion
  1030.6 9.8 collective-permute-done.89
  1044.8 12.9 %collective-permute-done.90 = bf16[128,2560]{1,0:T(8,128)(2,1)S(1)} collective-permute-done((bf16[128,2560]{1,0:T(8,128)(2,1)S(1)}, bf16[128,2560]{1,0:T(8,128)(2,1)S(1)}, u32[]{:S(2)}, u32[]{:S(2)}) %collective-permute-start.90) | collective-permute-done | bytes 655392 | tf_op jit(solution)/shard_map/ppermute | solution.py:408
  1062.1 12.7 %collective-permute-done.91 = bf16[128,2560]{1,0:T(8,128)(2,1)} collective-permute-done((bf16[128,2560]{1,0:T(8,128)(2,1)S(1)}, bf16[128,2560]{1,0:T(8,128)(2,1)}, u32[]{:S(2)}, u32[]{:S(2)}) %collective-permute-start.91) | collective-permute-done | bytes 655392 | tf_op jit(solution)/shard_map/ppermute | solution.py:408
  1132.4 33.8 %psum.7 = f32[2304]{0:T(1024)S(1)} all-reduce(f32[2304]{0:T(1024)S(1)} %maximum_add_fusion), channel_id=1, replica_groups=mesh['fsdp'=2,'ctx'=8,'tp'=2] {'ctx'}, use_global_device_ids=true, to_apply=%region_25.26 | all-reduce | flops 2304 | bytes 18432 | tf_op jit(solution)/shard_map/psum | solution.py:678
  1181.6 6.9 collective-permute-done.38
  (788 shorter events, 638.7 us)
Async XLA Ops:
  7.2 86.0 %all-gather.3.cloned.1.call-start = ((), (), s32[]{:S(2)}) async-start(), calls=%async_computation.2 | async-start | bytes 4718592 | tf_op jit(solution)/shard_map/all_gather | solution.py:490
  17.0 150.6 %all-gather.5.cloned.1.call-start = ((), (), s32[]{:S(2)}) async-start(), calls=%async_computation.3 | async-start | bytes 4718592 | tf_op jit(solution)/shard_map/all_gather | solution.py:489
  25.3 1056.4 %reduce-scatter.3.cloned.1.call-start = ((), (), s32[]{:S(2)}) async-start(), calls=%async_computation.4 | async-start | bytes 4718592 | tf_op jit(solution)/shard_map/reduce_scatter | solution.py:636
  26.3 293.3 %collective-permute-start.5 = (bf16[1024,1024]{1,0:T(8,128)(2,1)}, bf16[1024,1024]{1,0:T(8,128)(2,1)}, u32[]{:S(2)}, u32[]{:S(2)}) collective-permute-start(bf16[1024,1024]{1,0:T(8,128)(2,1)} %param.28), channel_id=1, source_target_pairs={{0,16},{16,0},{1,17},{17,1},{2,18},{18,2},{3,19},{19,3},{4,20},{20... | collective-permute-start | bytes 6291464 | tf_op jit(solution)/shard_map/ppermute | solution.py:357
  26.4 320.4 %collective-permute-start.7 = (bf16[1024,2560]{1,0:T(8,128)(2,1)}, bf16[1024,2560]{1,0:T(8,128)(2,1)}, u32[]{:S(2)}, u32[]{:S(2)}) collective-permute-start(bf16[1024,2560]{1,0:T(8,128)(2,1)} %param.31), channel_id=1, source_target_pairs={{0,16},{16,0},{1,17},{17,1},{2,18},{18,2},{3,19},{19,3},{4,20},{20... | collective-permute-start | bytes 15728648 | tf_op jit(solution)/shard_map/ppermute | solution.py:357
  26.8 324.0 %collective-permute-start.8 = (bf16[1024,2560]{1,0:T(8,128)(2,1)}, bf16[1024,2560]{1,0:T(8,128)(2,1)}, u32[]{:S(2)}, u32[]{:S(2)}) collective-permute-start(bf16[1024,2560]{1,0:T(8,128)(2,1)} %param.32), channel_id=1, source_target_pairs={{0,16},{16,0},{1,17},{17,1},{2,18},{18,2},{3,19},{19,3},{4,20},{20... | collective-permute-start | bytes 15728648 | tf_op jit(solution)/shard_map/ppermute | solution.py:357
  27.0 328.0 %collective-permute-start.10 = (bf16[2560,1024]{1,0:T(8,128)(2,1)}, bf16[2560,1024]{1,0:T(8,128)(2,1)}, u32[]{:S(2)}, u32[]{:S(2)}) collective-permute-start(bf16[2560,1024]{1,0:T(8,128)(2,1)} %param.33), channel_id=1, source_target_pairs={{0,16},{16,0},{1,17},{17,1},{2,18},{18,2},{3,19},{19,3},{4,20},{20... | collective-permute-start | bytes 15728648 | tf_op jit(solution)/shard_map/ppermute | solution.py:357
  382.5 23.4 %collective-permute-start.9 = (bf16[256,1024]{1,0:T(8,128)(2,1)}, bf16[256,1024]{1,0:T(8,128)(2,1)}, u32[]{:S(2)}, u32[]{:S(2)}) collective-permute-start(bf16[256,1024]{1,0:T(8,128)(2,1)} %convolution_convert_fusion.8), channel_id=1, source_target_pairs={{0,1},{1,0},{2,3},{3,2},{4,5},{5,4},{6,7},{7,6},{8,9},{9,8},{10,11... | collective-permute-start | bytes 1572872 | tf_op jit(solution)/shard_map/ppermute | solution.py:357
  388.8 25.3 %collective-permute-start.11 = (bf16[256,1024]{1,0:T(8,128)(2,1)}, bf16[256,1024]{1,0:T(8,128)(2,1)}, u32[]{:S(2)}, u32[]{:S(2)}) collective-permute-start(bf16[256,1024]{1,0:T(8,128)(2,1)} %convolution_convert_fusion.7), channel_id=1, source_target_pairs={{0,1},{1,0},{2,3},{3,2},{4,5},{5,4},{6,7},{7,6},{8,9},{9,8},{10,11... | collective-permute-start | bytes 1572872 | tf_op jit(solution)/shard_map/ppermute | solution.py:357
  568.6 516.3 %reduce-scatter.5.cloned.1.call-start = ((), (), s32[]{:S(2)}) async-start(), calls=%async_computation.5 | async-start | bytes 4718592 | tf_op jit(solution)/shard_map/reduce_scatter | solution.py:642
  569.5 56.1 %collective-permute-start.17 = (bf16[256,1024]{1,0:T(8,128)(2,1)}, bf16[256,1024]{1,0:T(8,128)(2,1)}, u32[]{:S(2)}, u32[]{:S(2)}) collective-permute-start(bf16[256,1024]{1,0:T(8,128)(2,1)} %copy-done.21), channel_id=1, source_target_pairs={{0,16},{16,0},{1,17},{17,1},{2,18},{18,2},{3,19},{19,3},{4,20},{20... | collective-permute-start | bytes 1572872 | tf_op jit(solution)/shard_map/ppermute | solution.py:357
  569.6 59.6 %collective-permute-start.63 = (bf16[256,1024]{0,1:T(8,128)(2,1)}, bf16[256,1024]{0,1:T(8,128)(2,1)}, u32[]{:S(2)}, u32[]{:S(2)}) collective-permute-start(bf16[256,1024]{0,1:T(8,128)(2,1)} %bitcast.241), channel_id=1, source_target_pairs={{0,16},{16,0},{1,17},{17,1},{2,18},{18,2},{3,19},{19,3},{4,20},{20... | collective-permute-start | bytes 1572872 | tf_op jit(solution)/shard_map/ppermute | solution.py:357
  640.2 65.2 %collective-permute-start.81 = (bf16[128,2560]{1,0:T(8,128)(2,1)}, bf16[128,2560]{1,0:T(8,128)(2,1)S(1)}, u32[]{:S(2)}, u32[]{:S(2)}) collective-permute-start(bf16[128,2560]{1,0:T(8,128)(2,1)} %constant_dynamic-slice_fusion.7), channel_id=1, source_target_pairs={{0,4},{4,8},{8,12},{12,14},{14,10},{10,6},{6,2},{2,0},{1,5},{5,9},... | collective-permute-start | bytes 1966088 | tf_op jit(solution)/shard_map/ppermute | solution.py:387
  644.5 63.1 %collective-permute-start.96 = (bf16[128,2560]{1,0:T(8,128)(2,1)}, bf16[128,2560]{1,0:T(8,128)(2,1)}, u32[]{:S(2)}, u32[]{:S(2)}) collective-permute-start(bf16[128,2560]{1,0:T(8,128)(2,1)} %constant_dynamic-slice_fusion.6), channel_id=1, source_target_pairs={{4,0},{8,4},{12,8},{14,12},{10,14},{6,10},{2,6},{0,2},{5,1},{9,5},... | collective-permute-start | bytes 1966088 | tf_op jit(solution)/shard_map/ppermute | solution.py:387
  650.3 35.3 %collective-permute-start.126 = (bf16[160,1024]{1,0:T(8,128)(2,1)S(1)}, bf16[160,1024]{1,0:T(8,128)(2,1)S(1)}, u32[]{:S(2)}, u32[]{:S(2)}) collective-permute-start(bf16[160,1024]{1,0:T(8,128)(2,1)S(1)} %constant_dynamic-slice_fusion.4), channel_id=1, source_target_pairs={{4,0},{8,4},{12,8},{14,12},{10,14},{6,10},{2,6},{0,2},{5,1},{9,5},... | collective-permute-start | bytes 983048 | tf_op jit(solution)/shard_map/ppermute | solution.py:387
  651.4 23.6 %collective-permute-start.20 = (bf16[128,1024]{1,0:T(8,128)(2,1)S(1)}, bf16[128,1024]{1,0:T(8,128)(2,1)S(1)}, u32[]{:S(2)}, u32[]{:S(2)}) collective-permute-start(bf16[128,1024]{1,0:T(8,128)(2,1)S(1)} %add_convert_fusion.55), channel_id=1, source_target_pairs={{0,4},{4,8},{8,12},{12,14},{14,10},{10,6},{6,2},{2,0},{1,5},{5,9},... | collective-permute-start | bytes 786440 | tf_op jit(solution)/shard_map/ppermute | solution.py:387
  654.5 29.8 %collective-permute-start.66 = (bf16[128,1024]{1,0:T(8,128)(2,1)S(1)}, bf16[128,1024]{1,0:T(8,128)(2,1)S(1)}, u32[]{:S(2)}, u32[]{:S(2)}) collective-permute-start(bf16[128,1024]{1,0:T(8,128)(2,1)S(1)} %add_convert_fusion.34), channel_id=1, source_target_pairs={{4,0},{8,4},{12,8},{14,12},{10,14},{6,10},{2,6},{0,2},{5,1},{9,5},... | collective-permute-start | bytes 786440 | tf_op jit(solution)/shard_map/ppermute | solution.py:387
  686.5 32.7 %collective-permute-start.127 = (bf16[160,1024]{1,0:T(8,128)(2,1)S(1)}, bf16[160,1024]{1,0:T(8,128)(2,1)S(1)}, u32[]{:S(2)}, u32[]{:S(2)}) collective-permute-start(bf16[160,1024]{1,0:T(8,128)(2,1)S(1)} %add_convert_fusion.20), channel_id=1, source_target_pairs={{4,0},{8,4},{12,8},{14,12},{10,14},{6,10},{2,6},{0,2},{5,1},{9,5},... | collective-permute-start | bytes 983048 | tf_op jit(solution)/shard_map/ppermute | solution.py:387
  705.3 23.5 %collective-permute-start.22 = (bf16[128,1024]{1,0:T(8,128)(2,1)S(1)}, bf16[128,1024]{1,0:T(8,128)(2,1)S(1)}, u32[]{:S(2)}, u32[]{:S(2)}) collective-permute-start(bf16[128,1024]{1,0:T(8,128)(2,1)S(1)} %add_convert_fusion.53), channel_id=1, source_target_pairs={{0,4},{4,8},{8,12},{12,14},{14,10},{10,6},{6,2},{2,0},{1,5},{5,9},... | collective-permute-start | bytes 786440 | tf_op jit(solution)/shard_map/ppermute | solution.py:387
  705.4 26.0 %collective-permute-start.68 = (bf16[128,1024]{1,0:T(8,128)(2,1)S(1)}, bf16[128,1024]{1,0:T(8,128)(2,1)S(1)}, u32[]{:S(2)}, u32[]{:S(2)}) collective-permute-start(bf16[128,1024]{1,0:T(8,128)(2,1)S(1)} %add_convert_fusion.32), channel_id=1, source_target_pairs={{4,0},{8,4},{12,8},{14,12},{10,14},{6,10},{2,6},{0,2},{5,1},{9,5},... | collective-permute-start | bytes 786440 | tf_op jit(solution)/shard_map/ppermute | solution.py:387
  707.6 65.1 %collective-permute-start.82 = (bf16[128,2560]{1,0:T(8,128)(2,1)S(1)}, bf16[128,2560]{1,0:T(8,128)(2,1)S(1)}, u32[]{:S(2)}, u32[]{:S(2)}) collective-permute-start(bf16[128,2560]{1,0:T(8,128)(2,1)S(1)} %add_convert_fusion.13), channel_id=1, source_target_pairs={{0,4},{4,8},{8,12},{12,14},{14,10},{10,6},{6,2},{2,0},{1,5},{5,9},... | collective-permute-start | bytes 1966088 | tf_op jit(solution)/shard_map/ppermute | solution.py:387
  719.2 56.2 %collective-permute-start.97 = (bf16[128,2560]{1,0:T(8,128)(2,1)S(1)}, bf16[128,2560]{1,0:T(8,128)(2,1)S(1)}, u32[]{:S(2)}, u32[]{:S(2)}) collective-permute-start(bf16[128,2560]{1,0:T(8,128)(2,1)S(1)} %add_convert_fusion.6), channel_id=1, source_target_pairs={{4,0},{8,4},{12,8},{14,12},{10,14},{6,10},{2,6},{0,2},{5,1},{9,5},... | collective-permute-start | bytes 1966088 | tf_op jit(solution)/shard_map/ppermute | solution.py:387
  719.3 41.5 %collective-permute-start.128 = (bf16[160,1024]{1,0:T(8,128)(2,1)S(1)}, bf16[160,1024]{1,0:T(8,128)(2,1)S(1)}, u32[]{:S(2)}, u32[]{:S(2)}) collective-permute-start(bf16[160,1024]{1,0:T(8,128)(2,1)S(1)} %add_convert_fusion.19), channel_id=1, source_target_pairs={{4,0},{8,4},{12,8},{14,12},{10,14},{6,10},{2,6},{0,2},{5,1},{9,5},... | collective-permute-start | bytes 983048 | tf_op jit(solution)/shard_map/ppermute | solution.py:387
  728.8 32.1 %collective-permute-start.114 = (bf16[160,1024]{1,0:T(8,128)(2,1)S(1)}, bf16[160,1024]{1,0:T(8,128)(2,1)S(1)}, u32[]{:S(2)}, u32[]{:S(2)}) collective-permute-start(bf16[160,1024]{1,0:T(8,128)(2,1)S(1)} %add_convert_fusion.26), channel_id=1, source_target_pairs={{0,4},{4,8},{8,12},{12,14},{14,10},{10,6},{6,2},{2,0},{1,5},{5,9},... | collective-permute-start | bytes 983048 | tf_op jit(solution)/shard_map/ppermute | solution.py:387
  731.4 32.7 %collective-permute-start.23 = (bf16[128,1024]{1,0:T(8,128)(2,1)S(1)}, bf16[128,1024]{1,0:T(8,128)(2,1)S(1)}, u32[]{:S(2)}, u32[]{:S(2)}) collective-permute-start(bf16[128,1024]{1,0:T(8,128)(2,1)S(1)} %add_convert_fusion.52), channel_id=1, source_target_pairs={{0,4},{4,8},{8,12},{12,14},{14,10},{10,6},{6,2},{2,0},{1,5},{5,9},... | collective-permute-start | bytes 786440 | tf_op jit(solution)/shard_map/ppermute | solution.py:387
  775.5 67.9 %collective-permute-start.83 = (bf16[128,2560]{1,0:T(8,128)(2,1)S(1)}, bf16[128,2560]{1,0:T(8,128)(2,1)S(1)}, u32[]{:S(2)}, u32[]{:S(2)}) collective-permute-start(bf16[128,2560]{1,0:T(8,128)(2,1)S(1)} %add_convert_fusion.12), channel_id=1, source_target_pairs={{0,4},{4,8},{8,12},{12,14},{14,10},{10,6},{6,2},{2,0},{1,5},{5,9},... | collective-permute-start | bytes 1966088 | tf_op jit(solution)/shard_map/ppermute | solution.py:387
  780.2 63.7 %collective-permute-start.98 = (bf16[128,2560]{1,0:T(8,128)(2,1)S(1)}, bf16[128,2560]{1,0:T(8,128)(2,1)S(1)}, u32[]{:S(2)}, u32[]{:S(2)}) collective-permute-start(bf16[128,2560]{1,0:T(8,128)(2,1)S(1)} %add_convert_fusion.5), channel_id=1, source_target_pairs={{4,0},{8,4},{12,8},{14,12},{10,14},{6,10},{2,6},{0,2},{5,1},{9,5},... | collective-permute-start | bytes 1966088 | tf_op jit(solution)/shard_map/ppermute | solution.py:387
  782.8 43.4 %collective-permute-start.130 = (bf16[160,1024]{1,0:T(8,128)(2,1)S(1)}, bf16[160,1024]{1,0:T(8,128)(2,1)S(1)}, u32[]{:S(2)}, u32[]{:S(2)}) collective-permute-start(bf16[160,1024]{1,0:T(8,128)(2,1)S(1)} %add_convert_fusion.17), channel_id=1, source_target_pairs={{4,0},{8,4},{12,8},{14,12},{10,14},{6,10},{2,6},{0,2},{5,1},{9,5},... | collective-permute-start | bytes 983048 | tf_op jit(solution)/shard_map/ppermute | solution.py:387
  786.3 25.8 %collective-permute-start.25 = (bf16[128,1024]{1,0:T(8,128)(2,1)S(1)}, bf16[128,1024]{1,0:T(8,128)(2,1)S(1)}, u32[]{:S(2)}, u32[]{:S(2)}) collective-permute-start(bf16[128,1024]{1,0:T(8,128)(2,1)S(1)} %add_convert_fusion.50), channel_id=1, source_target_pairs={{0,4},{4,8},{8,12},{12,14},{14,10},{10,6},{6,2},{2,0},{1,5},{5,9},... | collective-permute-start | bytes 786440 | tf_op jit(solution)/shard_map/ppermute | solution.py:387
  786.4 38.1 %collective-permute-start.71 = (bf16[128,1024]{1,0:T(8,128)(2,1)S(1)}, bf16[128,1024]{1,0:T(8,128)(2,1)S(1)}, u32[]{:S(2)}, u32[]{:S(2)}) collective-permute-start(bf16[128,1024]{1,0:T(8,128)(2,1)S(1)} %add_convert_fusion.29), channel_id=1, source_target_pairs={{4,0},{8,4},{12,8},{14,12},{10,14},{6,10},{2,6},{0,2},{5,1},{9,5},... | collective-permute-start | bytes 786440 | tf_op jit(solution)/shard_map/ppermute | solution.py:387
  843.9 40.4 %collective-permute-start.84 = (bf16[128,2560]{1,0:T(8,128)(2,1)S(1)}, bf16[128,2560]{1,0:T(8,128)(2,1)S(1)}, u32[]{:S(2)}, u32[]{:S(2)}) collective-permute-start(bf16[128,2560]{1,0:T(8,128)(2,1)S(1)} %add_convert_fusion.11), channel_id=1, source_target_pairs={{0,4},{4,8},{8,12},{12,14},{14,10},{10,6},{6,2},{2,0},{1,5},{5,9},... | collective-permute-start | bytes 1966088 | tf_op jit(solution)/shard_map/ppermute | solution.py:387
  847.2 42.6 %collective-permute-start.99 = (bf16[128,2560]{1,0:T(8,128)(2,1)S(1)}, bf16[128,2560]{1,0:T(8,128)(2,1)S(1)}, u32[]{:S(2)}, u32[]{:S(2)}) collective-permute-start(bf16[128,2560]{1,0:T(8,128)(2,1)S(1)} %add_convert_fusion.4), channel_id=1, source_target_pairs={{4,0},{8,4},{12,8},{14,12},{10,14},{6,10},{2,6},{0,2},{5,1},{9,5},... | collective-permute-start | bytes 1966088 | tf_op jit(solution)/shard_map/ppermute | solution.py:387
  881.7 31.3 %collective-permute-start.134 = (bf16[160,1024]{1,0:T(8,128)(2,1)S(1)}, bf16[160,1024]{1,0:T(8,128)(2,1)S(1)}, u32[]{:S(2)}, u32[]{:S(2)}) collective-permute-start(bf16[160,1024]{1,0:T(8,128)(2,1)S(1)} %collective-permute-done.133), channel_id=1, source_target_pairs={{4,0},{8,4},{12,8},{14,12},{10,14},{6,10},{2,6},{0,2},{5,1},{9,5},... | collective-permute-start | bytes 983048 | tf_op jit(solution)/shard_map/ppermute | solution.py:408
  884.3 31.7 %collective-permute-start.120 = (bf16[160,1024]{1,0:T(8,128)(2,1)S(1)}, bf16[160,1024]{1,0:T(8,128)(2,1)S(1)}, u32[]{:S(2)}, u32[]{:S(2)}) collective-permute-start(bf16[160,1024]{1,0:T(8,128)(2,1)S(1)} %collective-permute-done.119), channel_id=1, source_target_pairs={{0,4},{4,8},{8,12},{12,14},{14,10},{10,6},{6,2},{2,0},{1,5},{5,9},... | collective-permute-start | bytes 983048 | tf_op jit(solution)/shard_map/ppermute | solution.py:408
  887.3 55.2 %collective-permute-start.85 = (bf16[128,2560]{1,0:T(8,128)(2,1)S(1)}, bf16[128,2560]{1,0:T(8,128)(2,1)S(1)}, u32[]{:S(2)}, u32[]{:S(2)}) collective-permute-start(bf16[128,2560]{1,0:T(8,128)(2,1)S(1)} %add_convert_fusion.10), channel_id=1, source_target_pairs={{0,4},{4,8},{8,12},{12,14},{14,10},{10,6},{6,2},{2,0},{1,5},{5,9},... | collective-permute-start | bytes 1966088 | tf_op jit(solution)/shard_map/ppermute | solution.py:387
  910.3 34.1 %collective-permute-start.100 = (bf16[128,2560]{1,0:T(8,128)(2,1)S(1)}, bf16[128,2560]{1,0:T(8,128)(2,1)S(1)}, u32[]{:S(2)}, u32[]{:S(2)}) collective-permute-start(bf16[128,2560]{1,0:T(8,128)(2,1)S(1)} %add_convert_fusion.3), channel_id=1, source_target_pairs={{4,0},{8,4},{12,8},{14,12},{10,14},{6,10},{2,6},{0,2},{5,1},{9,5},... | collective-permute-start | bytes 1966088 | tf_op jit(solution)/shard_map/ppermute | solution.py:387
  944.4 32.3 %collective-permute-start.86 = (bf16[128,2560]{1,0:T(8,128)(2,1)S(1)}, bf16[128,2560]{1,0:T(8,128)(2,1)S(1)}, u32[]{:S(2)}, u32[]{:S(2)}) collective-permute-start(bf16[128,2560]{1,0:T(8,128)(2,1)S(1)} %add_convert_fusion.9), channel_id=1, source_target_pairs={{0,4},{4,8},{8,12},{12,14},{14,10},{10,6},{6,2},{2,0},{1,5},{5,9},... | collective-permute-start | bytes 1966088 | tf_op jit(solution)/shard_map/ppermute | solution.py:387
  944.6 32.3 %collective-permute-start.101 = (bf16[128,2560]{1,0:T(8,128)(2,1)S(1)}, bf16[128,2560]{1,0:T(8,128)(2,1)S(1)}, u32[]{:S(2)}, u32[]{:S(2)}) collective-permute-start(bf16[128,2560]{1,0:T(8,128)(2,1)S(1)} %add_convert_fusion.2), channel_id=1, source_target_pairs={{4,0},{8,4},{12,8},{14,12},{10,14},{6,10},{2,6},{0,2},{5,1},{9,5},... | collective-permute-start | bytes 1966088 | tf_op jit(solution)/shard_map/ppermute | solution.py:387
  977.2 24.9 %collective-permute-start.102 = (bf16[128,2560]{1,0:T(8,128)(2,1)S(1)}, bf16[128,2560]{1,0:T(8,128)(2,1)S(1)}, u32[]{:S(2)}, u32[]{:S(2)}) collective-permute-start(bf16[128,2560]{1,0:T(8,128)(2,1)S(1)} %add_convert_fusion.1), channel_id=1, source_target_pairs={{4,0},{8,4},{12,8},{14,12},{10,14},{6,10},{2,6},{0,2},{5,1},{9,5},... | collective-permute-start | bytes 1966088 | tf_op jit(solution)/shard_map/ppermute | solution.py:387
  985.6 27.1 %collective-permute-start.125 = (bf16[160,1024]{1,0:T(8,128)(2,1)S(1)}, bf16[160,1024]{1,0:T(8,128)(2,1)S(1)}, u32[]{:S(2)}, u32[]{:S(2)}) collective-permute-start(bf16[160,1024]{1,0:T(8,128)(2,1)S(1)} %collective-permute-done.124), channel_id=1, source_target_pairs={{0,4},{4,8},{8,12},{12,14},{14,10},{10,6},{6,2},{2,0},{1,5},{5,9},... | collective-permute-start | bytes 983048 | tf_op jit(solution)/shard_map/ppermute | solution.py:408
  1075.1 23.5 %collective-permute-start.107 = (bf16[128,2560]{1,0:T(8,128)(2,1)}, bf16[128,2560]{1,0:T(8,128)(2,1)}, u32[]{:S(2)}, u32[]{:S(2)}) collective-permute-start(bf16[128,2560]{1,0:T(8,128)(2,1)} %collective-permute-done.106), channel_id=1, source_target_pairs={{4,0},{8,4},{12,8},{14,12},{10,14},{6,10},{2,6},{0,2},{5,1},{9,5},... | collective-permute-start | bytes 1966088 | tf_op jit(solution)/shard_map/ppermute | solution.py:408
  1098.6 72.1 %collective-permute-start.93 = (bf16[128,2560]{1,0:T(8,128)(2,1)}, bf16[128,2560]{1,0:T(8,128)(2,1)}, u32[]{:S(2)}, u32[]{:S(2)}) collective-permute-start(bf16[128,2560]{1,0:T(8,128)(2,1)} %collective-permute-done.92), channel_id=1, source_target_pairs={{0,4},{4,8},{8,12},{12,14},{14,10},{10,6},{6,2},{2,0},{1,5},{5,9},... | collective-permute-start | bytes 1966088 | tf_op jit(solution)/shard_map/ppermute | solution.py:408
  1101.0 80.5 %collective-permute-start.108 = (bf16[128,2560]{1,0:T(8,128)(2,1)}, bf16[128,2560]{1,0:T(8,128)(2,1)}, u32[]{:S(2)}, u32[]{:S(2)}) collective-permute-start(bf16[128,2560]{1,0:T(8,128)(2,1)} %collective-permute-done.107), channel_id=1, source_target_pairs={{4,0},{8,4},{12,8},{14,12},{10,14},{6,10},{2,6},{0,2},{5,1},{9,5},... | collective-permute-start | bytes 1966088 | tf_op jit(solution)/shard_map/ppermute | solution.py:408
  1105.7 26.8 %collective-permute-start.16 = (f32[2304]{0:T(1024)S(1)}, f32[2304]{0:T(1024)S(1)}, u32[]{:S(2)}, u32[]{:S(2)}) collective-permute-start(f32[2304]{0:T(1024)S(1)} %pad_maximum_fusion.10), channel_id=1, source_target_pairs={{0,16},{16,0},{1,17},{17,1},{2,18},{18,2},{3,19},{19,3},{4,20},{20... | collective-permute-start | bytes 27656 | tf_op jit(solution)/shard_map/ppermute | solution.py:357
  1128.7 37.6 %collective-permute-start.36 = (bf16[128,1024]{1,0:T(8,128)(2,1)S(1)}, bf16[128,1024]{1,0:T(8,128)(2,1)S(1)}, u32[]{:S(2)}, u32[]{:S(2)}) collective-permute-start(bf16[128,1024]{1,0:T(8,128)(2,1)S(1)} %add_convert_fusion.47), channel_id=1, source_target_pairs={{0,4},{4,8},{8,12},{12,14},{14,10},{10,6},{6,2},{2,0},{1,5},{5,9},... | collective-permute-start | bytes 786440 | tf_op jit(solution)/shard_map/ppermute | solution.py:387
  1130.8 36.5 %collective-permute-start.51 = (bf16[128,1024]{1,0:T(8,128)(2,1)S(1)}, bf16[128,1024]{1,0:T(8,128)(2,1)S(1)}, u32[]{:S(2)}, u32[]{:S(2)}) collective-permute-start(bf16[128,1024]{1,0:T(8,128)(2,1)S(1)} %add_convert_fusion.40), channel_id=1, source_target_pairs={{4,0},{8,4},{12,8},{14,12},{10,14},{6,10},{2,6},{0,2},{5,1},{9,5},... | collective-permute-start | bytes 786440 | tf_op jit(solution)/shard_map/ppermute | solution.py:387
  1170.7 28.8 %collective-permute-start.94 = (bf16[128,2560]{1,0:T(8,128)(2,1)}, bf16[128,2560]{1,0:T(8,128)(2,1)S(1)}, u32[]{:S(2)}, u32[]{:S(2)}) collective-permute-start(bf16[128,2560]{1,0:T(8,128)(2,1)} %collective-permute-done.93), channel_id=1, source_target_pairs={{0,4},{4,8},{8,12},{12,14},{14,10},{10,6},{6,2},{2,0},{1,5},{5,9},... | collective-permute-start | bytes 1966088 | tf_op jit(solution)/shard_map/ppermute | solution.py:408
  1181.6 28.2 %collective-permute-start.109 = (bf16[128,2560]{1,0:T(8,128)(2,1)}, bf16[128,2560]{1,0:T(8,128)(2,1)S(1)}, u32[]{:S(2)}, u32[]{:S(2)}) collective-permute-start(bf16[128,2560]{1,0:T(8,128)(2,1)} %collective-permute-done.108), channel_id=1, source_target_pairs={{4,0},{8,4},{12,8},{14,12},{10,14},{6,10},{2,6},{0,2},{5,1},{9,5},... | collective-permute-start | bytes 1966088 | tf_op jit(solution)/shard_map/ppermute | solution.py:408
  (206 other events, 3315.5 us)
Sparse Core Ops, SparseCore 0:
  17.1 76.0 all-gather.2
  95.9 71.6 all-gather.4
  568.7 102.2 reduce-scatter.2
  675.5 141.4 reduce-scatter.4

commit v2 on v1

--- a/solution.py
+++ b/solution.py
@@ -1,6 +1,8 @@
 import jax
 import jax.numpy as jnp
 from jax import lax
+from jax.experimental import pallas as pl
+from jax.experimental.pallas import tpu as pltpu
 from jax.sharding import PartitionSpec as P
 
 DH = 64
@@ -369,47 +371,544 @@
     return lax.dot_general(left, right, (((0,), (0,)), ((), ())), preferred_element_type=F32)
 
 
-def ring_sum(forward_parts, backward_parts):
+BAND = 512
+
+
+TILE = 256
+PAIR = 2 * DH
+FAR_OFF = 1e30
+
+
+def lane_of(rows):
+    return lax.broadcasted_iota(jnp.int32, (rows, PAIR), 1)
+
+
+def head_lanes(lane, head):
+    own = lane < DH if head == 0 else lane >= DH
+    spare = lane - DH if head == 0 else lane
+    return (own, spare)
+
+
+def sequence_of(offsets, start):
+    position = start + lax.broadcasted_iota(jnp.int32, (TILE, PAIR), 0)
+    sequence = jnp.zeros((TILE, PAIR), jnp.int32)
+    for item in range(1, offsets.shape[0]):
+        sequence = sequence + (position >= offsets[item]).astype(jnp.int32)
+    return sequence
+
+
+def tile_rows(index):
+    return pl.ds(pl.multiple_of(index * TILE, TILE), TILE)
+
+
+def put_in_order(order_row, source, index):
+    position = index * TILE + lax.broadcasted_iota(jnp.int32, (TILE, source.shape[0]), 0)
+    hot = (order_row[...] == position).astype(F32).astype(BF16)
+    return dot_f32(hot, source[...])
+
+
+def put_back(order_col, source, index):
+    position = lax.broadcasted_iota(jnp.int32, (TILE, source.shape[0]), 1)
+    hot = (order_col[tile_rows(index), :] == position).astype(F32).astype(BF16)
+    return dot_f32(hot, source[...]).astype(BF16)
+
+
+def fill_strip(strip, table):
+    width = table.shape[1]
+    for head in range(2):
+        row = jnp.broadcast_to(table[pl.ds(head, 1), :], (TILE, width))
+        strip[head] = pltpu.roll(row, 1, 1, stride=1, stride_axis=0)
+
+
+def score_operands(query, key, sequence, head):
+    own, spare = head_lanes(lane_of(TILE), head)
+    differs = jnp.where((spare < 8) & (sequence != spare), 1.0, 0.0)
+    blocked = jnp.where(sequence == spare, -FAR_OFF, 0.0)
+    return (
+        jnp.where(own, query, differs).astype(BF16),
+        jnp.where(own, key, blocked).astype(BF16),
+    )
+
+
+def attend_kernel(
+    low, high, offsets, order_row, order_col, table, mixed,
+    ordered, context, exact, inverse, tops,
+    query_aug, key_aug, value_aug, strip, total, held,
+):
+    tiles = mixed.shape[0] // TILE
+    reach = strip.shape[2] // TILE // 2
+    lane = lane_of(TILE)
+    fill_strip(strip, table)
+    tops[...] = jnp.full(tops.shape, -FAR_OFF, F32)
+
+    @pl.loop(0, tiles)
+    def arrange(index):
+        rows = tile_rows(index)
+        block = put_in_order(order_row, mixed, index)
+        ordered[rows, :] = block.astype(BF16)
+        sequence = sequence_of(offsets, index * TILE)
+        for head in range(2):
+            own, spare = head_lanes(lane, head)
+            query, key = score_operands(
+                block[:, :PAIR], block[:, PAIR : 2 * PAIR], sequence, head
+            )
+            query_aug[head, rows, :] = query
+            key_aug[head, rows, :] = key
+            value_aug[head, rows, :] = jnp.where(
+                own, block[:, 2 * PAIR :], jnp.where(spare == 0, 1.0, 0.0)
+            ).astype(BF16)
+
+    @pl.loop(0, tiles)
+    def attend(index):
+        rows = tile_rows(index)
+        total[...] = jnp.zeros(total.shape, F32)
+
+        @pl.loop(low[index], high[index])
+        def keys(other):
+            columns = tile_rows(other)
+            place = tile_rows(other - index + reach)
+            for head in range(2):
+                raw = dot_nt(query_aug[head, rows, :], key_aug[head, columns, :])
+                tops[head] = jnp.maximum(
+                    tops[head], jnp.max(raw.reshape(TILE // 8, 8, TILE), axis=0)
+                )
+                weight = jnp.exp(raw + strip[head, :, place]).astype(BF16)
+                total[head] += dot_f32(weight, value_aug[head, columns, :])
+
+        parts = []
+        for head in range(2):
+            summed = total[head]
+            spot = DH if head == 0 else 0
+            row_total = summed[:, spot : spot + 1]
+            parts.append((summed / row_total, jnp.broadcast_to(1.0 / row_total, summed.shape)))
+        first = lane < DH
+        result = jnp.where(first, parts[0][0], parts[1][0])
+        exact[rows, :] = result
+        inverse[rows, :] = jnp.where(first, parts[0][1], parts[1][1])
+        held[rows, :] = result.astype(BF16)
+
+    @pl.loop(0, tiles)
+    def restore(index):
+        context[tile_rows(index), :] = put_back(order_col, held, index)
+
+
+def attend_back_kernel(
+    low, high, offsets, order_row, order_col, table, ordered, exact, inverse, incoming,
+    outgoing, slanted,
+    query_aug, key_aug, value_aug, grad_aug, grad_plain, key_turned,
+    strip, gathered, query_turned, key_sum, value_sum, held,
+):
+    rows_all = ordered.shape[0]
+    tiles = rows_all // TILE
+    reach = strip.shape[2] // TILE // 2
+    lane = lane_of(TILE)
+    fill_strip(strip, table)
+    gathered[...] = jnp.zeros(gathered.shape, F32)
+    key_sum[...] = jnp.zeros(key_sum.shape, F32)
+    value_sum[...] = jnp.zeros(value_sum.shape, F32)
+
+    @pl.loop(0, tiles)
+    def arrange(index):
+        rows = tile_rows(index)
+        block = ordered[rows, :].astype(F32)
+        sequence = sequence_of(offsets, index * TILE)
+        arrived = put_in_order(order_row, incoming, index)
+        scaled = arrived * inverse[rows, :]
+        grad_plain[rows, :] = scaled.astype(BF16)
+        product = scaled * exact[rows, :]
+        key_turned[:, rows] = block[:, PAIR : 2 * PAIR].T.astype(BF16)
+        for head in range(2):
+            own, spare = head_lanes(lane, head)
+            query, key = score_operands(
+                block[:, :PAIR], block[:, PAIR : 2 * PAIR], sequence, head
+            )
+            query_aug[head, rows, :] = query
+            key_aug[head, rows, :] = key
+            value_aug[head, rows, :] = jnp.where(
+                own, block[:, 2 * PAIR :], jnp.where(spare < 2, 1.0, 0.0)
+            ).astype(BF16)
+            shift = -jnp.sum(jnp.where(own, product, 0.0), axis=1, keepdims=True)
+            coarse = shift.astype(BF16).astype(F32)
+            fine = shift - coarse
+            extra = jnp.where(spare == 0, coarse, jnp.where(spare == 1, fine, 0.0))
+            grad_aug[head, rows, :] = jnp.where(own, scaled, extra).astype(BF16)
+
+    @pl.loop(0, tiles)
+    def attend(index):
+        rows = tile_rows(index)
+        query_turned[...] = jnp.zeros(query_turned.shape, F32)
+
+        @pl.loop(low[index], high[index])
+        def keys(other):
+            columns = tile_rows(other)
+            place = tile_rows(index - other + reach)
+            query_plain = ordered[rows, pl.ds(0, PAIR)]
+            key_parts, value_parts = ([], [])
+            for head in range(2):
+                raw = dot_nt(key_aug[head, columns, :], query_aug[head, rows, :])
+                weight = jnp.exp(raw + strip[head, :, place])
+                slope = dot_nt(value_aug[head, columns, :], grad_aug[head, rows, :])
+                score = weight * slope
+                gathered[head, :, place] += score
+                score = score.astype(BF16)
+                key_parts.append(dot_f32(score, query_plain))
+                value_parts.append(dot_f32(weight.astype(BF16), grad_plain[rows, :]))
+                query_turned[pl.ds(head * DH, DH), :] += dot_f32(
+                    key_turned[pl.ds(head * DH, DH), columns], score
+                )
+            first = lane < DH
+            key_sum[columns, :] += jnp.where(first, key_parts[0], key_parts[1])
+            value_sum[columns, :] += jnp.where(first, value_parts[0], value_parts[1])
+
+        held[rows, pl.ds(0, PAIR)] = query_turned[...].T.astype(BF16)
+
+    held[:, pl.ds(PAIR, PAIR)] = key_sum[...].astype(BF16)
+    held[:, pl.ds(2 * PAIR, PAIR)] = value_sum[...].astype(BF16)
+
+    @pl.loop(0, tiles)
+    def restore(index):
+        outgoing[tile_rows(index), :] = put_back(order_col, held, index)
+
+    width = gathered.shape[2]
+    for head in range(2):
+        folded = gathered[head]
+        size = TILE // 2
+        while size >= 8:
+            folded = folded[:size] + pltpu.roll(folded[size:], width - size, 1)
+            size //= 2
+        slanted[head] = folded
+
+
+def group_attention(low, high, offsets, order_row, order_col, table, mixed):
+    rows = mixed.shape[0]
+    smem = pl.BlockSpec(memory_space=pltpu.SMEM)
+    vmem = pl.BlockSpec(memory_space=pltpu.VMEM)
+    width = table.shape[1]
+    return pl.pallas_call(
+        attend_kernel,
+        out_shape=(
+            jax.ShapeDtypeStruct((rows, 3 * PAIR), BF16),
+            jax.ShapeDtypeStruct((rows, PAIR), BF16),
+            jax.ShapeDtypeStruct((rows, PAIR), F32),
+            jax.ShapeDtypeStruct((rows, PAIR), F32),
+            jax.ShapeDtypeStruct((2, 8, TILE), F32),
+        ),
+        in_specs=[smem] * 3 + [vmem] * 4,
+        out_specs=(vmem,) * 5,
+        scratch_shapes=[
+            pltpu.VMEM((2, rows, PAIR), BF16),
+            pltpu.VMEM((2, rows, PAIR), BF16),
+            pltpu.VMEM((2, rows, PAIR), BF16),
+            pltpu.VMEM((2, TILE, width), F32),
+            pltpu.VMEM((2, TILE, PAIR), F32),
+            pltpu.VMEM((rows, PAIR), BF16),
+        ],
+        name="attend",
+        compiler_params=pltpu.CompilerParams(vmem_limit_bytes=40 << 20),
+        cost_estimate=pl.CostEstimate(
+            flops=37_000_000_000, bytes_accessed=8_000_000, transcendentals=5_000_000
+        ),
+    )(low, high, offsets, order_row, order_col, table, mixed)
+
+
+def group_attention_back(
+    low, high, offsets, order_row, order_col, table, ordered, exact, inverse, incoming
+):
+    rows = ordered.shape[0]
+    smem = pl.BlockSpec(memory_space=pltpu.SMEM)
+    vmem = pl.BlockSpec(memory_space=pltpu.VMEM)
+    width = table.shape[1]
+    return pl.pallas_call(
+        attend_back_kernel,
+        out_shape=(
+            jax.ShapeDtypeStruct((rows, 3 * PAIR), BF16),
+            jax.ShapeDtypeStruct((2, 8, width), F32),
+        ),
+        in_specs=[smem] * 3 + [vmem] * 7,
+        out_specs=(vmem,) * 2,
+        scratch_shapes=[
+            pltpu.VMEM((2, rows, PAIR), BF16),
+            pltpu.VMEM((2, rows, PAIR), BF16),
+            pltpu.VMEM((2, rows, PAIR), BF16),
+            pltpu.VMEM((2, rows, PAIR), BF16),
+            pltpu.VMEM((rows, PAIR), BF16),
+            pltpu.VMEM((PAIR, rows), BF16),
+            pltpu.VMEM((2, TILE, width), F32),
+            pltpu.VMEM((2, TILE, width), F32),
+            pltpu.VMEM((PAIR, TILE), F32),
+            pltpu.VMEM((rows, PAIR), F32),
+            pltpu.VMEM((rows, PAIR), F32),
+            pltpu.VMEM((rows, 3 * PAIR), BF16),
+        ],
+        name="attend_back",
+        compiler_params=pltpu.CompilerParams(vmem_limit_bytes=50 << 20),
+        cost_estimate=pl.CostEstimate(
+            flops=45_000_000_000, bytes_accessed=12_000_000, transcendentals=5_000_000
+        ),
+    )(low, high, offsets, order_row, order_col, table, ordered, exact, inverse, incoming)
+
+
+def sequence_plan(lengths, rows):
+    offsets = jnp.cumsum(lengths) - lengths
+    ends = offsets + lengths
+    starts_at = jnp.arange(rows // TILE, dtype=jnp.int32) * TILE
+    seq_first = jnp.sum((starts_at[:, None] >= offsets[None, :]).astype(jnp.int32), axis=1) - 1
+    seq_last = (
+        jnp.sum((starts_at[:, None] + TILE - 1 >= offsets[None, :]).astype(jnp.int32), axis=1) - 1
+    )
+    picks = jnp.arange(lengths.shape[0], dtype=jnp.int32)[None, :]
+    low = jnp.sum(jnp.where(seq_first[:, None] == picks, offsets[None, :], 0), axis=1) // TILE
+    high = jnp.sum(jnp.where(seq_last[:, None] == picks, ends[None, :], 0), axis=1)
+    return (low, (high + TILE - 1) // TILE, offsets)
+
+
+def bias_tables(rel_buckets, bias_pair):
+    table_len = rel_buckets.shape[0]
+    reach = (table_len + 1) // 2 // TILE
+    width = (2 * reach + 1) * TILE
+    hot = (rel_buckets[None, :] == jnp.arange(NB, dtype=jnp.int32)[:, None]).astype(BF16)
+    table = dot_tn(bias_pair, hot)
+    pad = ((0, 0), (0, width - table_len))
+    return (jnp.pad(table, pad), jnp.pad(table[:, ::-1], pad))
+
+
+def bucket_sums(rel_buckets, slanted):
+    table_len = rel_buckets.shape[0]
+    width = slanted.shape[2]
+    total = jnp.zeros((2, table_len), F32)
+    for row in range(8):
+        total = total + slanted[:, row, row + 1 : row + 1 + table_len]
+    hot = (rel_buckets[::-1][:, None] == jnp.arange(NB, dtype=jnp.int32)[None, :]).astype(F32)
+    return jnp.dot(total, hot, precision=lax.Precision.HIGHEST, preferred_element_type=F32)
+
+
+def blank_arrays(shapes):
+    def leave(*refs):
+        pass
+
+    return pl.pallas_call(
+        leave,
+        out_shape=tuple(jax.ShapeDtypeStruct(shape, F32) for shape in shapes),
+        out_specs=tuple(pl.BlockSpec(memory_space=pl.ANY) for shape in shapes),
+        name="blank",
+    )()
+
+
+def fold_kernel(chunk, *refs):
+    *sources, sent = refs
+    got = sources.pop(0) if len(sources) == 4 else None
+    start = 0
+    for source in sources:
+        rows = source.shape[0]
+        for band in range(source.shape[1] // BAND):
+            value = source[:, band * BAND : (band + 1) * BAND]
+            place = pl.ds(start, rows)
+            if got is not None:
+                value = (value.astype(F32) + got[place, :].astype(F32)).astype(BF16)
+            sent[place, :] = value
+            start += rows
+
+
+def spread_kernel(chunk, message, *refs):
+    start = 0
+    for result in refs[-3:]:
+        rows = result.shape[0]
+        for band in range(result.shape[1] // BAND):
+            result[:, band * BAND : (band + 1) * BAND] = message[pl.ds(start, rows), :].astype(F32)
+            start += rows
+
+
+def whole_spec(shape):
+    return pl.BlockSpec(shape, lambda step, chunk: (0,) * len(shape))
+
+
+def row_spec(rows, width, first):
+    return pl.BlockSpec((rows, width), lambda step, chunk: (chunk[0] + first, 0))
+
+
+def fold_chunk(chunk, parts, got):
+    rows = sum(count * array_in.shape[1] // BAND for array_in, count, first, item in parts)
+    return pl.pallas_call(
+        fold_kernel,
+        grid_spec=pltpu.PrefetchScalarGridSpec(
+            num_scalar_prefetch=1,
+            grid=(1,),
+            in_specs=[whole_spec((rows, BAND))] * len(got)
+            + [row_spec(count, array_in.shape[1], first) for array_in, count, first, item in parts],
+            out_specs=whole_spec((rows, BAND)),
+        ),
+        out_shape=jax.ShapeDtypeStruct((rows, BAND), BF16),
+        name="fold",
+        cost_estimate=pl.CostEstimate(flops=0, bytes_accessed=6 * rows * BAND, transcendentals=0),
+    )(chunk.reshape(1), *got, *[array_in for array_in, count, first, item in parts])
+
+
+def spread_chunk(chunk, message, parts, results):
+    rows = message.shape[0]
+    kept = [pl.BlockSpec(memory_space=pl.ANY)] * len(results)
+    return pl.pallas_call(
+        spread_kernel,
+        grid_spec=pltpu.PrefetchScalarGridSpec(
+            num_scalar_prefetch=1,
+            grid=(1,),
+            in_specs=[whole_spec((rows, BAND))] + kept,
+            out_specs=tuple(
+                row_spec(count, array_in.shape[1], first) for array_in, count, first, item in parts
+            ),
+        ),
+        out_shape=tuple(jax.ShapeDtypeStruct(array_in.shape, F32) for array_in, count, first, item in parts),
+        input_output_aliases={2 + item: item for item in range(len(results))},
+        name="spread",
+        cost_estimate=pl.CostEstimate(flops=0, bytes_accessed=6 * rows * BAND, transcendentals=0),
+    )(chunk.reshape(1), message, *results)
+
+
+def heads_kernel(chunk, message, *refs):
+    for item, result in enumerate(refs[-3:]):
+        result[...] = message[:, item * PAIR : (item + 1) * PAIR].astype(F32)
+
+
+def spread_heads(chip, message, results):
+    rows, parts = message.shape[0], len(RING)
+    shape = jax.ShapeDtypeStruct((rows, parts * PAIR), F32)
+    spec = pl.BlockSpec((rows, PAIR), lambda step, chunk: (0, chunk[0]))
+    return pl.pallas_call(
+        heads_kernel,
+        grid_spec=pltpu.PrefetchScalarGridSpec(
+            num_scalar_prefetch=1,
+            grid=(1,),
+            in_specs=[whole_spec(message.shape)]
+            + [pl.BlockSpec(memory_space=pl.ANY)] * len(results),
+            out_specs=(spec,) * 3,
+        ),
+        out_shape=(shape,) * 3,
+        input_output_aliases={2 + item: item for item in range(len(results))},
+        name="spread_heads",
+        cost_estimate=pl.CostEstimate(flops=0, bytes_accessed=6 * message.size, transcendentals=0),
+    )(chip.reshape(1), message, *results)
+
+
+def tie(*values):
+    return lax.optimization_barrier(values)
+
+
+def ring_pairs(way):
     count = len(RING)
-    up_pairs = [(RING[i], RING[(i + 1) % count]) for i in range(count)]
-    down_pairs = [(after, before) for before, after in up_pairs]
-    me = look_up([RING.index(c) for c in range(count)], lax.axis_index("ctx"))
-    flows = [(array_in, 1, up_pairs) for array_in in forward_parts]
-    flows += [(array_in, -1, down_pairs) for array_in in backward_parts]
-
-    def piece(array_in, chunk):
-        rows = array_in.shape[0] // count
-        return lax.dynamic_slice_in_dim(array_in, jnp.mod(chunk, count) * rows, rows)
-
-    current = [piece(array_in, me) for array_in, way, pairs in flows]
-    for step in range(count - 1):
-        arrived = [
-            lax.ppermute(held, "ctx", pairs) for held, (array_in, way, pairs) in zip(current, flows)
+    return [(RING[i], RING[(i + way) % count]) for i in range(count)]
+
+
+def ring_place():
+    return look_up([RING.index(c) for c in range(len(RING))], lax.axis_index("ctx"))
+
+
+def ring_chip(place):
+    return look_up(RING, jnp.mod(place, len(RING)))
+
+
+def tiny_gather(values):
+    sent = jnp.broadcast_to(values[None], (len(RING),) + values.shape)
+    return lax.all_to_all(sent, "ctx", 0, 0, tiled=True)
+
+
+class RingSum:
+    def __init__(self, ahead, back, results):
+        self.flows = [(ahead, 1), (back, -1)]
+        self.me = ring_place()
+        self.step = 0
+        self.results = list(results)
+        self.arrived = None
+        self.ready = [fold_chunk(self.me, parts, []) for parts, way in self.flows]
+
+    @property
+    def done(self):
+        return self.step == 2 * (len(RING) - 1)
+
+    def send(self):
+        if self.done:
+            return
+        self.arrived = [
+            lax.ppermute(held, "ctx", ring_pairs(way))
+            for held, (parts, way) in zip(self.ready, self.flows)
         ]
-        current = [
-            (got.astype(F32) + piece(array_in, me - way * (step + 1)).astype(F32)).astype(BF16)
-            for got, (array_in, way, pairs) in zip(arrived, flows)
-        ]
-    results = [jnp.zeros(array_in.shape, F32) for array_in, way, pairs in flows]
-
-    def place(result, chunk, held):
-        rows = held.shape[0]
-        return lax.dynamic_update_slice_in_dim(
-            result, held.astype(F32), jnp.mod(chunk, count) * rows, 0
-        )
-
-    for step in range(count):
-        results = [
-            place(result, me - way * (count - 1 + step), held)
-            for result, held, (array_in, way, pairs) in zip(results, current, flows)
-        ]
-        if step < count - 1:
-            current = [
-                lax.ppermute(held, "ctx", pairs)
-                for held, (array_in, way, pairs) in zip(current, flows)
-            ]
-    forward_count = len(forward_parts)
-    return (results[:forward_count], results[forward_count:])
+
+    def absorb(self):
+        if self.done:
+            return
+        self.step += 1
+        for index, (parts, way) in enumerate(self.flows):
+            chunk = jnp.mod(self.me - way * self.step, len(RING))
+            got = self.arrived[index]
+            self.ready[index] = (
+                fold_chunk(chunk, parts, [got]) if self.step < len(RING) else got
+            )
+
+    def place(self):
+        if self.step < len(RING) - 1:
+            return
+        for index, (parts, way) in enumerate(self.flows):
+            chunk = jnp.mod(self.me - way * self.step, len(RING))
+            ids = [part[3] for part in parts]
+            written = spread_chunk(
+                chunk, self.ready[index], parts, [self.results[item] for item in ids]
+            )
+            for item, result in zip(ids, written):
+                self.results[item] = result
+
+
+class RingGather:
+    def __init__(self, block):
+        self.me = ring_place()
+        self.step = 0
+        self.ready = (block, block)
+        self.arrived = None
+        self.results = ()
+        self.found = [(lax.axis_index("ctx"), block)]
+
+    def send(self):
+        if self.step == len(RING) // 2:
+            return
+        self.step += 1
+        ahead, back = self.ready
+        ahead = lax.ppermute(ahead, "ctx", ring_pairs(1))
+        if self.step < len(RING) // 2:
+            back = lax.ppermute(back, "ctx", ring_pairs(-1))
+        self.arrived = (ahead, back)
+
+    def absorb(self):
+        if len(self.found) == len(RING):
+            return
+        self.ready = self.arrived
+        self.found.append((ring_chip(self.me - self.step), self.arrived[0]))
+        if self.step < len(RING) // 2:
+            self.found.append((ring_chip(self.me + self.step), self.arrived[1]))
+
+    def place(self):
+        pass
+
+
+class HeadRing(RingGather):
+    def __init__(self, block, results):
+        super().__init__(block)
+        self.results = results
+        self.placed = 0
+
+    def place(self):
+        for chip, block in self.found[self.placed :]:
+            self.results = spread_heads(chip, block, self.results)
+        self.placed = len(self.found)
+
+
+def stage(values, *rings):
+    values, arrived = tie(values, [(ring.arrived, ring.results) for ring in rings])
+    for ring, blocks in zip(rings, arrived):
+        ring.arrived, ring.results = blocks
+        ring.absorb()
+    values, ready = tie(values, [ring.ready for ring in rings])
+    for ring, blocks in zip(rings, ready):
+        ring.ready = blocks
+        ring.send()
+        ring.place()
+    return values
 
 
 def per_device_ring(
@@ -474,59 +973,39 @@
     queries = (dot_f32(normed_own, w_query) + dot_f32(normed_far, wq_far)).astype(BF16)
     keys_here = (dot_f32(normed_own, w_key) + dot_f32(normed_far, wk_far)).astype(BF16)
     values_here = (dot_f32(normed_own, w_value) + dot_f32(normed_far, wv_far)).astype(BF16)
-    key_block = min(512, group_rows)
-    block_count = group_rows // key_block
-    ranges = bucket_ranges(rel_buckets)
-    order_row = token_order[0]
-    seq_ids = segment_of(order_row, seq_lengths[0])
-    row_start = lax.axis_index("ctx") * local_rows
-    query_pos = lax.dynamic_slice_in_dim(order_row, row_start, local_rows)
-    query_seg = lax.dynamic_slice_in_dim(seq_ids, row_start, local_rows)
-    pos_blocks = order_row.reshape(block_count, key_block)
-    seg_blocks = seq_ids.reshape(block_count, key_block)
-    query_heads = queries.reshape(local_rows, head_count, DH)
-    key_all, value_all = (
-        lax.all_gather(keys_here, "ctx", axis=0, tiled=True),
-        lax.all_gather(values_here, "ctx", axis=0, tiled=True),
-    )
-
-    def blocked(array_in):
-        return array_in.reshape(block_count, key_block, head_count, DH)
-
-    def forward_block(running, inputs):
-        summed, totals, head_top = running
-        key_blk, value_blk, pos_blk, seg_blk = inputs
-        raw_scores = jnp.einsum(
-            "thd,khd->htk", query_heads, key_blk, preferred_element_type=jnp.float32
-        )
-        bucket_hot, pair_bias, same_seq = pair_terms(
-            query_pos, query_seg, pos_blk, seg_blk, ranges, bias_local
-        )
-        weights = jnp.where(same_seq, jnp.exp(raw_scores + pair_bias), 0.0)
-        totals = totals + jnp.sum(weights, axis=2)
-        summed = summed + jnp.einsum(
-            "htk,khd->thd",
-            weights.astype(jnp.bfloat16),
-            value_blk,
-            preferred_element_type=jnp.float32,
-        )
-        head_top = jnp.maximum(
-            head_top, jnp.max(jnp.where(same_seq, raw_scores, -1e30), axis=(1, 2))
-        )
-        return ((summed, totals, head_top), None)
-
-    start_state = (
-        jnp.zeros((local_rows, head_count, DH), jnp.float32),
-        jnp.zeros((head_count, local_rows), jnp.float32),
-        jnp.full((head_count,), -1e30, jnp.float32),
-    )
-    (summed, totals, head_top), unused = lax.scan(
-        forward_block, start_state, (blocked(key_all), blocked(value_all), pos_blocks, seg_blocks)
-    )
-    row_totals = jnp.transpose(totals)[:, :, None]
-    context_exact = summed / row_totals
-    context = context_exact.reshape(local_rows, head_count * DH).astype(jnp.bfloat16)
-    head_maxima = lax.pmax(head_top, ("fsdp", "ctx"))
+    parts = lax.axis_size("ctx")
+
+    def by_heads(items):
+        mixed = jnp.concatenate([item.reshape(local_rows, parts, 1, PAIR) for item in items], axis=2)
+        mixed = jnp.transpose(mixed.reshape(local_rows, parts, len(items) * PAIR), (1, 0, 2))
+        moved = lax.all_to_all(mixed, "ctx", 0, 0, tiled=True)
+        return moved.reshape(group_rows, len(items) * PAIR)
+
+    def by_rows(array_in):
+        count = array_in.shape[1] // PAIR
+        moved = lax.all_to_all(
+            array_in.reshape(parts, local_rows, count * PAIR), "ctx", 0, 0, tiled=True
+        )
+        moved = jnp.transpose(moved.reshape(parts, local_rows, count, PAIR), (2, 1, 0, 3))
+        return moved.reshape(count, local_rows, parts * PAIR)
+
+    order_row = token_order
+    order_col = token_order.reshape(group_rows, 1)
+    low, high, offsets = sequence_plan(seq_lengths[0], group_rows)
+    bias_pair = lax.dynamic_slice_in_dim(bias_local, ctx * 2, 2, axis=1)
+    table, table_back = bias_tables(rel_buckets, bias_pair)
+    mixed = by_heads([queries, keys_here, values_here])
+    mixed, normed_block = tie(mixed, jnp.concatenate([normed_own, normed_far], axis=1))
+    normed_ring = RingGather(normed_block)
+    normed_ring.send()
+    ordered, context_heads, exact, inverse, tops = group_attention(
+        low, high, offsets, order_row, order_col, table, mixed
+    )
+    context_heads, normed_ring.arrived = tie(context_heads, normed_ring.arrived)
+    normed_ring.absorb()
+    context = by_rows(context_heads)[0]
+    context, normed_ring.ready = tie(context, normed_ring.ready)
+    normed_ring.send()
 
     def tp_sum(own, far):
         own, far = (own.astype(BF16), far.astype(BF16))
@@ -536,6 +1015,7 @@
         )
 
     attn_own, attn_far = tp_sum(dot_f32(context, w_out), dot_f32(context, wo_far))
+    attn_own, attn_far = stage((attn_own, attn_far), normed_ring)
     hid_own, hid_far = (tok_own + attn_own, tok_far + attn_far)
     inner_grad = dot_nt(cot_own, w_down) + dot_nt(cot_far, wd_far)
     scale_f = norm_scale(hid_own, hid_far)
@@ -548,12 +1028,11 @@
     gate_grad, up_grad = geglu_back(inner_grad)
     gate_grad = gate_grad.astype(BF16)
     up_grad = up_grad.astype(BF16)
+    gate_grad, up_grad, inner_act = stage((gate_grad, up_grad, inner_act), normed_ring)
     dnf_own, dnf_far = tp_sum(
         dot_nt(gate_grad, w_gate) + dot_nt(up_grad, w_up),
         dot_nt(gate_grad, wg_far) + dot_nt(up_grad, wu_far),
     )
-    ffn_own, ffn_far = tp_sum(dot_f32(inner_act, w_down), dot_f32(inner_act, wd_far))
-    output = whole(hid_own + ffn_own, hid_far + ffn_far).astype(BF16)
 
     def pair_rows(own):
         return jnp.concatenate([own, swap(own, "fsdp")])
@@ -565,8 +1044,6 @@
     grad_gate = dot_tn(nffn_pair, pair_rows(gate_grad)).astype(BF16)
     grad_up = dot_tn(nffn_pair, pair_rows(up_grad)).astype(BF16)
     grad_down = dot_tn(pair_rows(inner_act), pair_half(cot_own, cot_far)).astype(BF16)
-    down_rows = grad_down.shape[0] // 2
-
     def norm_back(own, far, scale, gain_own, gain_far, dy_own, dy_far):
         mean_term = (
             jnp.sum(gain_own * dy_own * own, axis=1, keepdims=True)
@@ -588,100 +1065,112 @@
     ag_own, ag_far = (hgrad_own.astype(BF16), hgrad_far.astype(BF16))
     grad_out = dot_tn(pair_rows(context), pair_half(ag_own, ag_far)).astype(BF16)
     context_grad = dot_nt(ag_own, w_out) + dot_nt(ag_far, wo_far)
-    context_grad = context_grad.reshape(local_rows, head_count, DH)
-    summed_grad = (context_grad / row_totals).astype(jnp.bfloat16)
-    total_grad = jnp.transpose(-jnp.sum(context_grad * context_exact, axis=2) / row_totals[:, :, 0])
-    key_back, value_back = (key_all, value_all)
-
-    def backward_block(running, inputs):
-        query_acc, bias_acc = running
-        key_blk, value_blk, pos_blk, seg_blk = inputs
-        raw_scores = jnp.einsum(
-            "thd,khd->htk", query_heads, key_blk, preferred_element_type=jnp.float32
-        )
-        bucket_hot, pair_bias, same_seq = pair_terms(
-            query_pos, query_seg, pos_blk, seg_blk, ranges, bias_local
-        )
-        weights = jnp.where(same_seq, jnp.exp(raw_scores + pair_bias), 0.0)
-        prob_grad = (
-            jnp.einsum("thd,khd->htk", summed_grad, value_blk, preferred_element_type=jnp.float32)
-            + total_grad[:, :, None]
-        )
-        score_grad = (weights * prob_grad).astype(jnp.bfloat16)
-        query_acc = query_acc + jnp.einsum(
-            "htk,khd->thd", score_grad, key_blk, preferred_element_type=jnp.float32
-        )
-        key_grad = jnp.einsum(
-            "htk,thd->khd", score_grad, query_heads, preferred_element_type=jnp.float32
-        )
-        value_grad = jnp.einsum(
-            "htk,thd->khd",
-            weights.astype(jnp.bfloat16),
-            summed_grad,
-            preferred_element_type=jnp.float32,
-        )
-        bucket_sums = jnp.einsum(
-            "htk,btk->hb", score_grad, bucket_hot, preferred_element_type=jnp.float32
-        )
-        return ((query_acc, bias_acc + bucket_sums), (key_grad, value_grad))
-
-    zero_state = (
-        jnp.zeros((local_rows, head_count, DH), jnp.float32),
-        jnp.zeros((head_count, NB), jnp.float32),
-    )
-    (query_acc, bias_acc), (key_grads, value_grads) = lax.scan(
-        backward_block, zero_state, (blocked(key_back), blocked(value_back), pos_blocks, seg_blocks)
-    )
-    key_grad_all, value_grad_all = (
-        lax.psum_scatter(
-            key_grads.reshape(group_rows, head_count * DH).astype(jnp.bfloat16),
-            "ctx",
-            scatter_dimension=0,
-            tiled=True,
-        ).astype(jnp.float32),
-        lax.psum_scatter(
-            value_grads.reshape(group_rows, head_count * DH).astype(jnp.bfloat16),
-            "ctx",
-            scatter_dimension=0,
-            tiled=True,
-        ).astype(jnp.float32),
-    )
-    query_grad = query_acc.reshape(local_rows, head_count * DH).astype(jnp.bfloat16)
-    key_grad = key_grad_all.astype(jnp.bfloat16)
-    value_grad = value_grad_all.astype(jnp.bfloat16)
-    grad_bias = jnp.transpose(bias_acc)
-    (final_gate, down_low), (final_up, down_high) = ring_sum(
-        [grad_gate, grad_down[:down_rows]], [grad_up, grad_down[down_rows:]]
-    )
-    final_down = jnp.concatenate([down_low, down_high])
-    dn_own, dn_far = tp_sum(
+    grad_rows = grad_gate.shape[0] // len(RING)
+    down_rows = grad_down.shape[0] // (2 * len(RING))
+    out_rows = w_out.shape[0] // (2 * len(RING))
+    blanks = blank_arrays(
+        [grad_gate.shape, grad_up.shape, grad_down.shape, grad_out.shape] + [w_query.shape] * 3
+    )
+    context_grad, grad_out = stage((context_grad.astype(BF16), grad_out), normed_ring)
+    ring = RingSum(
+        [
+            (grad_gate, grad_rows, 0, 0),
+            (grad_down, down_rows, 0, 2),
+            (grad_out, out_rows, 0, 3),
+        ],
+        [
+            (grad_up, grad_rows, 0, 1),
+            (grad_down, down_rows, len(RING), 2),
+            (grad_out, out_rows, len(RING), 3),
+        ],
+        blanks[:4],
+    )
+    ring.send()
+    grad_mixed = by_heads([context_grad])
+    grad_mixed = stage(grad_mixed, ring)
+    outgoing, slanted = group_attention_back(
+        low, high, offsets, order_row, order_col, table_back, ordered, exact, inverse, grad_mixed
+    )
+    outgoing, found, tops, inner_act = stage(
+        (outgoing, [blocks for chip, blocks in normed_ring.found], tops, inner_act),
+        ring,
+    )
+    query_grad, key_grad, value_grad = by_rows(outgoing)
+    outgoing_turned = jnp.concatenate(
+        [
+            lax.dynamic_slice_in_dim(outgoing, chip * local_rows, local_rows)
+            for chip, blocks in normed_ring.found
+        ]
+    )
+    head_grads = dot_tn(jnp.concatenate(found), outgoing_turned)
+    head_grads, head_grads_sent = (head_grads[:half], head_grads[half:].astype(BF16))
+    head_grads = (head_grads + swap(head_grads_sent, "fsdp").astype(F32)).astype(BF16)
+    dn_parts = (
         dot_nt(query_grad, w_query) + dot_nt(key_grad, w_key) + dot_nt(value_grad, w_value),
         dot_nt(query_grad, wq_far) + dot_nt(key_grad, wk_far) + dot_nt(value_grad, wv_far),
     )
+    dn_parts = (dn_parts[0].astype(BF16), dn_parts[1].astype(BF16))
+    head_grads, dn_parts = stage((head_grads, dn_parts), ring)
+    head_ring = HeadRing(head_grads, blanks[4:])
+    head_ring.send()
+    head_ring.place()
+    dn_own, dn_far = tp_sum(*dn_parts)
+    dn_own, dn_far = stage((dn_own, dn_far), ring, head_ring)
     tback_own, tback_far, dga_own, dga_far = norm_back(
         tok_own, tok_far, scale_a, ga_own, ga_far, dn_own, dn_far
     )
     grad_tokens = whole(hgrad_own + tback_own, hgrad_far + tback_far)
-    normed_pair = pair_half(normed_own, normed_far)
-    grad_query = dot_tn(normed_pair, pair_rows(query_grad)).astype(BF16)
-    grad_key = dot_tn(normed_pair, pair_rows(key_grad)).astype(BF16)
-    grad_value = dot_tn(normed_pair, pair_rows(value_grad)).astype(BF16)
-    (final_query, final_key), (final_value, final_out) = ring_sum(
-        [grad_query, grad_key], [grad_value, grad_out]
-    )
-    bias_rows = rel_bias.shape[0]
+    ffn_own, ffn_far = tp_sum(dot_f32(inner_act, w_down), dot_f32(inner_act, wd_far))
+    output = whole(hid_own + ffn_own, hid_far + ffn_far).astype(BF16)
+    grad_tokens, output, dga_own, dga_far, tops = stage(
+        (grad_tokens, output, dga_own, dga_far, tops), ring, head_ring
+    )
+    pair_top = jnp.max(tops, axis=(1, 2))
+    pair_top = jnp.maximum(pair_top, swap(pair_top, "fsdp"))
+    here = jnp.arange(parts, dtype=jnp.int32)[:, None] == ctx
+    head_maxima = tiny_gather(pair_top).reshape(head_count)
+    pair_bias = bucket_sums(rel_buckets, slanted)
+    grad_bias = jnp.transpose(
+        jnp.where(here[:, :, None], pair_bias[None], 0.0).reshape(head_count, NB)
+    )
     small_own = jnp.concatenate([dga_own, dgf_own])
     small_sent = jnp.concatenate([dga_far, dgf_far])
     bias_flat = grad_bias.reshape(2, -1)
     small_own = jnp.concatenate([small_own, jnp.where(first, bias_flat[0], bias_flat[1])])
     small_sent = jnp.concatenate([small_sent, jnp.where(first, bias_flat[1], bias_flat[0])])
-    small_sum = lax.psum(small_own + swap(small_sent, "fsdp"), "ctx")
+    small_sum = jnp.sum(tiny_gather(small_own + swap(small_sent, "fsdp")), axis=0)
     final_gain_a, final_gain_f = (small_sum[:half], small_sum[half : 2 * half])
     final_bias = small_sum[2 * half :].reshape(rel_bias.shape)
     clip_scale = TAU_CLIP / jnp.maximum(head_maxima, TAU_CLIP)
     column_scale = jnp.repeat(jnp.sqrt(clip_scale), DH)
     query_clipped = (w_query.astype(F32) * column_scale[None, :]).astype(BF16)
     key_clipped = (w_key.astype(F32) * column_scale[None, :]).astype(BF16)
+    others = (
+        grad_tokens,
+        output,
+        final_gain_a,
+        final_gain_f,
+        final_bias,
+        head_maxima,
+        query_clipped,
+        key_clipped,
+    )
+    while not ring.done:
+        stage((), ring, head_ring)
+        if ring.step == len(RING) + 1:
+            others, ring.arrived = tie(others, ring.arrived)
+    final_gate, final_up, final_down, final_out = ring.results
+    final_query, final_key, final_value = head_ring.results
+    (
+        grad_tokens,
+        output,
+        final_gain_a,
+        final_gain_f,
+        final_bias,
+        head_maxima,
+        query_clipped,
+        key_clipped,
+    ) = others
     return (
         output,
         grad_tokens,

time: 1270 us -> 782 us (0.62)
  matrix products: 305 us -> 102 us
  Pallas kernels: 0 us -> 168 us
  waiting for transfers between devices: 502 us -> 335 us
  local copies, waits for them, and re-layouts: 143 us -> 40.9 us
  blocking collectives: 68.8 us -> 0 us
  other arithmetic: 102 us -> 39 us
  starting transfers between devices: 127 us -> 86.7 us
  between operations: 16.9 us -> 2.37 us
    dot_general x40 -> x1, matrix products: 197 us -> 0.58 us  [bucket_sums(): jnp.dot(total, hot, precision=lax.Precision.HIGHEST, preferred_element_ty...]
    pallas_call x0 -> x43, Pallas kernels: none -> 168 us  [the longest x16 44.8 us: fold_chunk(): pl.pallas_call(fold_kernel, grid_spec=pltpu.PrefetchScalarGridSpec(num_sc...]
    ppermute x112 -> x42, waiting for transfers between devices: 351 us -> 213 us  [the longest x28 116 us: send(): lax.ppermute(held, 'ctx', ring_pairs(way))]
    all_gather x2 -> x0, waiting for transfers between devices: 108 us -> none  [the longest x1 54.9 us: per_device_ring(): lax.all_gather(values_here, 'ctx', axis=0, tiled=True)]
    all_to_all x0 -> x6, waiting for transfers between devices: none -> 87.1 us  [the longest x2 60.1 us: by_heads(): moved = lax.all_to_all(mixed, 'ctx', 0, 0, tiled=True)]
    ppermute x112 -> x42, starting transfers between devices: 112 us -> 44 us  [the longest x28 29 us: send(): lax.ppermute(held, 'ctx', ring_pairs(way))]
    dynamic_update_slice x64 -> x0, other arithmetic: 46.2 us -> none  [place(): lax.dynamic_update_slice_in_dim(result, held.astype(F32), jnp.mod(chunk,...]
    dot_general x4 -> x0, local copies, waits for them, and re-layouts: 39.6 us -> none  [pair_terms(): jnp.einsum('btk,bh->htk', bucket_hot, bias_table, preferred_element_type=...]
  transfers between devices with their start and end apart: 144 -> 74, of which waited for: 71 -> 37; matrix products, arithmetic and copies ran while one was open for 29% -> 18% of each run, Pallas kernels for 0% -> 16%
where the time goes in v2:
time: 782 us; the launch traced here: 774 us
  waiting for transfers between devices  335 us (43%)
  Pallas kernels  168 us (21%)
  matrix products  102 us (13%)
  starting transfers between devices  86.7 us (11%)
  local copies, waits for them, and re-layouts  40.9 us (5%)
  other arithmetic  39 us (5%)
    ppermute x28, waiting for transfers between devices, send(): lax.ppermute(held, 'ctx', ring_pairs(way))  116 us
    ppermute x8, waiting for transfers between devices, send(): ahead = lax.ppermute(ahead, 'ctx', ring_pairs(1))  74.2 us
    all_to_all x2, waiting for transfers between devices, by_heads(): moved = lax.all_to_all(mixed, 'ctx', 0, 0, tiled=True)  60.1 us
    pallas_call x16, Pallas kernels, fold_chunk(): pl.pallas_call(fold_kernel, grid_spec=pltpu.PrefetchScalarGridSpec(num_sc...  44.8 us
    pallas_call x16, Pallas kernels, spread_chunk(): pl.pallas_call(spread_kernel, grid_spec=pltpu.PrefetchScalarGridSpec(num_...  42.8 us
    dot_general x14, matrix products, dot_nt(): lax.dot_general(left, right, (((1,), (1,)), ((), ())), preferred_element_...  39.8 us
    dot_general x14, matrix products, dot_f32(): return jnp.dot(left, right, preferred_element_type=F32)  37.3 us
    ppermute x26, waiting for transfers between devices, swap(): return lax.ppermute(array_in, axis_name, [(0, 1), (1, 0)])  34.9 us
  transfers between devices with their start and end apart: 74, of which 37 were waited for; matrix products, arithmetic and copies ran while one was open for 18% of the time, Pallas kernels for 16%

profile of v2, /device:TPU:0, one launch (start us, length us, event | category | flops | bytes accessed | tf_op | source)
XLA Modules:
  0.0 774.2 jit_solution(14897529506229714710)
XLA Ops:
  19.0 7.3 all-to-all-start
  30.3 33.3 %all-to-all-done = bf16[8,256,384]{2,1,0:T(8,128)(2,1)S(1)} async-done(((bf16[8,256,384]{2,1,0:T(8,128)(2,1)}), bf16[8,256,384]{2,1,0:T(8,128)(2,1)S(1)}, u32[]{:S(2)}, u32[]{:S(2)}) %all-to-all-start) | async-done | bytes 1572896 | tf_op jit(solution)/shard_map/all_to_all | solution.py:981
  65.6 27.7 %attend.1 = (bf16[2048,384]{1,0:T(8,128)(2,1)S(1)}, bf16[2048,128]{1,0:T(8,128)(2,1)S(1)}, f32[2048,128]{1,0:T(8,128)S(1)}, f32[2048,128]{1,0:T(8,128)S(1)}, f32[2,8,256]{2,1,0:T(8,128)S(1)}) custom-call(s32[8]{0:T(128)S(1)} %and_select_fusion.1.low, s32[8]{0:T(128)S(1)} %and_select_fusion.high, s32[3]{0:T(128)S(1)} %bitcast_subtract_fusion.offsets, ...), custom_call_target="tpu_custom_call" | custom-call | flops 36999999488 | bytes 8000000 | tf_op jit(solution)/shard_map/attend/pallas_call | solution.py:587
  97.5 4.3 all-to-all-start.1
  104.1 11.4 %all-to-all-done.1 = bf16[8,256,128]{1,2,0:T(8,128)(2,1)} async-done(((bf16[8,256,128]{1,2,0:T(8,128)(2,1)}), bf16[8,256,128]{1,2,0:T(8,128)(2,1)}, u32[]{:S(2)}, u32[]{:S(2)}) %all-to-all-start.1) | async-done | bytes 524320 | tf_op jit(solution)/shard_map/all_to_all | solution.py:986
  118.9 4.1 fusion.89
  127.1 5.2 collective-permute-done.6
  133.7 4.1 convolution_add_fusion.2
  141.0 8.9 %collective-permute-done.9 = bf16[256,2048]{1,0:T(8,128)(2,1)S(1)} collective-permute-done((bf16[256,2048]{1,0:T(8,128)(2,1)}, bf16[256,2048]{1,0:T(8,128)(2,1)S(1)}, u32[]{:S(2)}, u32[]{:S(2)}) %collective-permute-start.9) | collective-permute-done | bytes 1048608 | tf_op jit(solution)/shard_map/ppermute | solution.py:872
  149.8 5.6 collective-permute-done.10
  162.7 4.0 convolution_add_fusion
  166.7 7.0 multiply_convert_fusion.2
  174.7 3.2 fusion.92
  178.0 4.0 fusion.93
  182.0 5.3 fusion.19
  192.7 7.8 %collective-permute-done.17 = bf16[256,1024]{1,0:T(8,128)(2,1)} collective-permute-done((bf16[256,1024]{1,0:T(8,128)(2,1)}, bf16[256,1024]{1,0:T(8,128)(2,1)}, u32[]{:S(2)}, u32[]{:S(2)}) %collective-permute-start.17) | collective-permute-done | bytes 524320 | tf_op jit(solution)/shard_map/ppermute | solution.py:359
  200.5 5.6 collective-permute-done.16
  216.6 3.7 convolution_convert_fusion.3.refs_2_.refs_3_
  220.3 4.8 convolution_convert_fusion.refs_0_.refs_1_
  225.1 4.7 convolution_convert_fusion.1.refs_1_.refs_2_
  232.1 6.4 convolution_convert_fusion.2.refs_0_.refs_1_
  243.8 6.3 all-to-all-start.2
  251.6 26.8 %all-to-all-done.2 = bf16[8,256,128]{2,1,0:T(8,128)(2,1)S(1)} async-done(((bf16[8,256,128]{2,1,0:T(8,128)(2,1)}), bf16[8,256,128]{2,1,0:T(8,128)(2,1)S(1)}, u32[]{:S(2)}, u32[]{:S(2)}) %all-to-all-start.2) | async-done | bytes 524320 | tf_op jit(solution)/shard_map/all_to_all | solution.py:981
  288.9 34.0 %attend_back.1 = (bf16[2048,384]{1,0:T(8,128)(2,1)}, f32[2,8,2304]{2,1,0:T(8,128)S(1)}) custom-call(s32[8]{0:T(128)S(1)} %and_select_fusion.1.low, s32[8]{0:T(128)S(1)} %and_select_fusion.high, s32[3]{0:T(128)S(1)} %bitcast_subtract_fusion.offsets, s32[1,2048]{1,0:T(1,128)S(1)} %copy-done, s32[2048,1]{1,0:T(8,128)S(1)} %copy.151.order_col, ...), custom_call_target="tpu_custom_call" | custom-call | flops 44999999488 | bytes 12000000 | tf_op jit(solution)/shard_map/attend_back/pallas_call | solution.py:621
  332.8 5.4 all-to-all-start.3
  350.4 4.6 fusion.95
  355.1 4.9 convolution_convert_fusion.5
  361.6 4.9 convolution_convert_fusion.4
  370.4 5.2 all-to-all-done.3
  394.0 4.0 collective-permute-done.32.refs_0_
  411.4 6.4 collective-permute-done.33
  425.0 6.0 collective-permute-done.34
  433.4 15.1 %collective-permute-done.38.message = bf16[1024,384]{1,0:T(8,128)(2,1)} collective-permute-done((bf16[1024,384]{1,0:T(8,128)(2,1)S(1)}, bf16[1024,384]{1,0:T(8,128)(2,1)}, u32[]{:S(2)}, u32[]{:S(2)}) %collective-permute-start.38) | collective-permute-done | bytes 786464 | tf_op jit(solution)/shard_map/ppermute | solution.py:874
  460.7 4.8 broadcast_select_fusion.1
  475.3 21.3 %collective-permute-done.41.refs_0_ = bf16[1088,512]{1,0:T(8,128)(2,1)} collective-permute-done((bf16[1088,512]{1,0:T(8,128)(2,1)}, bf16[1088,512]{1,0:T(8,128)(2,1)}, u32[]{:S(2)}, u32[]{:S(2)}) %collective-permute-start.41) | collective-permute-done | bytes 1114144 | tf_op jit(solution)/shard_map/ppermute | solution.py:830
  511.2 32.2 %collective-permute-done.49.message = bf16[1024,384]{1,0:T(8,128)(2,1)S(1)} collective-permute-done((bf16[1024,384]{1,0:T(8,128)(2,1)}, bf16[1024,384]{1,0:T(8,128)(2,1)S(1)}, u32[]{:S(2)}, u32[]{:S(2)}) %collective-permute-start.49) | collective-permute-done | bytes 786464 | tf_op jit(solution)/shard_map/ppermute | solution.py:872
  559.4 31.1 %collective-permute-done.53.message = bf16[1024,384]{1,0:T(8,128)(2,1)S(1)} collective-permute-done((bf16[1024,384]{1,0:T(8,128)(2,1)}, bf16[1024,384]{1,0:T(8,128)(2,1)S(1)}, u32[]{:S(2)}, u32[]{:S(2)}) %collective-permute-start.53) | collective-permute-done | bytes 786464 | tf_op jit(solution)/shard_map/ppermute | solution.py:872
  590.5 3.5 fold.31.message
  606.8 14.5 %collective-permute-done.54.message = bf16[1088,512]{1,0:T(8,128)(2,1)S(1)} collective-permute-done((bf16[1088,512]{1,0:T(8,128)(2,1)}, bf16[1088,512]{1,0:T(8,128)(2,1)S(1)}, u32[]{:S(2)}, u32[]{:S(2)}) %collective-permute-start.54) | collective-permute-done | bytes 1114144 | tf_op jit(solution)/shard_map/ppermute | solution.py:830
  627.7 3.3 all-to-all-start.5
  636.5 9.7 %collective-permute-done.56.message = bf16[1088,512]{1,0:T(8,128)(2,1)} collective-permute-done((bf16[1088,512]{1,0:T(8,128)(2,1)S(1)}, bf16[1088,512]{1,0:T(8,128)(2,1)}, u32[]{:S(2)}, u32[]{:S(2)}) %collective-permute-start.56) | collective-permute-done | bytes 1114144 | tf_op jit(solution)/shard_map/ppermute | solution.py:830
  651.1 3.5 all-to-all-start.4
  654.6 4.9 multiply_convert_fusion
  659.5 10.4 %all-to-all-done.4 = f32[8,1,2304]{2,1,0:T(1,128)S(1)} async-done(((f32[8,1,2304]{2,1,0:T(1,128)}), f32[8,1,2304]{2,1,0:T(1,128)S(1)}, u32[]{:S(2)}, u32[]{:S(2)}) %all-to-all-start.4) | async-done | bytes 73760 | tf_op jit(solution)/shard_map/all_to_all | solution.py:810
  683.8 16.6 %collective-permute-done.60.message = bf16[1088,512]{1,0:T(8,128)(2,1)S(1)} collective-permute-done((bf16[1088,512]{1,0:T(8,128)(2,1)S(1)}, bf16[1088,512]{1,0:T(8,128)(2,1)S(1)}, u32[]{:S(2)}, u32[]{:S(2)}) %collective-permute-start.60) | collective-permute-done | bytes 1114144 | tf_op jit(solution)/shard_map/ppermute | solution.py:830
  709.4 15.4 %collective-permute-done.62.message = bf16[1088,512]{1,0:T(8,128)(2,1)S(1)} collective-permute-done((bf16[1088,512]{1,0:T(8,128)(2,1)S(1)}, bf16[1088,512]{1,0:T(8,128)(2,1)S(1)}, u32[]{:S(2)}, u32[]{:S(2)}) %collective-permute-start.62) | collective-permute-done | bytes 1114144 | tf_op jit(solution)/shard_map/ppermute | solution.py:830
  734.0 16.0 %collective-permute-done.64.message = bf16[1088,512]{1,0:T(8,128)(2,1)S(1)} collective-permute-done((bf16[1088,512]{1,0:T(8,128)(2,1)S(1)}, bf16[1088,512]{1,0:T(8,128)(2,1)S(1)}, u32[]{:S(2)}, u32[]{:S(2)}) %collective-permute-start.64) | collective-permute-done | bytes 1114144 | tf_op jit(solution)/shard_map/ppermute | solution.py:830
  758.9 8.4 %collective-permute-done.66.message = bf16[1088,512]{1,0:T(8,128)(2,1)} collective-permute-done((bf16[1088,512]{1,0:T(8,128)(2,1)S(1)}, bf16[1088,512]{1,0:T(8,128)(2,1)}, u32[]{:S(2)}, u32[]{:S(2)}) %collective-permute-start.66) | collective-permute-done | bytes 1114144 | tf_op jit(solution)/shard_map/ppermute | solution.py:830
  (455 shorter events, 284.6 us)
Async XLA Ops:
  19.0 44.6 %all-to-all-start = ((bf16[8,256,384]{2,1,0:T(8,128)(2,1)}), bf16[8,256,384]{2,1,0:T(8,128)(2,1)S(1)}, u32[]{:S(2)}, u32[]{:S(2)}) async-start(bf16[8,256,384]{2,1,0:T(8,128)(2,1)} %copy.150), calls=%async_computation | async-start | bytes 3145728 | tf_op jit(solution)/shard_map/all_to_all | solution.py:981
  26.3 96.7 %collective-permute-start.7 = (bf16[1024,1024]{1,0:T(8,128)(2,1)}, bf16[1024,1024]{1,0:T(8,128)(2,1)}, u32[]{:S(2)}, u32[]{:S(2)}) collective-permute-start(bf16[1024,1024]{1,0:T(8,128)(2,1)} %param.24), channel_id=1, source_target_pairs={{0,16},{16,0},{1,17},{17,1},{2,18},{18,2},{3,19},{19,3},{4,20},{20... | collective-permute-start | bytes 6291464 | tf_op jit(solution)/shard_map/ppermute | solution.py:359
  26.3 136.4 %collective-permute-start.13 = (bf16[1024,2560]{1,0:T(8,128)(2,1)}, bf16[1024,2560]{1,0:T(8,128)(2,1)}, u32[]{:S(2)}, u32[]{:S(2)}) collective-permute-start(bf16[1024,2560]{1,0:T(8,128)(2,1)} %param.27), channel_id=1, source_target_pairs={{0,16},{16,0},{1,17},{17,1},{2,18},{18,2},{3,19},{19,3},{4,20},{20... | collective-permute-start | bytes 15728648 | tf_op jit(solution)/shard_map/ppermute | solution.py:359
  26.8 99.4 %collective-permute-start.11 = (bf16[2560,1024]{1,0:T(8,128)(2,1)}, bf16[2560,1024]{1,0:T(8,128)(2,1)}, u32[]{:S(2)}, u32[]{:S(2)}) collective-permute-start(bf16[2560,1024]{1,0:T(8,128)(2,1)} %param.29), channel_id=1, source_target_pairs={{0,16},{16,0},{1,17},{17,1},{2,18},{18,2},{3,19},{19,3},{4,20},{20... | collective-permute-start | bytes 15728648 | tf_op jit(solution)/shard_map/ppermute | solution.py:359
  63.6 32.9 %collective-permute-start.5 = (bf16[256,2048]{1,0:T(8,128)(2,1)}, bf16[256,2048]{1,0:T(8,128)(2,1)}, u32[]{:S(2)}, u32[]{:S(2)}) collective-permute-start(bf16[256,2048]{1,0:T(8,128)(2,1)} %pad_maximum_fusion.1), channel_id=1, source_target_pairs={{0,2},{4,0},{8,4},{12,8},{14,12},{10,14},{6,10},{2,6},{1,3},{5,1},... | collective-permute-start | bytes 3145736 | tf_op jit(solution)/shard_map/ppermute | solution.py:874
  65.0 31.4 %collective-permute-start.4 = (bf16[256,2048]{1,0:T(8,128)(2,1)}, bf16[256,2048]{1,0:T(8,128)(2,1)}, u32[]{:S(2)}, u32[]{:S(2)}) collective-permute-start(bf16[256,2048]{1,0:T(8,128)(2,1)} %pad_maximum_fusion.1), channel_id=1, source_target_pairs={{0,4},{4,8},{8,12},{12,14},{14,10},{10,6},{6,2},{2,0},{1,5},{5,9},... | collective-permute-start | bytes 3145736 | tf_op jit(solution)/shard_map/ppermute | solution.py:872
  101.7 65.0 %collective-permute-start.12 = (bf16[1024,2560]{1,0:T(8,128)(2,1)}, bf16[1024,2560]{1,0:T(8,128)(2,1)}, u32[]{:S(2)}, u32[]{:S(2)}) collective-permute-start(bf16[1024,2560]{1,0:T(8,128)(2,1)} %param.28), channel_id=1, source_target_pairs={{0,16},{16,0},{1,17},{17,1},{2,18},{18,2},{3,19},{19,3},{4,20},{20... | collective-permute-start | bytes 15728648 | tf_op jit(solution)/shard_map/ppermute | solution.py:359
  126.1 23.7 %collective-permute-start.9 = (bf16[256,2048]{1,0:T(8,128)(2,1)}, bf16[256,2048]{1,0:T(8,128)(2,1)S(1)}, u32[]{:S(2)}, u32[]{:S(2)}) collective-permute-start(bf16[256,2048]{1,0:T(8,128)(2,1)} %collective-permute-done.4), channel_id=1, source_target_pairs={{0,4},{4,8},{8,12},{12,14},{14,10},{10,6},{6,2},{2,0},{1,5},{5,9},... | collective-permute-start | bytes 3145736 | tf_op jit(solution)/shard_map/ppermute | solution.py:872
  132.2 23.2 %collective-permute-start.10 = (bf16[256,2048]{1,0:T(8,128)(2,1)}, bf16[256,2048]{1,0:T(8,128)(2,1)S(1)}, u32[]{:S(2)}, u32[]{:S(2)}) collective-permute-start(bf16[256,2048]{1,0:T(8,128)(2,1)} %collective-permute-done.5), channel_id=1, source_target_pairs={{0,2},{4,0},{8,4},{12,8},{14,12},{10,14},{6,10},{2,6},{1,3},{5,1},... | collective-permute-start | bytes 3145736 | tf_op jit(solution)/shard_map/ppermute | solution.py:874
  192.2 28.0 %collective-permute-start.21 = (bf16[256,1024]{1,0:T(8,128)(2,1)}, bf16[256,1024]{1,0:T(8,128)(2,1)S(1)}, u32[]{:S(2)}, u32[]{:S(2)}) collective-permute-start(bf16[256,1024]{1,0:T(8,128)(2,1)} %copy-done.36), channel_id=1, source_target_pairs={{0,16},{16,0},{1,17},{17,1},{2,18},{18,2},{3,19},{19,3},{4,20},{20... | collective-permute-start | bytes 1572872 | tf_op jit(solution)/shard_map/ppermute | solution.py:359
  240.8 37.6 %collective-permute-start.25 = (bf16[1088,512]{1,0:T(8,128)(2,1)}, bf16[1088,512]{1,0:T(8,128)(2,1)}, u32[]{:S(2)}, u32[]{:S(2)}) collective-permute-start(bf16[1088,512]{1,0:T(8,128)(2,1)} %fold.16), channel_id=1, source_target_pairs={{0,4},{4,8},{8,12},{12,14},{14,10},{10,6},{6,2},{2,0},{1,5},{5,9},... | collective-permute-start | bytes 3342344 | tf_op jit(solution)/shard_map/ppermute | solution.py:830
  240.8 37.6 %collective-permute-start.27 = (bf16[1088,512]{1,0:T(8,128)(2,1)}, bf16[1088,512]{1,0:T(8,128)(2,1)}, u32[]{:S(2)}, u32[]{:S(2)}) collective-permute-start(bf16[1088,512]{1,0:T(8,128)(2,1)} %fold.17), channel_id=1, source_target_pairs={{0,2},{4,0},{8,4},{12,8},{14,12},{10,14},{6,10},{2,6},{1,3},{5,1},... | collective-permute-start | bytes 3342344 | tf_op jit(solution)/shard_map/ppermute | solution.py:830
  243.8 34.6 %all-to-all-start.2 = ((bf16[8,256,128]{2,1,0:T(8,128)(2,1)}), bf16[8,256,128]{2,1,0:T(8,128)(2,1)S(1)}, u32[]{:S(2)}, u32[]{:S(2)}) async-start(bf16[8,256,128]{2,1,0:T(8,128)(2,1)} %bitcast_bitcast_fusion), calls=%async_computation.2 | async-start | bytes 1048576 | tf_op jit(solution)/shard_map/all_to_all | solution.py:981
  284.0 38.9 %collective-permute-start.28 = (bf16[1088,512]{1,0:T(8,128)(2,1)}, bf16[1088,512]{1,0:T(8,128)(2,1)}, u32[]{:S(2)}, u32[]{:S(2)}) collective-permute-start(bf16[1088,512]{1,0:T(8,128)(2,1)} %fold.18), channel_id=1, source_target_pairs={{0,4},{4,8},{8,12},{12,14},{14,10},{10,6},{6,2},{2,0},{1,5},{5,9},... | collective-permute-start | bytes 3342344 | tf_op jit(solution)/shard_map/ppermute | solution.py:830
  285.8 37.2 %collective-permute-start.29 = (bf16[1088,512]{1,0:T(8,128)(2,1)}, bf16[1088,512]{1,0:T(8,128)(2,1)}, u32[]{:S(2)}, u32[]{:S(2)}) collective-permute-start(bf16[1088,512]{1,0:T(8,128)(2,1)} %fold.19), channel_id=1, source_target_pairs={{0,2},{4,0},{8,4},{12,8},{14,12},{10,14},{6,10},{2,6},{1,3},{5,1},... | collective-permute-start | bytes 3342344 | tf_op jit(solution)/shard_map/ppermute | solution.py:830
  332.8 42.8 %all-to-all-start.3 = ((bf16[8,256,384]{1,2,0:T(8,128)(2,1)}), bf16[8,256,384]{1,2,0:T(8,128)(2,1)}, u32[]{:S(2)}, u32[]{:S(2)}) async-start(bf16[8,256,384]{1,2,0:T(8,128)(2,1)} %copy.155), calls=%async_computation.3 | async-start | bytes 3145728 | tf_op jit(solution)/shard_map/all_to_all | solution.py:986
  360.0 47.2 %collective-permute-start.39 = (bf16[256,1024]{1,0:T(8,128)(2,1)}, bf16[256,1024]{1,0:T(8,128)(2,1)}, u32[]{:S(2)}, u32[]{:S(2)}) collective-permute-start(bf16[256,1024]{1,0:T(8,128)(2,1)} %convolution_convert_fusion.5), channel_id=1, source_target_pairs={{0,1},{1,0},{2,3},{3,2},{4,5},{5,4},{6,7},{7,6},{8,9},{9,8},{10,11... | collective-permute-start | bytes 1572872 | tf_op jit(solution)/shard_map/ppermute | solution.py:359
  366.5 40.7 %collective-permute-start.40 = (bf16[256,1024]{1,0:T(8,128)(2,1)}, bf16[256,1024]{1,0:T(8,128)(2,1)}, u32[]{:S(2)}, u32[]{:S(2)}) collective-permute-start(bf16[256,1024]{1,0:T(8,128)(2,1)} %convolution_convert_fusion.4), channel_id=1, source_target_pairs={{0,1},{1,0},{2,3},{3,2},{4,5},{5,4},{6,7},{7,6},{8,9},{9,8},{10,11... | collective-permute-start | bytes 1572872 | tf_op jit(solution)/shard_map/ppermute | solution.py:359
  367.0 27.0 %collective-permute-start.31 = (bf16[1088,512]{1,0:T(8,128)(2,1)}, bf16[1088,512]{1,0:T(8,128)(2,1)}, u32[]{:S(2)}, u32[]{:S(2)}) collective-permute-start(bf16[1088,512]{1,0:T(8,128)(2,1)} %fold.20), channel_id=1, source_target_pairs={{0,4},{4,8},{8,12},{12,14},{14,10},{10,6},{6,2},{2,0},{1,5},{5,9},... | collective-permute-start | bytes 3342344 | tf_op jit(solution)/shard_map/ppermute | solution.py:830
  369.0 29.0 %collective-permute-start.32 = (bf16[1088,512]{1,0:T(8,128)(2,1)}, bf16[1088,512]{1,0:T(8,128)(2,1)}, u32[]{:S(2)}, u32[]{:S(2)}) collective-permute-start(bf16[1088,512]{1,0:T(8,128)(2,1)} %fold.21), channel_id=1, source_target_pairs={{0,2},{4,0},{8,4},{12,8},{14,12},{10,14},{6,10},{2,6},{1,3},{5,1},... | collective-permute-start | bytes 3342344 | tf_op jit(solution)/shard_map/ppermute | solution.py:830
  405.2 43.3 %collective-permute-start.35 = (bf16[1088,512]{1,0:T(8,128)(2,1)}, bf16[1088,512]{1,0:T(8,128)(2,1)}, u32[]{:S(2)}, u32[]{:S(2)}) collective-permute-start(bf16[1088,512]{1,0:T(8,128)(2,1)} %fold.22), channel_id=1, source_target_pairs={{0,4},{4,8},{8,12},{12,14},{14,10},{10,6},{6,2},{2,0},{1,5},{5,9},... | collective-permute-start | bytes 3342344 | tf_op jit(solution)/shard_map/ppermute | solution.py:830
  405.8 42.7 %collective-permute-start.36 = (bf16[1088,512]{1,0:T(8,128)(2,1)}, bf16[1088,512]{1,0:T(8,128)(2,1)}, u32[]{:S(2)}, u32[]{:S(2)}) collective-permute-start(bf16[1088,512]{1,0:T(8,128)(2,1)} %fold.23), channel_id=1, source_target_pairs={{0,2},{4,0},{8,4},{12,8},{14,12},{10,14},{6,10},{2,6},{1,3},{5,1},... | collective-permute-start | bytes 3342344 | tf_op jit(solution)/shard_map/ppermute | solution.py:830
  409.3 39.2 %collective-permute-start.38 = (bf16[1024,384]{1,0:T(8,128)(2,1)S(1)}, bf16[1024,384]{1,0:T(8,128)(2,1)}, u32[]{:S(2)}, u32[]{:S(2)}) collective-permute-start(bf16[1024,384]{1,0:T(8,128)(2,1)S(1)} %copy-done.37), channel_id=1, source_target_pairs={{0,2},{4,0},{8,4},{12,8},{14,12},{10,14},{6,10},{2,6},{1,3},{5,1},... | collective-permute-start | bytes 2359304 | tf_op jit(solution)/shard_map/ppermute | solution.py:874
  410.4 38.1 %collective-permute-start.37 = (bf16[1024,384]{1,0:T(8,128)(2,1)S(1)}, bf16[1024,384]{1,0:T(8,128)(2,1)}, u32[]{:S(2)}, u32[]{:S(2)}) collective-permute-start(bf16[1024,384]{1,0:T(8,128)(2,1)S(1)} %copy-done.37), channel_id=1, source_target_pairs={{0,4},{4,8},{8,12},{12,14},{14,10},{10,6},{6,2},{2,0},{1,5},{5,9},... | collective-permute-start | bytes 2359304 | tf_op jit(solution)/shard_map/ppermute | solution.py:872
  454.1 20.8 %collective-permute-start.43 = (bf16[1024,384]{1,0:T(8,128)(2,1)}, bf16[1024,384]{1,0:T(8,128)(2,1)}, u32[]{:S(2)}, u32[]{:S(2)}) collective-permute-start(bf16[1024,384]{1,0:T(8,128)(2,1)} %collective-permute-done.37.message), channel_id=1, source_target_pairs={{0,4},{4,8},{8,12},{12,14},{14,10},{10,6},{6,2},{2,0},{1,5},{5,9},... | collective-permute-start | bytes 2359304 | tf_op jit(solution)/shard_map/ppermute | solution.py:872
  454.5 20.8 %collective-permute-start.44 = (bf16[1024,384]{1,0:T(8,128)(2,1)}, bf16[1024,384]{1,0:T(8,128)(2,1)}, u32[]{:S(2)}, u32[]{:S(2)}) collective-permute-start(bf16[1024,384]{1,0:T(8,128)(2,1)} %collective-permute-done.38.message), channel_id=1, source_target_pairs={{0,2},{4,0},{8,4},{12,8},{14,12},{10,14},{6,10},{2,6},{1,3},{5,1},... | collective-permute-start | bytes 2359304 | tf_op jit(solution)/shard_map/ppermute | solution.py:874
  456.2 40.4 %collective-permute-start.41 = (bf16[1088,512]{1,0:T(8,128)(2,1)}, bf16[1088,512]{1,0:T(8,128)(2,1)}, u32[]{:S(2)}, u32[]{:S(2)}) collective-permute-start(bf16[1088,512]{1,0:T(8,128)(2,1)} %fold.24), channel_id=1, source_target_pairs={{0,4},{4,8},{8,12},{12,14},{14,10},{10,6},{6,2},{2,0},{1,5},{5,9},... | collective-permute-start | bytes 3342344 | tf_op jit(solution)/shard_map/ppermute | solution.py:830
  456.5 40.2 %collective-permute-start.42 = (bf16[1088,512]{1,0:T(8,128)(2,1)}, bf16[1088,512]{1,0:T(8,128)(2,1)}, u32[]{:S(2)}, u32[]{:S(2)}) collective-permute-start(bf16[1088,512]{1,0:T(8,128)(2,1)} %fold.25), channel_id=1, source_target_pairs={{0,2},{4,0},{8,4},{12,8},{14,12},{10,14},{6,10},{2,6},{1,3},{5,1},... | collective-permute-start | bytes 3342344 | tf_op jit(solution)/shard_map/ppermute | solution.py:830
  502.3 42.0 %collective-permute-start.47 = (bf16[1088,512]{1,0:T(8,128)(2,1)S(1)}, bf16[1088,512]{1,0:T(8,128)(2,1)S(1)}, u32[]{:S(2)}, u32[]{:S(2)}) collective-permute-start(bf16[1088,512]{1,0:T(8,128)(2,1)S(1)} %copy-done.48), channel_id=1, source_target_pairs={{0,4},{4,8},{8,12},{12,14},{14,10},{10,6},{6,2},{2,0},{1,5},{5,9},... | collective-permute-start | bytes 3342344 | tf_op jit(solution)/shard_map/ppermute | solution.py:830
  503.6 40.7 %collective-permute-start.48 = (bf16[1088,512]{1,0:T(8,128)(2,1)}, bf16[1088,512]{1,0:T(8,128)(2,1)}, u32[]{:S(2)}, u32[]{:S(2)}) collective-permute-start(bf16[1088,512]{1,0:T(8,128)(2,1)} %fold.27), channel_id=1, source_target_pairs={{0,2},{4,0},{8,4},{12,8},{14,12},{10,14},{6,10},{2,6},{1,3},{5,1},... | collective-permute-start | bytes 3342344 | tf_op jit(solution)/shard_map/ppermute | solution.py:830
  504.3 39.1 %collective-permute-start.49 = (bf16[1024,384]{1,0:T(8,128)(2,1)}, bf16[1024,384]{1,0:T(8,128)(2,1)S(1)}, u32[]{:S(2)}, u32[]{:S(2)}) collective-permute-start(bf16[1024,384]{1,0:T(8,128)(2,1)} %collective-permute-done.43.message), channel_id=1, source_target_pairs={{0,4},{4,8},{8,12},{12,14},{14,10},{10,6},{6,2},{2,0},{1,5},{5,9},... | collective-permute-start | bytes 2359304 | tf_op jit(solution)/shard_map/ppermute | solution.py:872
  505.6 38.7 %collective-permute-start.50 = (bf16[1024,384]{1,0:T(8,128)(2,1)}, bf16[1024,384]{1,0:T(8,128)(2,1)}, u32[]{:S(2)}, u32[]{:S(2)}) collective-permute-start(bf16[1024,384]{1,0:T(8,128)(2,1)} %collective-permute-done.44.message), channel_id=1, source_target_pairs={{0,2},{4,0},{8,4},{12,8},{14,12},{10,14},{6,10},{2,6},{1,3},{5,1},... | collective-permute-start | bytes 2359304 | tf_op jit(solution)/shard_map/ppermute | solution.py:874
  551.0 39.5 %collective-permute-start.51 = (bf16[1088,512]{1,0:T(8,128)(2,1)S(1)}, bf16[1088,512]{1,0:T(8,128)(2,1)S(1)}, u32[]{:S(2)}, u32[]{:S(2)}) collective-permute-start(bf16[1088,512]{1,0:T(8,128)(2,1)S(1)} %copy-done.50), channel_id=1, source_target_pairs={{0,4},{4,8},{8,12},{12,14},{14,10},{10,6},{6,2},{2,0},{1,5},{5,9},... | collective-permute-start | bytes 3342344 | tf_op jit(solution)/shard_map/ppermute | solution.py:830
  552.7 37.8 %collective-permute-start.52 = (bf16[1088,512]{1,0:T(8,128)(2,1)}, bf16[1088,512]{1,0:T(8,128)(2,1)}, u32[]{:S(2)}, u32[]{:S(2)}) collective-permute-start(bf16[1088,512]{1,0:T(8,128)(2,1)} %fold.29), channel_id=1, source_target_pairs={{0,2},{4,0},{8,4},{12,8},{14,12},{10,14},{6,10},{2,6},{1,3},{5,1},... | collective-permute-start | bytes 3342344 | tf_op jit(solution)/shard_map/ppermute | solution.py:830
  553.0 37.5 %collective-permute-start.53 = (bf16[1024,384]{1,0:T(8,128)(2,1)}, bf16[1024,384]{1,0:T(8,128)(2,1)S(1)}, u32[]{:S(2)}, u32[]{:S(2)}) collective-permute-start(bf16[1024,384]{1,0:T(8,128)(2,1)} %copy-done.58), channel_id=1, source_target_pairs={{0,4},{4,8},{8,12},{12,14},{14,10},{10,6},{6,2},{2,0},{1,5},{5,9},... | collective-permute-start | bytes 2359304 | tf_op jit(solution)/shard_map/ppermute | solution.py:872
  596.9 24.5 %collective-permute-start.54 = (bf16[1088,512]{1,0:T(8,128)(2,1)}, bf16[1088,512]{1,0:T(8,128)(2,1)S(1)}, u32[]{:S(2)}, u32[]{:S(2)}) collective-permute-start(bf16[1088,512]{1,0:T(8,128)(2,1)} %fold.30.message), channel_id=1, source_target_pairs={{0,4},{4,8},{8,12},{12,14},{14,10},{10,6},{6,2},{2,0},{1,5},{5,9},... | collective-permute-start | bytes 3342344 | tf_op jit(solution)/shard_map/ppermute | solution.py:830
  598.6 23.8 %collective-permute-start.55 = (bf16[1088,512]{1,0:T(8,128)(2,1)S(1)}, bf16[1088,512]{1,0:T(8,128)(2,1)}, u32[]{:S(2)}, u32[]{:S(2)}) collective-permute-start(bf16[1088,512]{1,0:T(8,128)(2,1)S(1)} %copy-done.31), channel_id=1, source_target_pairs={{0,2},{4,0},{8,4},{12,8},{14,12},{10,14},{6,10},{2,6},{1,3},{5,1},... | collective-permute-start | bytes 3342344 | tf_op jit(solution)/shard_map/ppermute | solution.py:830
  622.4 23.7 %collective-permute-start.56 = (bf16[1088,512]{1,0:T(8,128)(2,1)S(1)}, bf16[1088,512]{1,0:T(8,128)(2,1)}, u32[]{:S(2)}, u32[]{:S(2)}) collective-permute-start(bf16[1088,512]{1,0:T(8,128)(2,1)S(1)} %collective-permute-done.54.message), channel_id=1, source_target_pairs={{0,4},{4,8},{8,12},{12,14},{14,10},{10,6},{6,2},{2,0},{1,5},{5,9},... | collective-permute-start | bytes 3342344 | tf_op jit(solution)/shard_map/ppermute | solution.py:830
  623.4 23.6 %collective-permute-start.57 = (bf16[1088,512]{1,0:T(8,128)(2,1)}, bf16[1088,512]{1,0:T(8,128)(2,1)}, u32[]{:S(2)}, u32[]{:S(2)}) collective-permute-start(bf16[1088,512]{1,0:T(8,128)(2,1)} %collective-permute-done.55.message), channel_id=1, source_target_pairs={{0,2},{4,0},{8,4},{12,8},{14,12},{10,14},{6,10},{2,6},{1,3},{5,1},... | collective-permute-start | bytes 3342344 | tf_op jit(solution)/shard_map/ppermute | solution.py:830
  627.7 21.3 %all-to-all-start.5 = ((f32[8,1,2]{2,1,0:T(1,128)}), f32[8,1,2]{2,1,0:T(1,128)S(1)}, u32[]{:S(2)}, u32[]{:S(2)}) async-start(f32[8,1,2]{2,1,0:T(1,128)} %broadcast_in_dim.53), calls=%async_computation.5 | async-start | bytes 8192 | tf_op jit(solution)/shard_map/all_to_all | solution.py:810
  647.0 29.5 %collective-permute-start.58 = (bf16[1088,512]{1,0:T(8,128)(2,1)}, bf16[1088,512]{1,0:T(8,128)(2,1)S(1)}, u32[]{:S(2)}, u32[]{:S(2)}) collective-permute-start(bf16[1088,512]{1,0:T(8,128)(2,1)} %collective-permute-done.56.message), channel_id=1, source_target_pairs={{0,4},{4,8},{8,12},{12,14},{14,10},{10,6},{6,2},{2,0},{1,5},{5,9},... | collective-permute-start | bytes 3342344 | tf_op jit(solution)/shard_map/ppermute | solution.py:830
  647.6 28.8 %collective-permute-start.59 = (bf16[1088,512]{1,0:T(8,128)(2,1)}, bf16[1088,512]{1,0:T(8,128)(2,1)}, u32[]{:S(2)}, u32[]{:S(2)}) collective-permute-start(bf16[1088,512]{1,0:T(8,128)(2,1)} %collective-permute-done.57.message), channel_id=1, source_target_pairs={{0,2},{4,0},{8,4},{12,8},{14,12},{10,14},{6,10},{2,6},{1,3},{5,1},... | collective-permute-start | bytes 3342344 | tf_op jit(solution)/shard_map/ppermute | solution.py:830
  676.5 24.0 %collective-permute-start.60 = (bf16[1088,512]{1,0:T(8,128)(2,1)S(1)}, bf16[1088,512]{1,0:T(8,128)(2,1)S(1)}, u32[]{:S(2)}, u32[]{:S(2)}) collective-permute-start(bf16[1088,512]{1,0:T(8,128)(2,1)S(1)} %collective-permute-done.58.message), channel_id=1, source_target_pairs={{0,4},{4,8},{8,12},{12,14},{14,10},{10,6},{6,2},{2,0},{1,5},{5,9},... | collective-permute-start | bytes 3342344 | tf_op jit(solution)/shard_map/ppermute | solution.py:830
  677.4 24.6 %collective-permute-start.61 = (bf16[1088,512]{1,0:T(8,128)(2,1)}, bf16[1088,512]{1,0:T(8,128)(2,1)}, u32[]{:S(2)}, u32[]{:S(2)}) collective-permute-start(bf16[1088,512]{1,0:T(8,128)(2,1)} %collective-permute-done.59.message), channel_id=1, source_target_pairs={{0,2},{4,0},{8,4},{12,8},{14,12},{10,14},{6,10},{2,6},{1,3},{5,1},... | collective-permute-start | bytes 3342344 | tf_op jit(solution)/shard_map/ppermute | solution.py:830
  702.0 22.7 %collective-permute-start.62 = (bf16[1088,512]{1,0:T(8,128)(2,1)S(1)}, bf16[1088,512]{1,0:T(8,128)(2,1)S(1)}, u32[]{:S(2)}, u32[]{:S(2)}) collective-permute-start(bf16[1088,512]{1,0:T(8,128)(2,1)S(1)} %collective-permute-done.60.message), channel_id=1, source_target_pairs={{0,4},{4,8},{8,12},{12,14},{14,10},{10,6},{6,2},{2,0},{1,5},{5,9},... | collective-permute-start | bytes 3342344 | tf_op jit(solution)/shard_map/ppermute | solution.py:830
  702.0 23.6 %collective-permute-start.63 = (bf16[1088,512]{1,0:T(8,128)(2,1)}, bf16[1088,512]{1,0:T(8,128)(2,1)S(1)}, u32[]{:S(2)}, u32[]{:S(2)}) collective-permute-start(bf16[1088,512]{1,0:T(8,128)(2,1)} %collective-permute-done.61.message), channel_id=1, source_target_pairs={{0,2},{4,0},{8,4},{12,8},{14,12},{10,14},{6,10},{2,6},{1,3},{5,1},... | collective-permute-start | bytes 3342344 | tf_op jit(solution)/shard_map/ppermute | solution.py:830
  726.7 23.3 %collective-permute-start.64 = (bf16[1088,512]{1,0:T(8,128)(2,1)S(1)}, bf16[1088,512]{1,0:T(8,128)(2,1)S(1)}, u32[]{:S(2)}, u32[]{:S(2)}) collective-permute-start(bf16[1088,512]{1,0:T(8,128)(2,1)S(1)} %collective-permute-done.62.message), channel_id=1, source_target_pairs={{0,4},{4,8},{8,12},{12,14},{14,10},{10,6},{6,2},{2,0},{1,5},{5,9},... | collective-permute-start | bytes 3342344 | tf_op jit(solution)/shard_map/ppermute | solution.py:830
  726.8 24.8 %collective-permute-start.65 = (bf16[1088,512]{1,0:T(8,128)(2,1)}, bf16[1088,512]{1,0:T(8,128)(2,1)S(1)}, u32[]{:S(2)}, u32[]{:S(2)}) collective-permute-start(bf16[1088,512]{1,0:T(8,128)(2,1)} %copy-done.45), channel_id=1, source_target_pairs={{0,2},{4,0},{8,4},{12,8},{14,12},{10,14},{6,10},{2,6},{1,3},{5,1},... | collective-permute-start | bytes 3342344 | tf_op jit(solution)/shard_map/ppermute | solution.py:830
  (112 other events, 911.5 us)

commit v3 on v2

--- a/solution.py
+++ b/solution.py
@@ -1,3 +1,5 @@
+import functools
+
 import jax
 import jax.numpy as jnp
 from jax import lax
@@ -344,6 +346,7 @@
 
 
 RING = (0, 2, 4, 6, 7, 5, 3, 1)
+OUT_ROUND = 1
 F32 = jnp.float32
 BF16 = jnp.bfloat16
 
@@ -401,16 +404,36 @@
     return pl.ds(pl.multiple_of(index * TILE, TILE), TILE)
 
 
-def put_in_order(order_row, source, index):
-    position = index * TILE + lax.broadcasted_iota(jnp.int32, (TILE, source.shape[0]), 0)
-    hot = (order_row[...] == position).astype(F32).astype(BF16)
-    return dot_f32(hot, source[...])
-
-
-def put_back(order_col, source, index):
-    position = lax.broadcasted_iota(jnp.int32, (TILE, source.shape[0]), 1)
-    hot = (order_col[tile_rows(index), :] == position).astype(F32).astype(BF16)
-    return dot_f32(hot, source[...]).astype(BF16)
+MOVED = 1024
+
+
+def moved_rows(index):
+    return pl.ds(pl.multiple_of(index * MOVED, MOVED), MOVED)
+
+
+def put_in_order(order_row, source, target):
+    @pl.loop(0, source.shape[0] // MOVED)
+    def part(index):
+        position = index * MOVED + lax.broadcasted_iota(jnp.int32, (MOVED, source.shape[0]), 0)
+        hot = (order_row[...] == position).astype(F32).astype(BF16)
+        target[moved_rows(index), :] = dot_f32(hot, source[...]).astype(BF16)
+
+
+def put_back(order_col, source, target):
+    @pl.loop(0, source.shape[0] // MOVED)
+    def part(index):
+        position = lax.broadcasted_iota(jnp.int32, (MOVED, source.shape[0]), 1)
+        hot = (order_col[moved_rows(index), :] == position).astype(F32).astype(BF16)
+        target[moved_rows(index), :] = dot_f32(hot, source[...]).astype(BF16)
+
+
+def tile_pairs(low, high, tiles):
+    pairs = (high - low + 1) // 2
+    return (jnp.minimum(low, tiles - 2 * pairs), pairs)
+
+
+def strip_place(distance, reach):
+    return tile_rows(jnp.clip(distance + reach, 0, 2 * reach))
 
 
 def fill_strip(strip, table):
@@ -439,13 +462,13 @@
     reach = strip.shape[2] // TILE // 2
     lane = lane_of(TILE)
     fill_strip(strip, table)
+    put_in_order(order_row, mixed, ordered)
     tops[...] = jnp.full(tops.shape, -FAR_OFF, F32)
 
     @pl.loop(0, tiles)
     def arrange(index):
         rows = tile_rows(index)
-        block = put_in_order(order_row, mixed, index)
-        ordered[rows, :] = block.astype(BF16)
+        block = ordered[rows, :].astype(F32)
         sequence = sequence_of(offsets, index * TILE)
         for head in range(2):
             own, spare = head_lanes(lane, head)
@@ -463,17 +486,35 @@
         rows = tile_rows(index)
         total[...] = jnp.zeros(total.shape, F32)
 
-        @pl.loop(low[index], high[index])
-        def keys(other):
-            columns = tile_rows(other)
-            place = tile_rows(other - index + reach)
+        start, pairs = tile_pairs(low[index], high[index], tiles)
+
+        @pl.loop(0, pairs)
+        def keys(pair):
+            others = [start + 2 * pair, start + 2 * pair + 1]
+            columns = [tile_rows(other) for other in others]
+            places = [strip_place(other - index, reach) for other in others]
+            cases = [(head, side) for head in range(2) for side in range(2)]
+            raws = [
+                dot_nt(query_aug[head, rows, :], key_aug[head, columns[side], :])
+                for head, side in cases
+            ]
+            weights = [
+                jnp.exp(raw + strip[head, :, places[side]]).astype(BF16)
+                for raw, (head, side) in zip(raws, cases)
+            ]
             for head in range(2):
-                raw = dot_nt(query_aug[head, rows, :], key_aug[head, columns, :])
                 tops[head] = jnp.maximum(
-                    tops[head], jnp.max(raw.reshape(TILE // 8, 8, TILE), axis=0)
+                    tops[head],
+                    jnp.max(
+                        jnp.maximum(raws[2 * head], raws[2 * head + 1]).reshape(
+                            TILE // 8, 8, TILE
+                        ),
+                        axis=0,
+                    ),
                 )
-                weight = jnp.exp(raw + strip[head, :, place]).astype(BF16)
-                total[head] += dot_f32(weight, value_aug[head, columns, :])
+                total[head] += dot_f32(
+                    weights[2 * head], value_aug[head, columns[0], :]
+                ) + dot_f32(weights[2 * head + 1], value_aug[head, columns[1], :])
 
         parts = []
         for head in range(2):
@@ -487,22 +528,24 @@
         inverse[rows, :] = jnp.where(first, parts[0][1], parts[1][1])
         held[rows, :] = result.astype(BF16)
 
-    @pl.loop(0, tiles)
-    def restore(index):
-        context[tile_rows(index), :] = put_back(order_col, held, index)
+    put_back(order_col, held, context)
 
 
 def attend_back_kernel(
     low, high, offsets, order_row, order_col, table, ordered, exact, inverse, incoming,
-    outgoing, slanted,
-    query_aug, key_aug, value_aug, grad_aug, grad_plain, key_turned,
-    strip, gathered, query_turned, key_sum, value_sum, held,
+    *refs,
 ):
+    (
+        outgoing, slanted,
+        query_aug, key_aug, value_aug, grad_aug, grad_plain, key_turned,
+        strip, gathered, query_turned, key_sum, value_sum, held, moved,
+    ) = refs[-15:]
     rows_all = ordered.shape[0]
     tiles = rows_all // TILE
     reach = strip.shape[2] // TILE // 2
     lane = lane_of(TILE)
     fill_strip(strip, table)
+    put_in_order(order_row, incoming, moved)
     gathered[...] = jnp.zeros(gathered.shape, F32)
     key_sum[...] = jnp.zeros(key_sum.shape, F32)
     value_sum[...] = jnp.zeros(value_sum.shape, F32)
@@ -512,7 +555,7 @@
         rows = tile_rows(index)
         block = ordered[rows, :].astype(F32)
         sequence = sequence_of(offsets, index * TILE)
-        arrived = put_in_order(order_row, incoming, index)
+        arrived = moved[rows, :].astype(F32)
         scaled = arrived * inverse[rows, :]
         grad_plain[rows, :] = scaled.astype(BF16)
         product = scaled * exact[rows, :]
@@ -565,9 +608,7 @@
     held[:, pl.ds(PAIR, PAIR)] = key_sum[...].astype(BF16)
     held[:, pl.ds(2 * PAIR, PAIR)] = value_sum[...].astype(BF16)
 
-    @pl.loop(0, tiles)
-    def restore(index):
-        outgoing[tile_rows(index), :] = put_back(order_col, held, index)
+    put_back(order_col, held, outgoing)
 
     width = gathered.shape[2]
     for head in range(2):
@@ -612,7 +653,7 @@
 
 
 def group_attention_back(
-    low, high, offsets, order_row, order_col, table, ordered, exact, inverse, incoming
+    low, high, offsets, order_row, order_col, table, ordered, exact, inverse, incoming, before=()
 ):
     rows = ordered.shape[0]
     smem = pl.BlockSpec(memory_space=pltpu.SMEM)
@@ -624,7 +665,7 @@
             jax.ShapeDtypeStruct((rows, 3 * PAIR), BF16),
             jax.ShapeDtypeStruct((2, 8, width), F32),
         ),
-        in_specs=[smem] * 3 + [vmem] * 7,
+        in_specs=[smem] * 3 + [vmem] * 7 + [pl.BlockSpec(memory_space=pl.ANY)] * len(before),
         out_specs=(vmem,) * 2,
         scratch_shapes=[
             pltpu.VMEM((2, rows, PAIR), BF16),
@@ -639,13 +680,14 @@
             pltpu.VMEM((rows, PAIR), F32),
             pltpu.VMEM((rows, PAIR), F32),
             pltpu.VMEM((rows, 3 * PAIR), BF16),
+            pltpu.VMEM((rows, PAIR), BF16),
         ],
         name="attend_back",
         compiler_params=pltpu.CompilerParams(vmem_limit_bytes=50 << 20),
         cost_estimate=pl.CostEstimate(
             flops=45_000_000_000, bytes_accessed=12_000_000, transcendentals=5_000_000
         ),
-    )(low, high, offsets, order_row, order_col, table, ordered, exact, inverse, incoming)
+    )(low, high, offsets, order_row, order_col, table, ordered, exact, inverse, incoming, *before)
 
 
 def sequence_plan(lengths, rows):
@@ -694,73 +736,92 @@
     )()
 
 
-def fold_kernel(chunk, *refs):
-    *sources, sent = refs
-    got = sources.pop(0) if len(sources) == 4 else None
-    start = 0
-    for source in sources:
-        rows = source.shape[0]
-        for band in range(source.shape[1] // BAND):
-            value = source[:, band * BAND : (band + 1) * BAND]
-            place = pl.ds(start, rows)
-            if got is not None:
-                value = (value.astype(F32) + got[place, :].astype(F32)).astype(BF16)
-            sent[place, :] = value
-            start += rows
-
-
-def spread_kernel(chunk, message, *refs):
-    start = 0
-    for result in refs[-3:]:
-        rows = result.shape[0]
-        for band in range(result.shape[1] // BAND):
-            result[:, band * BAND : (band + 1) * BAND] = message[pl.ds(start, rows), :].astype(F32)
-            start += rows
+def bands_of(width):
+    return [slice(band * BAND, (band + 1) * BAND) for band in range(width // BAND)]
+
+
+def pick_kernel(plan, outs, chunks, *refs):
+    picked = refs[len(refs) - outs :]
+    for flow, start, source, count in plan:
+        if source is None:
+            picked[flow][pl.ds(start, count), :] = jnp.zeros((count, BAND), BF16)
+            continue
+        part = refs[source]
+        rows = part.shape[0]
+        for band, columns in enumerate(bands_of(part.shape[1])):
+            picked[flow][pl.ds(start + band * rows, rows), :] = part[:, columns]
+
+
+def spread_kernel(starts, chunks, message, *refs):
+    parts = len(starts)
+    results, wide, sems = (refs[parts : 2 * parts], refs[2 * parts : 3 * parts], refs[3 * parts])
+    copies = []
+    for index, start in enumerate(starts):
+        rows = wide[index].shape[0]
+        place = pl.ds(pl.multiple_of(chunks[index] * rows, rows), rows)
+        for band, columns in enumerate(bands_of(wide[index].shape[1])):
+            wide[index][:, columns] = message[pl.ds(start + band * rows, rows), :].astype(F32)
+            copy = pltpu.make_async_copy(
+                wide[index].at[:, columns],
+                results[index].at[place, columns],
+                sems.at[len(copies)],
+            )
+            copy.start()
+            copies.append(copy)
+    for copy in copies:
+        copy.wait()
 
 
 def whole_spec(shape):
     return pl.BlockSpec(shape, lambda step, chunk: (0,) * len(shape))
 
 
-def row_spec(rows, width, first):
-    return pl.BlockSpec((rows, width), lambda step, chunk: (chunk[0] + first, 0))
-
-
-def fold_chunk(chunk, parts, got):
-    rows = sum(count * array_in.shape[1] // BAND for array_in, count, first, item in parts)
+def row_spec(rows, width, place):
+    return pl.BlockSpec((rows, width), lambda step, chunk: (chunk[place], 0))
+
+
+def pick_chunks(plan, rows, chunks, sources):
+    shapes = tuple(jax.ShapeDtypeStruct((count, BAND), BF16) for count in rows)
     return pl.pallas_call(
-        fold_kernel,
+        functools.partial(pick_kernel, plan, len(rows)),
         grid_spec=pltpu.PrefetchScalarGridSpec(
             num_scalar_prefetch=1,
             grid=(1,),
-            in_specs=[whole_spec((rows, BAND))] * len(got)
-            + [row_spec(count, array_in.shape[1], first) for array_in, count, first, item in parts],
-            out_specs=whole_spec((rows, BAND)),
+            in_specs=[
+                row_spec(count, array_in.shape[1], place)
+                for place, (array_in, count) in enumerate(sources)
+            ],
+            out_specs=tuple(whole_spec(shape.shape) for shape in shapes),
         ),
-        out_shape=jax.ShapeDtypeStruct((rows, BAND), BF16),
-        name="fold",
-        cost_estimate=pl.CostEstimate(flops=0, bytes_accessed=6 * rows * BAND, transcendentals=0),
-    )(chunk.reshape(1), *got, *[array_in for array_in, count, first, item in parts])
-
-
-def spread_chunk(chunk, message, parts, results):
-    rows = message.shape[0]
+        out_shape=shapes,
+        name="pick",
+        cost_estimate=pl.CostEstimate(
+            flops=0, bytes_accessed=4 * sum(rows) * BAND, transcendentals=0
+        ),
+    )(chunks, *[array_in for array_in, count in sources])
+
+
+def spread_chunks(starts, chunks, message, counts, results):
     kept = [pl.BlockSpec(memory_space=pl.ANY)] * len(results)
+    shapes = [(count, result.shape[1]) for count, result in zip(counts, results)]
+    copies = sum(width // BAND for count, width in shapes)
     return pl.pallas_call(
-        spread_kernel,
-        grid_spec=pltpu.PrefetchScalarGridSpec(
-            num_scalar_prefetch=1,
-            grid=(1,),
-            in_specs=[whole_spec((rows, BAND))] + kept,
-            out_specs=tuple(
-                row_spec(count, array_in.shape[1], first) for array_in, count, first, item in parts
-            ),
-        ),
-        out_shape=tuple(jax.ShapeDtypeStruct(array_in.shape, F32) for array_in, count, first, item in parts),
+        functools.partial(spread_kernel, starts),
+        in_specs=[
+            pl.BlockSpec(memory_space=pltpu.SMEM),
+            pl.BlockSpec(memory_space=pltpu.VMEM),
+        ]
+        + kept,
+        out_specs=tuple(kept),
+        out_shape=tuple(jax.ShapeDtypeStruct(result.shape, F32) for result in results),
+        scratch_shapes=[pltpu.VMEM(shape, F32) for shape in shapes]
+        + [pltpu.SemaphoreType.DMA((copies,))],
         input_output_aliases={2 + item: item for item in range(len(results))},
         name="spread",
-        cost_estimate=pl.CostEstimate(flops=0, bytes_accessed=6 * rows * BAND, transcendentals=0),
-    )(chunk.reshape(1), message, *results)
+        cost_estimate=pl.CostEstimate(
+            flops=0, bytes_accessed=6 * message.size, transcendentals=0
+        ),
+    )(chunks, message, *results)
 
 
 def heads_kernel(chunk, message, *refs):
@@ -811,17 +872,74 @@
 
 
 class RingSum:
-    def __init__(self, ahead, back, results):
+    def __init__(self, ahead, back, results, widths):
         self.flows = [(ahead, 1), (back, -1)]
+        self.widths = widths
         self.me = ring_place()
-        self.step = 0
-        self.results = list(results)
-        self.arrived = None
-        self.ready = [fold_chunk(self.me, parts, []) for parts, way in self.flows]
+        self.round = 0
+        self.results = tuple(results)
+        self.arrived = [None, None]
+        self.ready = [None, None]
+        self.arrays = {}
+        self.last = 2 * (len(RING) - 1)
+        self.rounds = self.last + max(part[4] for part in ahead)
 
     @property
     def done(self):
-        return self.step == 2 * (len(RING) - 1)
+        return self.round == self.rounds
+
+    def part_rows(self, part):
+        return part[1] * (self.widths[part[3]] // BAND)
+
+    def layout(self, parts, round_at):
+        start, starts = (0, {})
+        for index, part in enumerate(parts):
+            if 0 <= round_at - part[4] < self.last:
+                starts[index] = start
+                start += self.part_rows(part)
+        return (starts, start)
+
+    def chunk(self, part, way, hops):
+        return jnp.mod(self.me - way * hops, len(RING)) + part[2]
+
+    def pick(self, round_at):
+        self.picked = None
+        plan, sources, chunks, message_rows = ([], [], [], [])
+        for flow, (parts, way) in enumerate(self.flows):
+            starts, rows = self.layout(parts, round_at)
+            message_rows.append(rows)
+            for index, start in starts.items():
+                part = parts[index]
+                hops = round_at - part[4]
+                if hops < len(RING):
+                    plan.append((flow, start, len(sources), self.part_rows(part)))
+                    sources.append((self.arrays[part[3]], part[1]))
+                    chunks.append(self.chunk(part, way, hops))
+                else:
+                    plan.append((flow, start, None, self.part_rows(part)))
+        if sources:
+            self.picked = pick_chunks(tuple(plan), message_rows, jnp.stack(chunks), sources)
+
+    def make(self):
+        self.ready = []
+        for flow, (parts, way) in enumerate(self.flows):
+            got = self.arrived[flow]
+            if self.round == 0:
+                self.ready.append(self.picked[flow])
+                continue
+            starts, rows = self.layout(parts, self.round)
+            before, rows_before = self.layout(parts, self.round - 1)
+            kept = [index for index in starts if index in before]
+            if kept != list(before):
+                got = jnp.concatenate(
+                    [got[before[index] : before[index] + self.part_rows(parts[index])] for index in kept]
+                )
+            if self.picked is not None:
+                picked = self.picked[flow]
+                same = got.shape[0]
+                added = (got.astype(F32) + picked[:same].astype(F32)).astype(BF16)
+                got = added if same == rows else jnp.concatenate([added, picked[same:]])
+            self.ready.append(got)
 
     def send(self):
         if self.done:
@@ -834,25 +952,45 @@
     def absorb(self):
         if self.done:
             return
-        self.step += 1
-        for index, (parts, way) in enumerate(self.flows):
-            chunk = jnp.mod(self.me - way * self.step, len(RING))
-            got = self.arrived[index]
-            self.ready[index] = (
-                fold_chunk(chunk, parts, [got]) if self.step < len(RING) else got
-            )
+        self.round += 1
+        self.landed = list(self.arrived)
+        if not self.done:
+            self.make()
+
+    def prepare(self):
+        if self.round + 1 < self.rounds:
+            self.pick(self.round + 1)
 
     def place(self):
-        if self.step < len(RING) - 1:
-            return
-        for index, (parts, way) in enumerate(self.flows):
-            chunk = jnp.mod(self.me - way * self.step, len(RING))
-            ids = [part[3] for part in parts]
-            written = spread_chunk(
-                chunk, self.ready[index], parts, [self.results[item] for item in ids]
-            )
-            for item, result in zip(ids, written):
-                self.results[item] = result
+        results = list(self.results)
+        for flow, (parts, way) in enumerate(self.flows):
+            sent_starts, rows = self.layout(parts, self.round)
+            came_starts, rows = self.layout(parts, self.round - 1)
+            for starts, message, ends in (
+                (sent_starts, self.ready[flow], False),
+                (came_starts, self.landed[flow], True),
+            ):
+                picked, ids, counts, chunks = ([], [], [], [])
+                for index, start in starts.items():
+                    part = parts[index]
+                    hops = self.round - part[4]
+                    if hops < len(RING) - 1 or ends != (hops == self.last):
+                        continue
+                    picked.append(start)
+                    ids.append(part[3])
+                    counts.append(part[1])
+                    chunks.append(self.chunk(part, way, hops))
+                if picked:
+                    written = spread_chunks(
+                        tuple(picked),
+                        jnp.stack(chunks),
+                        message,
+                        counts,
+                        [results[item] for item in ids],
+                    )
+                    for item, result in zip(ids, written):
+                        results[item] = result
+        self.results = tuple(results)
 
 
 class RingGather:
@@ -862,6 +1000,8 @@
         self.ready = (block, block)
         self.arrived = None
         self.results = ()
+        self.arrays = ()
+        self.landed = ()
         self.found = [(lax.axis_index("ctx"), block)]
 
     def send(self):
@@ -869,21 +1009,30 @@
             return
         self.step += 1
         ahead, back = self.ready
-        ahead = lax.ppermute(ahead, "ctx", ring_pairs(1))
-        if self.step < len(RING) // 2:
-            back = lax.ppermute(back, "ctx", ring_pairs(-1))
-        self.arrived = (ahead, back)
+        if self.step == len(RING) // 2:
+            rows = ahead.shape[0] // 2
+            ahead, back = (ahead[:rows], back[rows:])
+        self.arrived = (
+            lax.ppermute(ahead, "ctx", ring_pairs(1)),
+            lax.ppermute(back, "ctx", ring_pairs(-1)),
+        )
+
+    def place(self):
+        pass
+
+    def prepare(self):
+        pass
 
     def absorb(self):
         if len(self.found) == len(RING):
             return
         self.ready = self.arrived
-        self.found.append((ring_chip(self.me - self.step), self.arrived[0]))
+        ahead, back = self.arrived
         if self.step < len(RING) // 2:
-            self.found.append((ring_chip(self.me + self.step), self.arrived[1]))
-
-    def place(self):
-        pass
+            self.found.append((ring_chip(self.me - self.step), ahead))
+            self.found.append((ring_chip(self.me + self.step), back))
+        else:
+            self.found.append((ring_chip(self.me - self.step), jnp.concatenate([ahead, back])))
 
 
 class HeadRing(RingGather):
@@ -899,14 +1048,15 @@
 
 
 def stage(values, *rings):
-    values, arrived = tie(values, [(ring.arrived, ring.results) for ring in rings])
+    values, arrived = tie(values, [(ring.arrived, ring.results, ring.arrays) for ring in rings])
     for ring, blocks in zip(rings, arrived):
-        ring.arrived, ring.results = blocks
+        ring.arrived, ring.results, ring.arrays = blocks
         ring.absorb()
     values, ready = tie(values, [ring.ready for ring in rings])
     for ring, blocks in zip(rings, ready):
         ring.ready = blocks
         ring.send()
+        ring.prepare()
         ring.place()
     return values
 
@@ -1015,7 +1165,7 @@
         )
 
     attn_own, attn_far = tp_sum(dot_f32(context, w_out), dot_f32(context, wo_far))
-    attn_own, attn_far = stage((attn_own, attn_far), normed_ring)
+    attn_own = stage(attn_own, normed_ring)
     hid_own, hid_far = (tok_own + attn_own, tok_far + attn_far)
     inner_grad = dot_nt(cot_own, w_down) + dot_nt(cot_far, wd_far)
     scale_f = norm_scale(hid_own, hid_far)
@@ -1028,11 +1178,6 @@
     gate_grad, up_grad = geglu_back(inner_grad)
     gate_grad = gate_grad.astype(BF16)
     up_grad = up_grad.astype(BF16)
-    gate_grad, up_grad, inner_act = stage((gate_grad, up_grad, inner_act), normed_ring)
-    dnf_own, dnf_far = tp_sum(
-        dot_nt(gate_grad, w_gate) + dot_nt(up_grad, w_up),
-        dot_nt(gate_grad, wg_far) + dot_nt(up_grad, wu_far),
-    )
 
     def pair_rows(own):
         return jnp.concatenate([own, swap(own, "fsdp")])
@@ -1041,9 +1186,44 @@
         return jnp.concatenate([own, swap(far, "fsdp")])
 
     nffn_pair = pair_half(nffn_own, nffn_far)
-    grad_gate = dot_tn(nffn_pair, pair_rows(gate_grad)).astype(BF16)
-    grad_up = dot_tn(nffn_pair, pair_rows(up_grad)).astype(BF16)
-    grad_down = dot_tn(pair_rows(inner_act), pair_half(cot_own, cot_far)).astype(BF16)
+    gate_pair, up_pair, act_pair = (pair_rows(gate_grad), pair_rows(up_grad), pair_rows(inner_act))
+    cot_pair = pair_half(cot_own, cot_far)
+    dnf_parts = [
+        (dot_nt(gate_grad, w_gate) + dot_nt(up_grad, w_up)).astype(BF16),
+        (dot_nt(gate_grad, wg_far) + dot_nt(up_grad, wu_far)).astype(BF16),
+    ]
+    dnf_parts, nffn_pair, act_pair = tie(dnf_parts, nffn_pair, act_pair)
+    dnf_own, dnf_far = tp_sum(*dnf_parts)
+    grad_down = dot_tn(act_pair, cot_pair).astype(BF16)
+    grad_gate = dot_tn(nffn_pair, gate_pair).astype(BF16)
+    grad_up = dot_tn(nffn_pair, up_pair).astype(BF16)
+    parts_round = len(RING)
+    grad_rows = grad_gate.shape[0] // parts_round
+    down_rows = grad_down.shape[0] // (2 * parts_round)
+    out_rows = w_out.shape[0] // (2 * parts_round)
+    out_shape = (w_out.shape[0], half)
+    blanks = blank_arrays(
+        [grad_gate.shape, grad_up.shape, grad_down.shape, out_shape] + [w_query.shape] * 3
+    )
+    ring = RingSum(
+        [
+            (None, grad_rows, 0, 0, 0),
+            (None, down_rows, 0, 2, 0),
+            (None, out_rows, 0, 3, OUT_ROUND),
+        ],
+        [
+            (None, grad_rows, 0, 1, 0),
+            (None, down_rows, parts_round, 2, 0),
+            (None, out_rows, parts_round, 3, OUT_ROUND),
+        ],
+        blanks[:4],
+        [grad_gate.shape[1], grad_up.shape[1], half, half],
+    )
+    ring.arrays = {0: grad_gate, 1: grad_up, 2: grad_down}
+    ring.pick(0)
+    ring.make()
+    ring.send()
+
     def norm_back(own, far, scale, gain_own, gain_far, dy_own, dy_far):
         mean_term = (
             jnp.sum(gain_own * dy_own * own, axis=1, keepdims=True)
@@ -1065,36 +1245,17 @@
     ag_own, ag_far = (hgrad_own.astype(BF16), hgrad_far.astype(BF16))
     grad_out = dot_tn(pair_rows(context), pair_half(ag_own, ag_far)).astype(BF16)
     context_grad = dot_nt(ag_own, w_out) + dot_nt(ag_far, wo_far)
-    grad_rows = grad_gate.shape[0] // len(RING)
-    down_rows = grad_down.shape[0] // (2 * len(RING))
-    out_rows = w_out.shape[0] // (2 * len(RING))
-    blanks = blank_arrays(
-        [grad_gate.shape, grad_up.shape, grad_down.shape, grad_out.shape] + [w_query.shape] * 3
-    )
-    context_grad, grad_out = stage((context_grad.astype(BF16), grad_out), normed_ring)
-    ring = RingSum(
-        [
-            (grad_gate, grad_rows, 0, 0),
-            (grad_down, down_rows, 0, 2),
-            (grad_out, out_rows, 0, 3),
-        ],
-        [
-            (grad_up, grad_rows, 0, 1),
-            (grad_down, down_rows, len(RING), 2),
-            (grad_out, out_rows, len(RING), 3),
-        ],
-        blanks[:4],
-    )
-    ring.send()
+    context_grad, ring.ready = tie(context_grad.astype(BF16), ring.ready)
     grad_mixed = by_heads([context_grad])
-    grad_mixed = stage(grad_mixed, ring)
+    ring.arrays[3] = grad_out
+    ring.prepare()
+    grad_mixed = stage(grad_mixed, normed_ring, ring)
     outgoing, slanted = group_attention_back(
-        low, high, offsets, order_row, order_col, table_back, ordered, exact, inverse, grad_mixed
-    )
-    outgoing, found, tops, inner_act = stage(
-        (outgoing, [blocks for chip, blocks in normed_ring.found], tops, inner_act),
-        ring,
-    )
+        low, high, offsets, order_row, order_col, table_back, ordered, exact, inverse, grad_mixed, ring.picked
+    )
+    outgoing, tops, inner_act = stage((outgoing, tops, inner_act), ring)
+    outgoing = stage(outgoing, normed_ring)
+    outgoing, found = tie(outgoing, [block for chip, block in normed_ring.found])
     query_grad, key_grad, value_grad = by_rows(outgoing)
     outgoing_turned = jnp.concatenate(
         [
@@ -1105,15 +1266,15 @@
     head_grads = dot_tn(jnp.concatenate(found), outgoing_turned)
     head_grads, head_grads_sent = (head_grads[:half], head_grads[half:].astype(BF16))
     head_grads = (head_grads + swap(head_grads_sent, "fsdp").astype(F32)).astype(BF16)
+    head_grads = stage(head_grads, ring)
+    head_ring = HeadRing(head_grads, blanks[4:])
+    head_ring.send()
+    head_ring.place()
     dn_parts = (
         dot_nt(query_grad, w_query) + dot_nt(key_grad, w_key) + dot_nt(value_grad, w_value),
         dot_nt(query_grad, wq_far) + dot_nt(key_grad, wk_far) + dot_nt(value_grad, wv_far),
     )
     dn_parts = (dn_parts[0].astype(BF16), dn_parts[1].astype(BF16))
-    head_grads, dn_parts = stage((head_grads, dn_parts), ring)
-    head_ring = HeadRing(head_grads, blanks[4:])
-    head_ring.send()
-    head_ring.place()
     dn_own, dn_far = tp_sum(*dn_parts)
     dn_own, dn_far = stage((dn_own, dn_far), ring, head_ring)
     tback_own, tback_far, dga_own, dga_far = norm_back(
@@ -1122,23 +1283,30 @@
     grad_tokens = whole(hgrad_own + tback_own, hgrad_far + tback_far)
     ffn_own, ffn_far = tp_sum(dot_f32(inner_act, w_down), dot_f32(inner_act, wd_far))
     output = whole(hid_own + ffn_own, hid_far + ffn_far).astype(BF16)
-    grad_tokens, output, dga_own, dga_far, tops = stage(
-        (grad_tokens, output, dga_own, dga_far, tops), ring, head_ring
-    )
     pair_top = jnp.max(tops, axis=(1, 2))
-    pair_top = jnp.maximum(pair_top, swap(pair_top, "fsdp"))
     here = jnp.arange(parts, dtype=jnp.int32)[:, None] == ctx
-    head_maxima = tiny_gather(pair_top).reshape(head_count)
     pair_bias = bucket_sums(rel_buckets, slanted)
     grad_bias = jnp.transpose(
         jnp.where(here[:, :, None], pair_bias[None], 0.0).reshape(head_count, NB)
     )
-    small_own = jnp.concatenate([dga_own, dgf_own])
-    small_sent = jnp.concatenate([dga_far, dgf_far])
     bias_flat = grad_bias.reshape(2, -1)
-    small_own = jnp.concatenate([small_own, jnp.where(first, bias_flat[0], bias_flat[1])])
-    small_sent = jnp.concatenate([small_sent, jnp.where(first, bias_flat[1], bias_flat[0])])
-    small_sum = jnp.sum(tiny_gather(small_own + swap(small_sent, "fsdp")), axis=0)
+    small_own = jnp.concatenate(
+        [dga_own, dgf_own, jnp.where(first, bias_flat[0], bias_flat[1]), pair_top]
+    )
+    small_sent = jnp.concatenate(
+        [dga_far, dgf_far, jnp.where(first, bias_flat[1], bias_flat[0]), pair_top]
+    )
+    small_got = swap(small_sent, "fsdp")
+    grad_tokens, output, small_own, small_got = stage(
+        (grad_tokens, output, small_own, small_got), ring, head_ring
+    )
+    small_both = jnp.concatenate(
+        [small_own[:-2] + small_got[:-2], jnp.maximum(small_own[-2:], small_got[-2:])]
+    )
+    small_all = tiny_gather(small_both)
+    stage((), ring, head_ring)
+    head_maxima = small_all[:, -2:].reshape(head_count)
+    small_sum = jnp.sum(small_all[:, :-2], axis=0)
     final_gain_a, final_gain_f = (small_sum[:half], small_sum[half : 2 * half])
     final_bias = small_sum[2 * half :].reshape(rel_bias.shape)
     clip_scale = TAU_CLIP / jnp.maximum(head_maxima, TAU_CLIP)
@@ -1157,7 +1325,7 @@
     )
     while not ring.done:
         stage((), ring, head_ring)
-        if ring.step == len(RING) + 1:
+        if ring.round == len(RING) + 2:
             others, ring.arrived = tie(others, ring.arrived)
     final_gate, final_up, final_down, final_out = ring.results
     final_query, final_key, final_value = head_ring.results

time: 782 us -> 761 us (0.973)
  waiting for transfers between devices: 335 us -> 275 us
  other arithmetic: 39 us -> 84 us
  Pallas kernels: 168 us -> 155 us
  matrix products: 102 us -> 92.8 us
    convert_element_type x0 -> x16, other arithmetic: none -> 35.8 us  [make(): added = (got.astype(F32) + picked[:same].astype(F32)).astype(BF16)]
    ppermute x14 -> x16, waiting for transfers between devices: 97.1 us -> 69.5 us  [the longest x8 44.5 us: send(): lax.ppermute(ahead, 'ctx', ring_pairs(1))]
    ppermute x26 -> x25, waiting for transfers between devices: 34.9 us -> 14.2 us  [swap(): return lax.ppermute(array_in, axis_name, [(0, 1), (1, 0)])]
    all_to_all x2, waiting for transfers between devices: 60.1 us -> 44.4 us  [by_heads(): moved = lax.all_to_all(mixed, 'ctx', 0, 0, tiled=True)]
    all_to_all x2, waiting for transfers between devices: 16.6 us -> 28.5 us  [by_rows(): lax.all_to_all(array_in.reshape(parts, local_rows, count * PAIR), 'ctx',...]
    all_to_all x2 -> x1, waiting for transfers between devices: 10.4 us -> 0.01 us  [tiny_gather(): return lax.all_to_all(sent, 'ctx', 0, 0, tiled=True)]
    pallas_call x1, Pallas kernels: 27.7 us -> 18.9 us  [group_attention(): pl.pallas_call(attend_kernel, out_shape=(jax.ShapeDtypeStruct((rows, 3 *...]
    ppermute x14 -> x16, starting transfers between devices: 15 us -> 21.7 us  [the longest x8 11.5 us: send(): lax.ppermute(ahead, 'ctx', ring_pairs(1))]
  transfers between devices with their start and end apart: 74 -> 76, of which waited for: 37 -> 30; matrix products, arithmetic and copies ran while one was open for 18% -> 23% of each run, Pallas kernels for 16% -> 20%
where the time goes in v3:
time: 761 us; the launch traced here: 748 us
  waiting for transfers between devices  275 us (36%)
  Pallas kernels  155 us (20%)
  matrix products  92.8 us (12%)
  starting transfers between devices  90.4 us (12%)
  other arithmetic  84 us (11%)
  local copies, waits for them, and re-layouts  47.8 us (6%)
    ppermute x30, waiting for transfers between devices, send(): lax.ppermute(held, 'ctx', ring_pairs(way))  118 us
    pallas_call x20, Pallas kernels, spread_chunks(): pl.pallas_call(functools.partial(spread_kernel, starts), in_specs=[pl.Blo...  49.4 us
    ppermute x8, waiting for transfers between devices, send(): lax.ppermute(ahead, 'ctx', ring_pairs(1))  44.5 us
    all_to_all x2, waiting for transfers between devices, by_heads(): moved = lax.all_to_all(mixed, 'ctx', 0, 0, tiled=True)  44.4 us
    convert_element_type x16, other arithmetic, make(): added = (got.astype(F32) + picked[:same].astype(F32)).astype(BF16)  35.8 us
    pallas_call x1, Pallas kernels, group_attention_back(): pl.pallas_call(attend_back_kernel, out_shape=(jax.ShapeDtypeStruct((rows,...  35.4 us
    dot_general x14, matrix products, dot_f32(): return jnp.dot(left, right, preferred_element_type=F32)  35.2 us
    dot_general x14, matrix products, dot_nt(): lax.dot_general(left, right, (((1,), (1,)), ((), ())), preferred_element_...  33.8 us
  transfers between devices with their start and end apart: 76, of which 30 were waited for; matrix products, arithmetic and copies ran while one was open for 23% of the time, Pallas kernels for 20%

profile of v3, /device:TPU:0, one launch (start us, length us, event | category | flops | bytes accessed | tf_op | source)
XLA Modules:
  0.0 747.7 jit_solution(7384795532152276444)
XLA Ops:
  17.7 7.4 all-to-all-start
  29.0 33.2 %all-to-all-done = bf16[8,256,384]{2,1,0:T(8,128)(2,1)S(1)} async-done(((bf16[8,256,384]{2,1,0:T(8,128)(2,1)}), bf16[8,256,384]{2,1,0:T(8,128)(2,1)S(1)}, u32[]{:S(2)}, u32[]{:S(2)}) %all-to-all-start) | async-done | bytes 1572896 | tf_op jit(solution)/shard_map/all_to_all | solution.py:1131
  64.3 18.9 %attend.1 = (bf16[2048,384]{1,0:T(8,128)(2,1)S(1)}, bf16[2048,128]{1,0:T(8,128)(2,1)S(1)}, f32[2048,128]{1,0:T(8,128)S(1)}, f32[2048,128]{1,0:T(8,128)S(1)}, f32[2,8,256]{2,1,0:T(8,128)S(1)}) custom-call(s32[8]{0:T(128)S(1)} %get-tuple-element.803.low, s32[8]{0:T(128)S(1)} %and_select_fusion.high, s32[3]{0:T(128)S(1)} %bitcast_subtract_fusion.offsets, ...), custom_call_target="tpu_custom_call" | custom-call | flops 36999999488 | bytes 8000000 | tf_op jit(solution)/shard_map/attend/pallas_call | solution.py:628
  89.0 5.1 all-to-all-start.1
  96.4 11.2 %all-to-all-done.1 = bf16[8,256,128]{1,2,0:T(8,128)(2,1)} async-done(((bf16[8,256,128]{1,2,0:T(8,128)(2,1)}), bf16[8,256,128]{1,2,0:T(8,128)(2,1)}, u32[]{:S(2)}, u32[]{:S(2)}) %all-to-all-start.1) | async-done | bytes 524320 | tf_op jit(solution)/shard_map/all_to_all | solution.py:1136
  111.8 5.5 fusion.86
  125.2 4.3 convolution_add_fusion.2
  134.2 10.1 %collective-permute-done.7 = bf16[256,2048]{1,0:T(8,128)(2,1)} collective-permute-done((bf16[256,2048]{1,0:T(8,128)(2,1)}, bf16[256,2048]{1,0:T(8,128)(2,1)}, u32[]{:S(2)}, u32[]{:S(2)}) %collective-permute-start.7) | collective-permute-done | bytes 1048608 | tf_op jit(solution)/shard_map/ppermute | solution.py:1016
  149.8 4.0 convolution_add_fusion
  153.8 5.8 multiply_convert_fusion.2
  161.8 4.0 fusion.90
  168.1 5.0 fusion.16
  175.2 4.8 convolution_convert_fusion.1.refs_1_.refs_3_.refs_4_
  180.7 4.7 convolution_convert_fusion.refs_2_.refs_3_
  187.2 4.7 convolution_convert_fusion.2.refs_0_
  191.9 3.5 pick.9
  195.6 3.9 collective-permute-done.17
  210.3 5.2 all-to-all-start.2
  220.9 4.1 convolution_convert_fusion.3.refs_2_.refs_5_.refs_0_.refs_1_
  224.9 3.6 pick.10
  232.8 11.1 %all-to-all-done.2 = bf16[8,256,128]{2,1,0:T(8,128)(2,1)S(1)} async-done(((bf16[8,256,128]{2,1,0:T(8,128)(2,1)}), bf16[8,256,128]{2,1,0:T(8,128)(2,1)S(1)}, u32[]{:S(2)}, u32[]{:S(2)}) %all-to-all-start.2) | async-done | bytes 524320 | tf_op jit(solution)/shard_map/all_to_all | solution.py:1131
  257.6 3.7 pick.11
  263.8 35.4 %attend_back.1 = (bf16[2048,384]{1,0:T(8,128)(2,1)}, f32[2,8,2304]{2,1,0:T(8,128)S(1)}) custom-call(s32[8]{0:T(128)S(1)} %get-tuple-element.803.low, s32[8]{0:T(128)S(1)} %and_select_fusion.high, s32[3]{0:T(128)S(1)} %bitcast_subtract_fusion.offsets, s32[1,2048]{1,0:T(1,128)S(1)} %copy-done, s32[2048,1]{1,0:T(8,128)S(1)} %copy.140.order_col, ...), custom_call_target="tpu_custom_call" | custom-call | flops 44999999488 | bytes 12000000 | tf_op jit(solution)/shard_map/attend_back/pallas_call | solution.py:662
  305.4 4.8 convolution_convert_fusion.5
  311.7 4.8 convolution_convert_fusion.4
  323.6 4.3 all-to-all-start.3
  338.2 4.6 fusion.95
  345.2 3.8 pick.12
  349.0 3.2 select_convert_fusion.1
  364.0 17.4 %all-to-all-done.3 = bf16[8,256,384]{1,2,0:T(8,128)(2,1)} async-done(((bf16[8,256,384]{1,2,0:T(8,128)(2,1)}), bf16[8,256,384]{1,2,0:T(8,128)(2,1)}, u32[]{:S(2)}, u32[]{:S(2)}) %all-to-all-start.3) | async-done | bytes 1572896 | tf_op jit(solution)/shard_map/all_to_all | solution.py:1136
  394.3 5.2 collective-permute-done.31
  404.1 3.8 pick.13
  416.6 7.4 collective-permute-start.45
  435.5 3.7 pick.14
  444.8 20.9 %collective-permute-done.43 = bf16[1088,512]{1,0:T(8,128)(2,1)} collective-permute-done((bf16[1088,512]{1,0:T(8,128)(2,1)}, bf16[1088,512]{1,0:T(8,128)(2,1)}, u32[]{:S(2)}, u32[]{:S(2)}) %collective-permute-start.43) | collective-permute-done | bytes 1114144 | tf_op jit(solution)/shard_map/ppermute | solution.py:948
  481.6 3.7 pick.15
  485.3 29.9 %collective-permute-done.49.message = bf16[1024,384]{1,0:T(8,128)(2,1)S(1)} collective-permute-done((bf16[1024,384]{1,0:T(8,128)(2,1)}, bf16[1024,384]{1,0:T(8,128)(2,1)S(1)}, u32[]{:S(2)}, u32[]{:S(2)}) %collective-permute-start.49) | collective-permute-done | bytes 786464 | tf_op jit(solution)/shard_map/ppermute | solution.py:1016
  529.9 3.7 pick.16
  533.5 21.0 %collective-permute-done.54 = bf16[512,384]{1,0:T(8,128)(2,1)S(1)} collective-permute-done((bf16[512,384]{1,0:T(8,128)(2,1)S(1)}, bf16[512,384]{1,0:T(8,128)(2,1)S(1)}, u32[]{:S(2)}, u32[]{:S(2)}) %collective-permute-start.54) | collective-permute-done | bytes 393248 | tf_op jit(solution)/shard_map/ppermute | solution.py:1017
  575.2 8.0 %collective-permute-done.55 = bf16[1088,512]{1,0:T(8,128)(2,1)S(1)} collective-permute-done((bf16[1088,512]{1,0:T(8,128)(2,1)S(1)}, bf16[1088,512]{1,0:T(8,128)(2,1)S(1)}, u32[]{:S(2)}, u32[]{:S(2)}) %collective-permute-start.55) | collective-permute-done | bytes 1114144 | tf_op jit(solution)/shard_map/ppermute | solution.py:948
  595.4 15.3 %collective-permute-done.57.message = bf16[1088,512]{1,0:T(8,128)(2,1)S(1)} collective-permute-done((bf16[1088,512]{1,0:T(8,128)(2,1)S(1)}, bf16[1088,512]{1,0:T(8,128)(2,1)S(1)}, u32[]{:S(2)}, u32[]{:S(2)}) %collective-permute-start.57) | collective-permute-done | bytes 1114144 | tf_op jit(solution)/shard_map/ppermute | solution.py:948
  614.5 3.7 all-to-all-start.4
  624.3 13.0 %collective-permute-done.59.message = bf16[1088,512]{1,0:T(8,128)(2,1)S(1)} collective-permute-done((bf16[1088,512]{1,0:T(8,128)(2,1)}, bf16[1088,512]{1,0:T(8,128)(2,1)S(1)}, u32[]{:S(2)}, u32[]{:S(2)}) %collective-permute-start.59) | collective-permute-done | bytes 1114144 | tf_op jit(solution)/shard_map/ppermute | solution.py:948
  641.6 4.9 multiply_convert_fusion
  651.9 9.7 %collective-permute-done.61.message = bf16[1088,512]{1,0:T(8,128)(2,1)} collective-permute-done((bf16[1088,512]{1,0:T(8,128)(2,1)S(1)}, bf16[1088,512]{1,0:T(8,128)(2,1)}, u32[]{:S(2)}, u32[]{:S(2)}) %collective-permute-start.61) | collective-permute-done | bytes 1114144 | tf_op jit(solution)/shard_map/ppermute | solution.py:948
  669.6 16.8 %collective-permute-done.63.message = bf16[1088,512]{1,0:T(8,128)(2,1)S(1)} collective-permute-done((bf16[1088,512]{1,0:T(8,128)(2,1)}, bf16[1088,512]{1,0:T(8,128)(2,1)S(1)}, u32[]{:S(2)}, u32[]{:S(2)}) %collective-permute-start.63) | collective-permute-done | bytes 1114144 | tf_op jit(solution)/shard_map/ppermute | solution.py:948
  694.6 16.5 %collective-permute-done.65.message = bf16[1088,512]{1,0:T(8,128)(2,1)S(1)} collective-permute-done((bf16[1088,512]{1,0:T(8,128)(2,1)S(1)}, bf16[1088,512]{1,0:T(8,128)(2,1)S(1)}, u32[]{:S(2)}, u32[]{:S(2)}) %collective-permute-start.65) | collective-permute-done | bytes 1114144 | tf_op jit(solution)/shard_map/ppermute | solution.py:948
  719.3 12.4 %collective-permute-done.67.message = bf16[1088,512]{1,0:T(8,128)(2,1)S(1)} collective-permute-done((bf16[1088,512]{1,0:T(8,128)(2,1)S(1)}, bf16[1088,512]{1,0:T(8,128)(2,1)S(1)}, u32[]{:S(2)}, u32[]{:S(2)}) %collective-permute-start.67) | collective-permute-done | bytes 1114144 | tf_op jit(solution)/shard_map/ppermute | solution.py:948
  (512 shorter events, 303.0 us)
Async XLA Ops:
  17.7 44.6 %all-to-all-start = ((bf16[8,256,384]{2,1,0:T(8,128)(2,1)}), bf16[8,256,384]{2,1,0:T(8,128)(2,1)S(1)}, u32[]{:S(2)}, u32[]{:S(2)}) async-start(bf16[8,256,384]{2,1,0:T(8,128)(2,1)} %copy.139), calls=%async_computation | async-start | bytes 3145728 | tf_op jit(solution)/shard_map/all_to_all | solution.py:1131
  25.1 92.9 %collective-permute-start.9 = (bf16[1024,1024]{1,0:T(8,128)(2,1)}, bf16[1024,1024]{1,0:T(8,128)(2,1)}, u32[]{:S(2)}, u32[]{:S(2)}) collective-permute-start(bf16[1024,1024]{1,0:T(8,128)(2,1)} %param.24), channel_id=1, source_target_pairs={{0,16},{16,0},{1,17},{17,1},{2,18},{18,2},{3,19},{19,3},{4,20},{20... | collective-permute-start | bytes 6291464 | tf_op jit(solution)/shard_map/ppermute | solution.py:362
  25.1 124.7 %collective-permute-start.13 = (bf16[1024,2560]{1,0:T(8,128)(2,1)}, bf16[1024,2560]{1,0:T(8,128)(2,1)}, u32[]{:S(2)}, u32[]{:S(2)}) collective-permute-start(bf16[1024,2560]{1,0:T(8,128)(2,1)} %param.27), channel_id=1, source_target_pairs={{0,16},{16,0},{1,17},{17,1},{2,18},{18,2},{3,19},{19,3},{4,20},{20... | collective-permute-start | bytes 15728648 | tf_op jit(solution)/shard_map/ppermute | solution.py:362
  25.6 95.6 %collective-permute-start.11 = (bf16[2560,1024]{1,0:T(8,128)(2,1)}, bf16[2560,1024]{1,0:T(8,128)(2,1)}, u32[]{:S(2)}, u32[]{:S(2)}) collective-permute-start(bf16[2560,1024]{1,0:T(8,128)(2,1)} %param.29), channel_id=1, source_target_pairs={{0,16},{16,0},{1,17},{17,1},{2,18},{18,2},{3,19},{19,3},{4,20},{20... | collective-permute-start | bytes 15728648 | tf_op jit(solution)/shard_map/ppermute | solution.py:362
  62.3 24.3 %collective-permute-start.5 = (bf16[256,2048]{1,0:T(8,128)(2,1)}, bf16[256,2048]{1,0:T(8,128)(2,1)}, u32[]{:S(2)}, u32[]{:S(2)}) collective-permute-start(bf16[256,2048]{1,0:T(8,128)(2,1)} %pad_maximum_fusion.4), channel_id=1, source_target_pairs={{0,2},{4,0},{8,4},{12,8},{14,12},{10,14},{6,10},{2,6},{1,3},{5,1},... | collective-permute-start | bytes 3145736 | tf_op jit(solution)/shard_map/ppermute | solution.py:1017
  63.8 24.2 %collective-permute-start.4 = (bf16[256,2048]{1,0:T(8,128)(2,1)}, bf16[256,2048]{1,0:T(8,128)(2,1)}, u32[]{:S(2)}, u32[]{:S(2)}) collective-permute-start(bf16[256,2048]{1,0:T(8,128)(2,1)} %pad_maximum_fusion.4), channel_id=1, source_target_pairs={{0,4},{4,8},{8,12},{12,14},{14,10},{10,6},{6,2},{2,0},{1,5},{5,9},... | collective-permute-start | bytes 3145736 | tf_op jit(solution)/shard_map/ppermute | solution.py:1016
  94.1 59.7 %collective-permute-start.12 = (bf16[1024,2560]{1,0:T(8,128)(2,1)}, bf16[1024,2560]{1,0:T(8,128)(2,1)}, u32[]{:S(2)}, u32[]{:S(2)}) collective-permute-start(bf16[1024,2560]{1,0:T(8,128)(2,1)} %param.28), channel_id=1, source_target_pairs={{0,16},{16,0},{1,17},{17,1},{2,18},{18,2},{3,19},{19,3},{4,20},{20... | collective-permute-start | bytes 15728648 | tf_op jit(solution)/shard_map/ppermute | solution.py:362
  133.9 39.7 %collective-permute-start.19 = (bf16[256,1024]{1,0:T(8,128)(2,1)}, bf16[256,1024]{1,0:T(8,128)(2,1)S(1)}, u32[]{:S(2)}, u32[]{:S(2)}) collective-permute-start(bf16[256,1024]{1,0:T(8,128)(2,1)} %get-tuple-element.767), channel_id=1, source_target_pairs={{0,16},{16,0},{1,17},{17,1},{2,18},{18,2},{3,19},{19,3},{4,20},{20... | collective-permute-start | bytes 1572872 | tf_op jit(solution)/shard_map/ppermute | solution.py:362
  144.4 71.1 %collective-permute-start.25 = (bf16[256,1024]{0,1:T(8,128)(2,1)}, bf16[256,1024]{0,1:T(8,128)(2,1)}, u32[]{:S(2)}, u32[]{:S(2)}) collective-permute-start(bf16[256,1024]{0,1:T(8,128)(2,1)} %bitcast.15), channel_id=1, source_target_pairs={{0,16},{16,0},{1,17},{17,1},{2,18},{18,2},{3,19},{19,3},{4,20},{20... | collective-permute-start | bytes 1572872 | tf_op jit(solution)/shard_map/ppermute | solution.py:362
  146.0 27.2 %collective-permute-start.14 = (bf16[256,1024]{1,0:T(8,128)(2,1)S(1)}, bf16[256,1024]{1,0:T(8,128)(2,1)S(1)}, u32[]{:S(2)}, u32[]{:S(2)}) collective-permute-start(bf16[256,1024]{1,0:T(8,128)(2,1)S(1)} %get-tuple-element.781), channel_id=1, source_target_pairs={{0,16},{16,0},{1,17},{17,1},{2,18},{18,2},{3,19},{19,3},{4,20},{20... | collective-permute-start | bytes 1572872 | tf_op jit(solution)/shard_map/ppermute | solution.py:362
  173.4 57.1 %collective-permute-start.21 = (bf16[256,2048]{1,0:T(8,128)(2,1)}, bf16[256,2048]{1,0:T(8,128)(2,1)}, u32[]{:S(2)}, u32[]{:S(2)}) collective-permute-start(bf16[256,2048]{1,0:T(8,128)(2,1)} %collective-permute-done.7), channel_id=1, source_target_pairs={{0,4},{4,8},{8,12},{12,14},{14,10},{10,6},{6,2},{2,0},{1,5},{5,9},... | collective-permute-start | bytes 3145736 | tf_op jit(solution)/shard_map/ppermute | solution.py:1016
  185.4 45.1 %collective-permute-start.22 = (bf16[256,2048]{1,0:T(8,128)(2,1)}, bf16[256,2048]{1,0:T(8,128)(2,1)}, u32[]{:S(2)}, u32[]{:S(2)}) collective-permute-start(bf16[256,2048]{1,0:T(8,128)(2,1)} %collective-permute-done.8), channel_id=1, source_target_pairs={{0,2},{4,0},{8,4},{12,8},{14,12},{10,14},{6,10},{2,6},{1,3},{5,1},... | collective-permute-start | bytes 3145736 | tf_op jit(solution)/shard_map/ppermute | solution.py:1017
  195.4 35.1 %collective-permute-start.23 = (bf16[960,512]{1,0:T(8,128)(2,1)}, bf16[960,512]{1,0:T(8,128)(2,1)}, u32[]{:S(2)}, u32[]{:S(2)}) collective-permute-start(bf16[960,512]{1,0:T(8,128)(2,1)} %get-tuple-element.392), channel_id=1, source_target_pairs={{0,4},{4,8},{8,12},{12,14},{14,10},{10,6},{6,2},{2,0},{1,5},{5,9},... | collective-permute-start | bytes 2949128 | tf_op jit(solution)/shard_map/ppermute | solution.py:948
  199.5 33.2 %collective-permute-start.24 = (bf16[960,512]{1,0:T(8,128)(2,1)}, bf16[960,512]{1,0:T(8,128)(2,1)}, u32[]{:S(2)}, u32[]{:S(2)}) collective-permute-start(bf16[960,512]{1,0:T(8,128)(2,1)} %get-tuple-element.393), channel_id=1, source_target_pairs={{0,2},{4,0},{8,4},{12,8},{14,12},{10,14},{6,10},{2,6},{1,3},{5,1},... | collective-permute-start | bytes 2949128 | tf_op jit(solution)/shard_map/ppermute | solution.py:948
  210.3 33.6 %all-to-all-start.2 = ((bf16[8,256,128]{2,1,0:T(8,128)(2,1)}), bf16[8,256,128]{2,1,0:T(8,128)(2,1)S(1)}, u32[]{:S(2)}, u32[]{:S(2)}) async-start(bf16[8,256,128]{2,1,0:T(8,128)(2,1)} %bitcast_bitcast_fusion), calls=%async_computation.2 | async-start | bytes 1048576 | tf_op jit(solution)/shard_map/all_to_all | solution.py:1131
  253.2 52.2 %collective-permute-start.30 = (bf16[128,2048]{1,0:T(8,128)(2,1)}, bf16[128,2048]{1,0:T(8,128)(2,1)}, u32[]{:S(2)}, u32[]{:S(2)}) collective-permute-start(bf16[128,2048]{1,0:T(8,128)(2,1)} %slice.150), channel_id=1, source_target_pairs={{0,2},{4,0},{8,4},{12,8},{14,12},{10,14},{6,10},{2,6},{1,3},{5,1},... | collective-permute-start | bytes 1572872 | tf_op jit(solution)/shard_map/ppermute | solution.py:1017
  253.9 51.4 %collective-permute-start.29 = (bf16[128,2048]{1,0:T(8,128)(2,1)}, bf16[128,2048]{1,0:T(8,128)(2,1)}, u32[]{:S(2)}, u32[]{:S(2)}) collective-permute-start(bf16[128,2048]{1,0:T(8,128)(2,1)} %slice.149), channel_id=1, source_target_pairs={{0,4},{4,8},{8,12},{12,14},{14,10},{10,6},{6,2},{2,0},{1,5},{5,9},... | collective-permute-start | bytes 1572872 | tf_op jit(solution)/shard_map/ppermute | solution.py:1016
  255.2 44.9 %collective-permute-start.27 = (bf16[1088,512]{1,0:T(8,128)(2,1)}, bf16[1088,512]{1,0:T(8,128)(2,1)}, u32[]{:S(2)}, u32[]{:S(2)}) collective-permute-start(bf16[1088,512]{1,0:T(8,128)(2,1)} %pad_maximum_fusion.2), channel_id=1, source_target_pairs={{0,4},{4,8},{8,12},{12,14},{14,10},{10,6},{6,2},{2,0},{1,5},{5,9},... | collective-permute-start | bytes 3342344 | tf_op jit(solution)/shard_map/ppermute | solution.py:948
  255.2 44.9 %collective-permute-start.28 = (bf16[1088,512]{1,0:T(8,128)(2,1)}, bf16[1088,512]{1,0:T(8,128)(2,1)}, u32[]{:S(2)}, u32[]{:S(2)}) collective-permute-start(bf16[1088,512]{1,0:T(8,128)(2,1)} %pad_maximum_fusion.3), channel_id=1, source_target_pairs={{0,2},{4,0},{8,4},{12,8},{14,12},{10,14},{6,10},{2,6},{1,3},{5,1},... | collective-permute-start | bytes 3342344 | tf_op jit(solution)/shard_map/ppermute | solution.py:948
  310.2 38.8 %collective-permute-start.40 = (bf16[256,1024]{1,0:T(8,128)(2,1)}, bf16[256,1024]{1,0:T(8,128)(2,1)}, u32[]{:S(2)}, u32[]{:S(2)}) collective-permute-start(bf16[256,1024]{1,0:T(8,128)(2,1)} %convolution_convert_fusion.5), channel_id=1, source_target_pairs={{0,1},{1,0},{2,3},{3,2},{4,5},{5,4},{6,7},{7,6},{8,9},{9,8},{10,11... | collective-permute-start | bytes 1572872 | tf_op jit(solution)/shard_map/ppermute | solution.py:362
  316.5 32.5 %collective-permute-start.41 = (bf16[256,1024]{1,0:T(8,128)(2,1)}, bf16[256,1024]{1,0:T(8,128)(2,1)}, u32[]{:S(2)}, u32[]{:S(2)}) collective-permute-start(bf16[256,1024]{1,0:T(8,128)(2,1)} %convolution_convert_fusion.4), channel_id=1, source_target_pairs={{0,1},{1,0},{2,3},{3,2},{4,5},{5,4},{6,7},{7,6},{8,9},{9,8},{10,11... | collective-permute-start | bytes 1572872 | tf_op jit(solution)/shard_map/ppermute | solution.py:362
  319.3 35.2 %collective-permute-start.34 = (bf16[1088,512]{1,0:T(8,128)(2,1)}, bf16[1088,512]{1,0:T(8,128)(2,1)}, u32[]{:S(2)}, u32[]{:S(2)}) collective-permute-start(bf16[1088,512]{1,0:T(8,128)(2,1)} %add_convert_fusion.13), channel_id=1, source_target_pairs={{0,4},{4,8},{8,12},{12,14},{14,10},{10,6},{6,2},{2,0},{1,5},{5,9},... | collective-permute-start | bytes 3342344 | tf_op jit(solution)/shard_map/ppermute | solution.py:948
  319.3 35.2 %collective-permute-start.35 = (bf16[1088,512]{1,0:T(8,128)(2,1)}, bf16[1088,512]{1,0:T(8,128)(2,1)}, u32[]{:S(2)}, u32[]{:S(2)}) collective-permute-start(bf16[1088,512]{1,0:T(8,128)(2,1)} %add_convert_fusion.12), channel_id=1, source_target_pairs={{0,2},{4,0},{8,4},{12,8},{14,12},{10,14},{6,10},{2,6},{1,3},{5,1},... | collective-permute-start | bytes 3342344 | tf_op jit(solution)/shard_map/ppermute | solution.py:948
  323.6 57.7 %all-to-all-start.3 = ((bf16[8,256,384]{1,2,0:T(8,128)(2,1)}), bf16[8,256,384]{1,2,0:T(8,128)(2,1)}, u32[]{:S(2)}, u32[]{:S(2)}) async-start(bf16[8,256,384]{1,2,0:T(8,128)(2,1)} %copy.144), calls=%async_computation.3 | async-start | bytes 3145728 | tf_op jit(solution)/shard_map/all_to_all | solution.py:1136
  359.8 50.7 %collective-permute-start.39 = (bf16[1024,384]{1,0:T(8,128)(2,1)}, bf16[1024,384]{1,0:T(8,128)(2,1)}, u32[]{:S(2)}, u32[]{:S(2)}) collective-permute-start(bf16[1024,384]{1,0:T(8,128)(2,1)} %fusion.13.message), channel_id=1, source_target_pairs={{0,2},{4,0},{8,4},{12,8},{14,12},{10,14},{6,10},{2,6},{1,3},{5,1},... | collective-permute-start | bytes 2359304 | tf_op jit(solution)/shard_map/ppermute | solution.py:1017
  361.7 48.8 %collective-permute-start.38 = (bf16[1024,384]{1,0:T(8,128)(2,1)}, bf16[1024,384]{1,0:T(8,128)(2,1)}, u32[]{:S(2)}, u32[]{:S(2)}) collective-permute-start(bf16[1024,384]{1,0:T(8,128)(2,1)} %fusion.13.message), channel_id=1, source_target_pairs={{0,4},{4,8},{8,12},{12,14},{14,10},{10,6},{6,2},{2,0},{1,5},{5,9},... | collective-permute-start | bytes 2359304 | tf_op jit(solution)/shard_map/ppermute | solution.py:1016
  361.8 48.7 %collective-permute-start.36 = (bf16[1088,512]{1,0:T(8,128)(2,1)}, bf16[1088,512]{1,0:T(8,128)(2,1)}, u32[]{:S(2)}, u32[]{:S(2)}) collective-permute-start(bf16[1088,512]{1,0:T(8,128)(2,1)} %add_convert_fusion.11), channel_id=1, source_target_pairs={{0,4},{4,8},{8,12},{12,14},{14,10},{10,6},{6,2},{2,0},{1,5},{5,9},... | collective-permute-start | bytes 3342344 | tf_op jit(solution)/shard_map/ppermute | solution.py:948
  363.7 46.8 %collective-permute-start.37 = (bf16[1088,512]{1,0:T(8,128)(2,1)}, bf16[1088,512]{1,0:T(8,128)(2,1)}, u32[]{:S(2)}, u32[]{:S(2)}) collective-permute-start(bf16[1088,512]{1,0:T(8,128)(2,1)} %add_convert_fusion.10), channel_id=1, source_target_pairs={{0,2},{4,0},{8,4},{12,8},{14,12},{10,14},{6,10},{2,6},{1,3},{5,1},... | collective-permute-start | bytes 3342344 | tf_op jit(solution)/shard_map/ppermute | solution.py:948
  416.6 25.6 %collective-permute-start.45 = (bf16[1024,384]{1,0:T(8,128)(2,1)}, bf16[1024,384]{1,0:T(8,128)(2,1)}, u32[]{:S(2)}, u32[]{:S(2)}) collective-permute-start(bf16[1024,384]{1,0:T(8,128)(2,1)} %collective-permute-done.38.message), channel_id=1, source_target_pairs={{0,4},{4,8},{8,12},{12,14},{14,10},{10,6},{6,2},{2,0},{1,5},{5,9},... | collective-permute-start | bytes 2359304 | tf_op jit(solution)/shard_map/ppermute | solution.py:1016
  424.1 41.6 %collective-permute-start.43 = (bf16[1088,512]{1,0:T(8,128)(2,1)}, bf16[1088,512]{1,0:T(8,128)(2,1)}, u32[]{:S(2)}, u32[]{:S(2)}) collective-permute-start(bf16[1088,512]{1,0:T(8,128)(2,1)} %add_convert_fusion.9), channel_id=1, source_target_pairs={{0,4},{4,8},{8,12},{12,14},{14,10},{10,6},{6,2},{2,0},{1,5},{5,9},... | collective-permute-start | bytes 3342344 | tf_op jit(solution)/shard_map/ppermute | solution.py:948
  426.1 41.8 %collective-permute-start.44 = (bf16[1088,512]{1,0:T(8,128)(2,1)}, bf16[1088,512]{1,0:T(8,128)(2,1)}, u32[]{:S(2)}, u32[]{:S(2)}) collective-permute-start(bf16[1088,512]{1,0:T(8,128)(2,1)} %add_convert_fusion.8), channel_id=1, source_target_pairs={{0,2},{4,0},{8,4},{12,8},{14,12},{10,14},{6,10},{2,6},{1,3},{5,1},... | collective-permute-start | bytes 3342344 | tf_op jit(solution)/shard_map/ppermute | solution.py:948
  472.4 43.0 %collective-permute-start.47 = (bf16[1088,512]{1,0:T(8,128)(2,1)}, bf16[1088,512]{1,0:T(8,128)(2,1)}, u32[]{:S(2)}, u32[]{:S(2)}) collective-permute-start(bf16[1088,512]{1,0:T(8,128)(2,1)} %add_convert_fusion.7), channel_id=1, source_target_pairs={{0,4},{4,8},{8,12},{12,14},{14,10},{10,6},{6,2},{2,0},{1,5},{5,9},... | collective-permute-start | bytes 3342344 | tf_op jit(solution)/shard_map/ppermute | solution.py:948
  472.6 42.7 %collective-permute-start.48 = (bf16[1088,512]{1,0:T(8,128)(2,1)S(1)}, bf16[1088,512]{1,0:T(8,128)(2,1)}, u32[]{:S(2)}, u32[]{:S(2)}) collective-permute-start(bf16[1088,512]{1,0:T(8,128)(2,1)S(1)} %add_convert_fusion.6), channel_id=1, source_target_pairs={{0,2},{4,0},{8,4},{12,8},{14,12},{10,14},{6,10},{2,6},{1,3},{5,1},... | collective-permute-start | bytes 3342344 | tf_op jit(solution)/shard_map/ppermute | solution.py:948
  474.4 40.8 %collective-permute-start.49 = (bf16[1024,384]{1,0:T(8,128)(2,1)}, bf16[1024,384]{1,0:T(8,128)(2,1)S(1)}, u32[]{:S(2)}, u32[]{:S(2)}) collective-permute-start(bf16[1024,384]{1,0:T(8,128)(2,1)} %collective-permute-done.45.message), channel_id=1, source_target_pairs={{0,4},{4,8},{8,12},{12,14},{14,10},{10,6},{6,2},{2,0},{1,5},{5,9},... | collective-permute-start | bytes 2359304 | tf_op jit(solution)/shard_map/ppermute | solution.py:1016
  474.7 40.7 %collective-permute-start.50 = (bf16[1024,384]{1,0:T(8,128)(2,1)}, bf16[1024,384]{1,0:T(8,128)(2,1)S(1)}, u32[]{:S(2)}, u32[]{:S(2)}) collective-permute-start(bf16[1024,384]{1,0:T(8,128)(2,1)} %collective-permute-done.46.message), channel_id=1, source_target_pairs={{0,2},{4,0},{8,4},{12,8},{14,12},{10,14},{6,10},{2,6},{1,3},{5,1},... | collective-permute-start | bytes 2359304 | tf_op jit(solution)/shard_map/ppermute | solution.py:1017
  520.3 34.2 %collective-permute-start.51 = (bf16[1088,512]{1,0:T(8,128)(2,1)S(1)}, bf16[1088,512]{1,0:T(8,128)(2,1)}, u32[]{:S(2)}, u32[]{:S(2)}) collective-permute-start(bf16[1088,512]{1,0:T(8,128)(2,1)S(1)} %add_convert_fusion.5), channel_id=1, source_target_pairs={{0,4},{4,8},{8,12},{12,14},{14,10},{10,6},{6,2},{2,0},{1,5},{5,9},... | collective-permute-start | bytes 3342344 | tf_op jit(solution)/shard_map/ppermute | solution.py:948
  520.9 33.6 %collective-permute-start.52 = (bf16[1088,512]{1,0:T(8,128)(2,1)}, bf16[1088,512]{1,0:T(8,128)(2,1)}, u32[]{:S(2)}, u32[]{:S(2)}) collective-permute-start(bf16[1088,512]{1,0:T(8,128)(2,1)} %add_convert_fusion.4), channel_id=1, source_target_pairs={{0,2},{4,0},{8,4},{12,8},{14,12},{10,14},{6,10},{2,6},{1,3},{5,1},... | collective-permute-start | bytes 3342344 | tf_op jit(solution)/shard_map/ppermute | solution.py:948
  522.4 32.1 %collective-permute-start.54 = (bf16[512,384]{1,0:T(8,128)(2,1)S(1)}, bf16[512,384]{1,0:T(8,128)(2,1)S(1)}, u32[]{:S(2)}, u32[]{:S(2)}) collective-permute-start(bf16[512,384]{1,0:T(8,128)(2,1)S(1)} %slice.173), channel_id=1, source_target_pairs={{0,2},{4,0},{8,4},{12,8},{14,12},{10,14},{6,10},{2,6},{1,3},{5,1},... | collective-permute-start | bytes 1179656 | tf_op jit(solution)/shard_map/ppermute | solution.py:1017
  523.7 30.8 %collective-permute-start.53 = (bf16[512,384]{1,0:T(8,128)(2,1)S(1)}, bf16[512,384]{1,0:T(8,128)(2,1)S(1)}, u32[]{:S(2)}, u32[]{:S(2)}) collective-permute-start(bf16[512,384]{1,0:T(8,128)(2,1)S(1)} %slice.172), channel_id=1, source_target_pairs={{0,4},{4,8},{8,12},{12,14},{14,10},{10,6},{6,2},{2,0},{1,5},{5,9},... | collective-permute-start | bytes 1179656 | tf_op jit(solution)/shard_map/ppermute | solution.py:1016
  559.2 24.1 %collective-permute-start.55 = (bf16[1088,512]{1,0:T(8,128)(2,1)S(1)}, bf16[1088,512]{1,0:T(8,128)(2,1)S(1)}, u32[]{:S(2)}, u32[]{:S(2)}) collective-permute-start(bf16[1088,512]{1,0:T(8,128)(2,1)S(1)} %add_convert_fusion.3.message), channel_id=1, source_target_pairs={{0,4},{4,8},{8,12},{12,14},{14,10},{10,6},{6,2},{2,0},{1,5},{5,9},... | collective-permute-start | bytes 3342344 | tf_op jit(solution)/shard_map/ppermute | solution.py:948
  560.1 23.6 %collective-permute-start.56 = (bf16[1088,512]{1,0:T(8,128)(2,1)S(1)}, bf16[1088,512]{1,0:T(8,128)(2,1)}, u32[]{:S(2)}, u32[]{:S(2)}) collective-permute-start(bf16[1088,512]{1,0:T(8,128)(2,1)S(1)} %add_convert_fusion.2.message), channel_id=1, source_target_pairs={{0,2},{4,0},{8,4},{12,8},{14,12},{10,14},{6,10},{2,6},{1,3},{5,1},... | collective-permute-start | bytes 3342344 | tf_op jit(solution)/shard_map/ppermute | solution.py:948
  587.3 23.5 %collective-permute-start.57 = (bf16[1088,512]{1,0:T(8,128)(2,1)S(1)}, bf16[1088,512]{1,0:T(8,128)(2,1)S(1)}, u32[]{:S(2)}, u32[]{:S(2)}) collective-permute-start(bf16[1088,512]{1,0:T(8,128)(2,1)S(1)} %add_convert_fusion.1.message), channel_id=1, source_target_pairs={{0,4},{4,8},{8,12},{12,14},{14,10},{10,6},{6,2},{2,0},{1,5},{5,9},... | collective-permute-start | bytes 3342344 | tf_op jit(solution)/shard_map/ppermute | solution.py:948
  611.7 25.6 %collective-permute-start.59 = (bf16[1088,512]{1,0:T(8,128)(2,1)}, bf16[1088,512]{1,0:T(8,128)(2,1)S(1)}, u32[]{:S(2)}, u32[]{:S(2)}) collective-permute-start(bf16[1088,512]{1,0:T(8,128)(2,1)} %copy-done.52), channel_id=1, source_target_pairs={{0,4},{4,8},{8,12},{12,14},{14,10},{10,6},{6,2},{2,0},{1,5},{5,9},... | collective-permute-start | bytes 3342344 | tf_op jit(solution)/shard_map/ppermute | solution.py:948
  612.2 25.2 %collective-permute-start.60 = (bf16[1088,512]{1,0:T(8,128)(2,1)}, bf16[1088,512]{1,0:T(8,128)(2,1)}, u32[]{:S(2)}, u32[]{:S(2)}) collective-permute-start(bf16[1088,512]{1,0:T(8,128)(2,1)} %collective-permute-done.58.message), channel_id=1, source_target_pairs={{0,2},{4,0},{8,4},{12,8},{14,12},{10,14},{6,10},{2,6},{1,3},{5,1},... | collective-permute-start | bytes 3342344 | tf_op jit(solution)/shard_map/ppermute | solution.py:948
  614.5 25.6 %all-to-all-start.4 = ((f32[8,1,2306]{2,1,0:T(1,128)}), f32[8,1,2306]{2,1,0:T(1,128)S(1)}, u32[]{:S(2)}, u32[]{:S(2)}) async-start(f32[8,1,2306]{2,1,0:T(1,128)} %broadcast_in_dim.50), calls=%async_computation.4 | async-start | bytes 155648 | tf_op jit(solution)/shard_map/all_to_all | solution.py:871
  637.3 24.2 %collective-permute-start.61 = (bf16[1088,512]{1,0:T(8,128)(2,1)S(1)}, bf16[1088,512]{1,0:T(8,128)(2,1)}, u32[]{:S(2)}, u32[]{:S(2)}) collective-permute-start(bf16[1088,512]{1,0:T(8,128)(2,1)S(1)} %collective-permute-done.59.message), channel_id=1, source_target_pairs={{0,4},{4,8},{8,12},{12,14},{14,10},{10,6},{6,2},{2,0},{1,5},{5,9},... | collective-permute-start | bytes 3342344 | tf_op jit(solution)/shard_map/ppermute | solution.py:948
  661.6 24.9 %collective-permute-start.63 = (bf16[1088,512]{1,0:T(8,128)(2,1)}, bf16[1088,512]{1,0:T(8,128)(2,1)S(1)}, u32[]{:S(2)}, u32[]{:S(2)}) collective-permute-start(bf16[1088,512]{1,0:T(8,128)(2,1)} %collective-permute-done.61.message), channel_id=1, source_target_pairs={{0,4},{4,8},{8,12},{12,14},{14,10},{10,6},{6,2},{2,0},{1,5},{5,9},... | collective-permute-start | bytes 3342344 | tf_op jit(solution)/shard_map/ppermute | solution.py:948
  686.5 24.7 %collective-permute-start.65 = (bf16[1088,512]{1,0:T(8,128)(2,1)S(1)}, bf16[1088,512]{1,0:T(8,128)(2,1)S(1)}, u32[]{:S(2)}, u32[]{:S(2)}) collective-permute-start(bf16[1088,512]{1,0:T(8,128)(2,1)S(1)} %collective-permute-done.63.message), channel_id=1, source_target_pairs={{0,4},{4,8},{8,12},{12,14},{14,10},{10,6},{6,2},{2,0},{1,5},{5,9},... | collective-permute-start | bytes 3342344 | tf_op jit(solution)/shard_map/ppermute | solution.py:948
  (119 other events, 1049.7 us)
